TPU v7x, 32 devices: a whole 2x2x4 slice. The times are simulated.
32 devices in a mesh: row: 8 (over z, x), col: 4 (over y, core).
Axes of the slice: x: 2, y: 2, z: 4, core: 2. Of those that a mesh axis runs over, the one named last changes fastest.
Arguments:
- flow: bfloat16 [2048, 2048], P('row', 'col'), may hold values from 0.0009994507 to 1
- pattern: int32 [8, 8], P('row', 'col'), may hold values 0 or 1
- keep: int32 [8, 8], P('row', 'col'), may hold values 0 or 1
Outputs:
- clustered: float32 [2048, 2048], P('row', 'col')
All inputs are finite; a program needn't handle non-finite values. No bound on the sum of `pattern` or of `keep` on one device may be relied on, other than what follows from the above.
Results may differ from a plain program's by a relative error of at most 0.00046.
Values may be sent and summed in bfloat16 or wider, within the bound.
No kernel may reach another device: no remote copies, remote signals or barrier semaphores. Data moves between devices by JAX's collectives and lax.ppermute only.
A program may use at most 128 MiB of HBM per device.

v0:
```python
import jax
import jax.numpy as jnp
from jax import lax
from jax.sharding import PartitionSpec as P


def spread_tiles(grid, tile):
    trows, tcols = grid.shape
    wide = jnp.broadcast_to(grid[:, None, :, None], (trows, tile, tcols, tile))
    return wide.reshape(trows * tile, tcols * tile)


def body(flow, pattern, keep):
    rows_dev, cols_dev = flow.shape
    trows, tcols = pattern.shape
    tile = rows_dev // trows
    row_start = lax.axis_index("row") * rows_dev
    col_start = lax.axis_index("col") * cols_dev
    global_rows = row_start + lax.iota(jnp.int32, rows_dev)
    global_cols = col_start + lax.iota(jnp.int32, cols_dev)
    loops = (global_rows[:, None] == global_cols[None, :]).astype(jnp.float32)
    base = flow.astype(jnp.float32) * spread_tiles((pattern > 0).astype(jnp.float32), tile) + loops
    mass = lax.psum(jnp.sum(base, axis=0), "row")
    stochastic = (base / mass[None, :]).astype(jnp.bfloat16)
    left = lax.all_gather(stochastic, "col", axis=1, tiled=True)
    right = lax.all_gather(stochastic, "row", axis=0, tiled=True)
    expanded = jnp.dot(left, right, preferred_element_type=jnp.float32)
    tile_rows = lax.axis_index("row") * trows + lax.iota(jnp.int32, trows)
    tile_cols = lax.axis_index("col") * tcols + lax.iota(jnp.int32, tcols)
    kept = jnp.logical_or(keep > 0, tile_rows[:, None] == tile_cols[None, :]).astype(jnp.float32)
    expanded = expanded * spread_tiles(kept, tile)
    inflated = expanded * expanded
    partial_totals = jnp.sum(inflated, axis=0)
    order = rows_dev * lax.axis_size("row")
    totals = lax.psum(partial_totals, "row")
    scale = order / totals
    return inflated * scale[None, :]


def solution(mesh):
    return jax.shard_map(
        body,
        mesh=mesh,
        in_specs=(P("row", "col"), P("row", "col"), P("row", "col")),
        out_specs=P("row", "col"),
        check_vma=False,
    )
```

profile of v0, /device:TPU:0, one launch (start us, length us, event | category | flops | bytes accessed | tf_op | source)
XLA Modules:
  0.0 128.2 jit_solution(11294470787226683302)
XLA Ops:
  6.5 0.0 all-gather.3.cloned.1.call-start
  6.5 0.7 fusion.2
  7.2 0.1 broadcast_bitcast_fusion.1
  7.3 1.1 fusion.1
  8.4 23.1 %psum.14 = f32[512]{0:T(512)S(1)} all-reduce(f32[512]{0:T(512)S(1)} %fusion.1), channel_id=1, replica_groups=mesh['row'=8,'col'=4] {'row'}, use_global_device_ids=true, to_apply=%region_1.0 | all-reduce | flops 512 | bytes 4096 | tf_op jit(solution)/shard_map/psum | solution.py:23
  31.5 1.8 %divide_convert_fusion = bf16[256,512]{1,0:T(8,128)(2,1)} fusion(bf16[256,512]{1,0:T(8,128)(2,1)} %param.3, f32[512]{0:T(512)S(1)} %psum.14, s32[512]{0:T(512)S(1)} %iota_add_fusion, f32[512]{0:T(512)S(1)} %bitcast.13, s32[256]{0:T(256)S(1)} %iota_add_fusion.1), kind=kLoop, calls=%fused_computation.2 | loop fusion | flops 917504 | bytes 531456 | tf_op jit(solution)/shard_map/convert_element_type | solution.py:24
  33.3 0.0 all-gather.3.cloned.1.call-update
  33.3 0.0 all-gather.5.cloned.1.call-start
  33.4 0.7 all-gather.5.cloned.1.call-update
  34.1 0.7 fusion.3
  34.7 0.1 broadcast_bitcast_fusion
  34.8 12.7 %all-gather.3.cloned.1.call-done = bf16[256,2048]{1,0:T(8,128)(2,1)} async-done(((bf16[256,512]{1,0:T(8,128)(2,1)}), bf16[256,2048]{1,0:T(8,128)(2,1)}) %all-gather.3.cloned.1.call-update) | async-done | bytes 1048592 | tf_op jit(solution)/shard_map/all_gather | solution.py:25
  47.5 51.5 %all-gather.5.cloned.1.call-done = bf16[2048,512]{1,0:T(8,128)(2,1)} async-done(((bf16[256,512]{1,0:T(8,128)(2,1)}), bf16[2048,512]{1,0:T(8,128)(2,1)}) %all-gather.5.cloned.1.call-update) | async-done | bytes 2097168 | tf_op jit(solution)/shard_map/all_gather | solution.py:26
  98.9 2.6 %fusion.4 = (f32[512]{0:T(512)S(1)}, f32[256,512]{1,0:T(8,128)S(1)}) fusion(f32[512]{0:T(512)S(1)} %bitcast.14, bf16[256,2048]{1,0:T(8,128)(2,1)} %all-gather.3.cloned.1.call-done, bf16[2048,512]{1,0:T(8,128)(2,1)} %all-gather.5.cloned.1.call-done), kind=kOutput, calls=%fused_computation.15 | convolution fusion | flops 537263616 | bytes 3674112 | tf_op jit(solution)/shard_map/dot_general | solution.py:27
  101.6 18.9 %psum.15 = f32[512]{0:T(512)S(1)} all-reduce(f32[512]{0:T(512)S(1)} %get-tuple-element.5), channel_id=1, replica_groups=mesh['row'=8,'col'=4] {'row'}, use_global_device_ids=true, to_apply=%region_3.0 | all-reduce | flops 512 | bytes 4096 | tf_op jit(solution)/shard_map/psum | solution.py:35
  120.5 0.9 broadcast_multiply_fusion
  (5 shorter events, 0.0 us)
Async XLA Ops:
  6.5 40.9 %all-gather.3.cloned.1.call-start = ((), (), s32[]{:S(2)}) async-start(), calls=%async_computation | async-start | bytes 1310720 | tf_op jit(solution)/shard_map/all_gather | solution.py:25
  33.3 65.6 %all-gather.5.cloned.1.call-start = ((), (), s32[]{:S(2)}) async-start(), calls=%async_computation.1 | async-start | bytes 2359296 | tf_op jit(solution)/shard_map/all_gather | solution.py:26
Sparse Core Ops, SparseCore 0:
  33.4 14.0 all-gather.2
  49.6 49.2 all-gather.4
where the time goes:
time: 128 us
  waiting for transfers between devices  64.8 us (51%)
  blocking collectives  42 us (33%)
  between operations  13.4 us (10%)
  other arithmetic  5.1 us (4%)
  matrix products  2.64 us (2%)
    all_gather x1, waiting for transfers between devices, body(): right = lax.all_gather(stochastic, 'row', axis=0, tiled=True)  51.5 us
    psum x1, blocking collectives, body(): mass = lax.psum(jnp.sum(base, axis=0), 'row')  23.1 us
    psum x1, blocking collectives, body(): totals = lax.psum(partial_totals, 'row')  18.9 us
    all_gather x1, waiting for transfers between devices, body(): left = lax.all_gather(stochastic, 'col', axis=1, tiled=True)  12.7 us
    dot_general x1, matrix products, body(): expanded = jnp.dot(left, right, preferred_element_type=jnp.float32)  2.64 us
  transfers between devices with their start and end apart: 2, of which 2 were waited for; matrix products, arithmetic and copies ran while one was open for 1% of the time, Pallas kernels for 0%

commit v1 on v0

v1 whole, which is shorter than its diff:
```python
import functools

import jax
import jax.numpy as jnp
from jax import lax
from jax.experimental import pallas as pl
from jax.experimental.pallas import tpu as pltpu
from jax.sharding import PartitionSpec as P

LANES = 128
VMEM = pltpu.VMEM
SMEM = pltpu.SMEM


def ring_order(count):
    return list(range(0, count, 2)) + list(range(count - 1, 0, -2))


def ring_position(index, count):
    return jnp.where(index % 2 == 0, index // 2, count - 1 - index // 2)


def ring_member(position, count):
    position = lax.rem(position + count, count)
    return jnp.where(position < count // 2, 2 * position, 2 * (count - 1 - position) + 1)


def identity(tile):
    rows = lax.broadcasted_iota(jnp.int32, (tile, tile), 0)
    return (rows == lax.broadcasted_iota(jnp.int32, (tile, tile), 1)).astype(jnp.float32)


def mask_kernel(flow_ref, pattern_ref, masked_ref, sums_ref):
    tile = flow_ref.shape[0]
    tcols = flow_ref.shape[1] // tile
    row, col = lax.axis_index("row"), lax.axis_index("col")
    for t in range(tcols):
        cut = slice(t * tile, (t + 1) * tile)
        listed = (pattern_ref[0, t] > 0).astype(jnp.float32)
        block = flow_ref[:, cut].astype(jnp.float32) * listed
        masked_ref[:, cut] = block.astype(jnp.bfloat16)
        loop = (col * tcols + t == row).astype(jnp.float32)
        sums_ref[:, cut] = jnp.sum(block, axis=0, keepdims=True) + loop


def store_normalized(place, block, inverse, is_diagonal):
    place[...] = (block[...].astype(jnp.float32) * inverse).astype(jnp.bfloat16)

    @pl.when(is_diagonal)
    def _():
        base = block[...].astype(jnp.float32) + identity(block.shape[0])
        place[...] = (base * inverse).astype(jnp.bfloat16)


def square_kernel(rows_n, cols_n, last, *refs):
    blocks, refs = refs[: rows_n - 1], refs[rows_n - 1 :]
    own_cols, refs = refs[:cols_n], refs[cols_n:]
    mate_cols, refs = refs[:cols_n], refs[cols_n:]
    masses, refs = refs[:cols_n], refs[cols_n:]
    chunk_mass, acc_ref, left_last_ref, left, right = refs
    step = pl.program_id(0)
    row, col = lax.axis_index("row"), lax.axis_index("col")
    position = ring_position(row, rows_n)
    mate = row ^ (rows_n // 2)
    tile, cols_dev = own_cols[0].shape
    tcols = cols_dev // tile
    width = acc_ref.shape[1]

    @pl.when(step == 0)
    def _():
        for q in range(cols_n):
            for t in range(tcols):
                cut = slice(t * tile, (t + 1) * tile)
                inverse = 1.0 / masses[q][:, cut]
                k = (col ^ q) * tcols + t
                slot = lax.rem(ring_position(k, rows_n) - position + rows_n, rows_n)
                lanes = pl.ds(pl.multiple_of(slot * tile, tile), tile)
                store_normalized(left.at[0:tile, lanes], own_cols[q].at[:, cut], inverse, k == row)
                store_normalized(left.at[tile : 2 * tile, lanes], mate_cols[q].at[:, cut], inverse, k == mate)
        left_last_ref[...] = left[:, last * tile : (last + 1) * tile]

    slots = [s for s in range(rows_n) if s != last]
    for slot, block in zip(slots, blocks):
        r = ring_member(position + slot, rows_n)
        for t in range(width // tile):
            cut = slice(t * tile, (t + 1) * tile)
            tile_col = col * tcols + step * (width // tile) + t
            store_normalized(
                right.at[slot * tile : (slot + 1) * tile, cut], block.at[:, cut], 1.0 / chunk_mass[:, cut], tile_col == r
            )
    group = 4
    pieces = [(a, min(a + group, last)) for a in range(0, last, group)]
    pieces += [(a, min(a + group, rows_n)) for a in range(last + 1, rows_n, group)]
    for number, (a, b) in enumerate(pieces):
        span = slice(a * tile, b * tile)
        product = jnp.dot(left[:, span], right[span, :], preferred_element_type=jnp.float32)
        acc_ref[...] = product if number == 0 else acc_ref[...] + product


def inflate_kernel(rows_n, last, acc_ref, left_ref, top_ref, bottom_ref, mass_ref, kept_ref, out_ref, tot_ref, right):
    step = pl.program_id(0)
    row, col = lax.axis_index("row"), lax.axis_index("col")
    r = ring_member(ring_position(row, rows_n) + last, rows_n)
    tile, width = out_ref.shape
    per_step = width // tile
    tcols = per_step * pl.num_programs(0)
    half = top_ref.shape[0]
    for t in range(per_step):
        cut = slice(t * tile, (t + 1) * tile)
        inverse = 1.0 / mass_ref[:, cut]
        right[0:half, cut] = (top_ref[:, cut].astype(jnp.float32) * inverse).astype(jnp.bfloat16)
        right[half:tile, cut] = (bottom_ref[:, cut].astype(jnp.float32) * inverse).astype(jnp.bfloat16)

        @pl.when(col * tcols + step * per_step + t == r)
        def _():
            eye = identity(tile)
            top = top_ref[:, cut].astype(jnp.float32) + eye[0:half]
            bottom = bottom_ref[:, cut].astype(jnp.float32) + eye[half:tile]
            right[0:half, cut] = (top * inverse).astype(jnp.bfloat16)
            right[half:tile, cut] = (bottom * inverse).astype(jnp.bfloat16)

    for t in range(per_step):
        cut = slice(t * tile, (t + 1) * tile)
        product = acc_ref[:, cut] + jnp.dot(left_ref[...], right[:, cut], preferred_element_type=jnp.float32)
        mine = product[0:tile] * kept_ref[0, step * per_step + t]
        mine = mine * mine
        out_ref[:, cut] = mine
        other = product[tile : 2 * tile] * kept_ref[1, step * per_step + t]
        tot_ref[:, cut] = jnp.sum(mine + other * other, axis=0, keepdims=True)


def whole(shape=None):
    return pl.BlockSpec(memory_space=VMEM) if shape is None else pl.BlockSpec(shape, lambda j: (0, 0), memory_space=VMEM)


def body(rows_n, cols_n, flow, pattern, keep):
    tile, cols_dev = flow.shape
    tcols = pattern.shape[1]
    row, col = lax.axis_index("row"), lax.axis_index("col")
    position = ring_position(row, rows_n)
    half_ring, quarter = rows_n // 2, rows_n // 4
    width = min(cols_dev, 2 * tile)
    grid = (cols_dev // width,)

    order = ring_order(rows_n)
    up = [(order[i], order[(i + 1) % rows_n]) for i in range(rows_n)]
    down = [(b, a) for a, b in up]

    def send(value, axis, count, bit):
        return lax.ppermute(value, axis, [(i, i ^ bit) for i in range(count)])

    def send_row(value, bit):
        return send(value, "row", rows_n, bit)

    def col_blocks(value):
        held = {0: value}
        bit = cols_n // 2
        while bit:
            held.update({q ^ bit: send(v, "col", cols_n, bit) for q, v in list(held.items())})
            bit //= 2
        return [held[q] for q in range(cols_n)]

    masked, mass = pl.pallas_call(
        mask_kernel,
        out_shape=(
            jax.ShapeDtypeStruct(flow.shape, jnp.bfloat16),
            jax.ShapeDtypeStruct((1, cols_dev), jnp.float32),
        ),
        in_specs=[whole(), pl.BlockSpec(memory_space=SMEM)],
        out_specs=(whole(), whole()),
        compiler_params=pltpu.CompilerParams(vmem_limit_bytes=8 * tile * cols_dev * 2),
    )(flow, pattern)

    ring = {0: masked}
    bits = [1 << b for b in range(rows_n.bit_length() - 1)]
    tile_col = col * tcols + lax.iota(jnp.int32, tcols)
    kept = jnp.logical_or(keep > 0, (tile_col == row)[None, :]).astype(jnp.float32)
    behind = ahead = masked
    own_cols = mate_cols = masses = None
    for s in range(1, half_ring):
        behind, ahead = lax.ppermute(behind, "row", up), lax.ppermute(ahead, "row", down)
        ring[s], ring[rows_n - s] = ahead, behind
        if s == 1:
            own_cols = col_blocks(masked)
        if bits:
            for bit in (bits[:2] if s == 1 else bits):
                if bit == half_ring:
                    pad = jnp.zeros((1, LANES - tcols), jnp.float32)
                    other = send_row(jnp.concatenate([mass, kept, pad], axis=1), bit)
                    mass = mass + other[:, :cols_dev]
                    kept = jnp.concatenate([kept, other[:, cols_dev : cols_dev + tcols]], axis=0)
                else:
                    mass = mass + send_row(mass, bit)
            bits = bits[2:] if s == 1 else []
        elif masses is None:
            masses = col_blocks(mass)
        if s == quarter:
            mate = jnp.where(position % half_ring < quarter, ring[quarter], ring[rows_n - quarter])
        if s == quarter + 1:
            mate_cols = col_blocks(mate)
        behind, ahead, mass = lax.optimization_barrier((behind, ahead, mass))
    half = tile // 2
    top = lax.ppermute(behind[:half], "row", up)
    bottom = lax.ppermute(ahead[half:], "row", down)

    blocks = [ring[o] for o in range(rows_n) if o != half_ring]
    col_block = pl.BlockSpec((tile, width), lambda j: (0, j), memory_space=VMEM)
    col_row = pl.BlockSpec((1, width), lambda j: (0, j), memory_space=VMEM)
    full = whole((tile, cols_dev))
    acc, left_last = pl.pallas_call(
        functools.partial(square_kernel, rows_n, cols_n, half_ring),
        grid=grid,
        out_shape=(
            jax.ShapeDtypeStruct((2 * tile, cols_dev), jnp.float32),
            jax.ShapeDtypeStruct((2 * tile, tile), jnp.bfloat16),
        ),
        in_specs=[col_block] * len(blocks) + [full] * (2 * cols_n) + [whole((1, cols_dev))] * cols_n + [col_row],
        out_specs=(
            pl.BlockSpec((2 * tile, width), lambda j: (0, j), memory_space=VMEM),
            whole((2 * tile, tile)),
        ),
        scratch_shapes=[
            VMEM((2 * tile, rows_n * tile), jnp.bfloat16),
            VMEM((rows_n * tile, width), jnp.bfloat16),
        ],
        cost_estimate=pl.CostEstimate(
            flops=4 * tile * tile * rows_n * cols_dev, bytes_accessed=24 * tile * cols_dev, transcendentals=0
        ),
        compiler_params=pltpu.CompilerParams(
            vmem_limit_bytes=(20 if rows_n * tile <= 2048 else 60) * 1024 * 1024
        ),
    )(*blocks, *own_cols, *mate_cols, *masses, mass)

    inflated, totals = pl.pallas_call(
        functools.partial(inflate_kernel, rows_n, half_ring),
        grid=grid,
        out_shape=(
            jax.ShapeDtypeStruct((tile, cols_dev), jnp.float32),
            jax.ShapeDtypeStruct((1, cols_dev), jnp.float32),
        ),
        in_specs=[
            pl.BlockSpec((2 * tile, width), lambda j: (0, j), memory_space=VMEM),
            whole((2 * tile, tile)),
            pl.BlockSpec((half, width), lambda j: (0, j), memory_space=VMEM),
            pl.BlockSpec((half, width), lambda j: (0, j), memory_space=VMEM),
            col_row,
            pl.BlockSpec(memory_space=SMEM),
        ],
        out_specs=(col_block, col_row),
        scratch_shapes=[VMEM((tile, width), jnp.bfloat16)],
        cost_estimate=pl.CostEstimate(
            flops=4 * tile * tile * cols_dev, bytes_accessed=16 * tile * cols_dev, transcendentals=0
        ),
        compiler_params=pltpu.CompilerParams(vmem_limit_bytes=16 * 1024 * 1024),
    )(acc, left_last, top, bottom, mass, kept)

    bit = 1
    while bit < half_ring:
        wide = 2 * bit < half_ring
        if wide:
            walk = [0, 2 * bit, 3 * bit, bit]
            turn = [(i, (i & ~(3 * bit)) | walk[(walk.index(i & (3 * bit)) + 1) % 4]) for i in range(rows_n)]
            back = [(b, a) for a, b in turn]
            across = [(i, i ^ (3 * bit)) for i in range(rows_n)]
            totals = totals + sum(lax.ppermute(totals, "row", p) for p in (turn, back, across))
        else:
            totals = totals + send_row(totals, bit)
        bit *= 4 if wide else 2
    return inflated * (rows_n * tile / totals)


def solution(mesh):
    return jax.shard_map(
        functools.partial(body, mesh.shape["row"], mesh.shape["col"]),
        mesh=mesh,
        in_specs=(P("row", "col"), P("row", "col"), P("row", "col")),
        out_specs=P("row", "col"),
        check_vma=False,
    )
```

time: 128 us -> 50.6 us (0.40)
  waiting for transfers between devices: 64.8 us -> 19.4 us
  blocking collectives: 42 us -> 0 us
  starting transfers between devices: 0.04 us -> 24.6 us
  between operations: 13.4 us -> 0.17 us
  other arithmetic: 5.1 us -> 0.93 us
  Pallas kernels: 0 us -> 3.69 us
  matrix products: 2.64 us -> 0 us
  local copies, waits for them, and re-layouts: 0.15 us -> 1.72 us
    all_gather x2 -> x0, waiting for transfers between devices: 64.1 us -> none  [the longest x1 51.5 us: body(): right = lax.all_gather(stochastic, 'row', axis=0, tiled=True)]
    psum x2 -> x0, blocking collectives: 42 us -> none  [the longest x1 23.1 us: body(): mass = lax.psum(jnp.sum(base, axis=0), 'row')]
    ppermute x0 -> x23, starting transfers between devices: none -> 24.6 us  [the longest x12 9.8 us: send(): return lax.ppermute(value, axis, [(i, i ^ bit) for i in range(count)])]
    ppermute x0 -> x23, waiting for transfers between devices: none -> 19.4 us  [the longest x12 11.2 us: send(): return lax.ppermute(value, axis, [(i, i ^ bit) for i in range(count)])]
    pallas_call x0 -> x3, Pallas kernels: none -> 3.69 us  [the longest x1 2.15 us: body(): pl.pallas_call(functools.partial(square_kernel, rows_n, cols_n, half_ring...]
    dot_general x1 -> x0, matrix products: 2.64 us -> none  [body(): expanded = jnp.dot(left, right, preferred_element_type=jnp.float32)]
    convert_element_type x1, other arithmetic: 1.8 us -> 0.01 us  [body(): jnp.logical_or(keep > 0, (tile_col == row)[None, :]).astype(jnp.float32)]
    unnamed x4 -> x8, local copies, waits for them, and re-layouts: 0.15 us -> 1.61 us
  transfers between devices with their start and end apart: 2 -> 23, of which waited for: 2 -> 11; matrix products, arithmetic and copies ran while one was open for 1% -> 0% of each run, Pallas kernels for 0% -> 4%
where the time goes in v1:
time: 50.6 us; the launch traced here: 50.5 us
  starting transfers between devices  24.6 us (49%)
  waiting for transfers between devices  19.4 us (38%)
  Pallas kernels  3.69 us (7%)
  local copies, waits for them, and re-layouts  1.72 us (3%)
  other arithmetic  0.93 us (2%)
    ppermute x12, waiting for transfers between devices, send(): return lax.ppermute(value, axis, [(i, i ^ bit) for i in range(count)])  11.2 us
    ppermute x12, starting transfers between devices, send(): return lax.ppermute(value, axis, [(i, i ^ bit) for i in range(count)])  9.8 us
    ppermute x3, starting transfers between devices, body(): lax.ppermute(totals, 'row', p)  5.49 us
    ppermute x3, starting transfers between devices, body(): lax.ppermute(behind, 'row', up)  4.62 us
    ppermute x3, waiting for transfers between devices, body(): lax.ppermute(ahead, 'row', down)  2.64 us
    ppermute x3, starting transfers between devices, body(): lax.ppermute(ahead, 'row', down)  2.62 us
    pallas_call x1, Pallas kernels, body(): pl.pallas_call(functools.partial(square_kernel, rows_n, cols_n, half_ring...  2.15 us
    ppermute x3, waiting for transfers between devices, body(): lax.ppermute(behind, 'row', up)  1.88 us
  transfers between devices with their start and end apart: 23, of which 11 were waited for; matrix products, arithmetic and copies ran while one was open for 0% of the time, Pallas kernels for 4%

profile of v1, /device:TPU:0, one launch (start us, length us, event | category | flops | bytes accessed | tf_op | source)
XLA Modules:
  0.0 50.5 jit_solution(9047933674668740420)
XLA Ops:
  0.0 0.0 copy-start
  0.0 0.9 %copy-done = bf16[256,512]{1,0:T(8,128)(2,1)S(1)} copy-done((bf16[256,512]{1,0:T(8,128)(2,1)S(1)}, bf16[256,512]{1,0:T(8,128)(2,1)}, u32[]{:S(2)}) %copy-start) | copy-done | bytes 262168
  1.0 0.0 copy-start.1
  1.0 0.7 %copy-done.1 = s32[1,2]{1,0:T(1,128)S(1)} copy-done((s32[1,2]{1,0:T(1,128)S(1)}, s32[1,2]{1,0:T(1,128)}, u32[]{:S(2)}) %copy-start.1) | copy-done | bytes 32
  1.6 0.6 %shard_map.37 = (bf16[256,512]{1,0:T(8,128)(2,1)S(1)}, f32[1,512]{1,0:T(1,128)S(1)}) custom-call(bf16[256,512]{1,0:T(8,128)(2,1)S(1)} %copy-done, s32[1,2]{1,0:T(1,128)S(1)} %copy-done.1), custom_call_target="tpu_custom_call" | custom-call | tf_op jit(solution)/shard_map/pallas_call | solution.py:163
  2.2 3.1 %collective-permute-start.1 = (bf16[256,512]{1,0:T(8,128)(2,1)S(1)}, bf16[256,512]{1,0:T(8,128)(2,1)S(1)}, u32[]{:S(2)}, u32[]{:S(2)}) collective-permute-start(bf16[256,512]{1,0:T(8,128)(2,1)S(1)} %get-tuple-element.20.refs_0_.refs_7_), channel_id=1, source_target_pairs={{0,8},{8,16},{16,24},{24,28},{28,20},{20,12},{12,4},{4,0},{1,9},{9... | collective-permute-start | bytes 786440 | tf_op jit(solution)/shard_map/ppermute | solution.py:181
  5.3 0.0 collective-permute-start
  5.3 1.9 %collective-permute-start.2 = (f32[1,512]{1,0:T(1,128)S(1)}, f32[1,512]{1,0:T(1,128)S(1)}, u32[]{:S(2)}, u32[]{:S(2)}) collective-permute-start(f32[1,512]{1,0:T(1,128)S(1)} %get-tuple-element.21), channel_id=1, source_target_pairs={{0,4},{4,0},{8,12},{12,8},{16,20},{20,16},{24,28},{28,24},{1,5},{5... | collective-permute-start | bytes 6152 | tf_op jit(solution)/shard_map/ppermute | solution.py:150
  7.2 1.5 %collective-permute-start.10 = (bf16[256,512]{1,0:T(8,128)(2,1)S(1)}, bf16[256,512]{1,0:T(8,128)(2,1)S(1)}, u32[]{:S(2)}, u32[]{:S(2)}) collective-permute-start(bf16[256,512]{1,0:T(8,128)(2,1)S(1)} %get-tuple-element.20.refs_0_.refs_7_), channel_id=1, source_target_pairs={{0,2},{1,3},{2,0},{3,1},{4,6},{5,7},{6,4},{7,5},{8,10},{9,11},{10,... | collective-permute-start | bytes 786440 | tf_op jit(solution)/shard_map/ppermute | solution.py:150
  8.8 0.0 collective-permute-start.9
  8.8 2.8 %collective-permute-done.2 = f32[1,512]{1,0:T(1,128)S(1)} collective-permute-done((f32[1,512]{1,0:T(1,128)S(1)}, f32[1,512]{1,0:T(1,128)S(1)}, u32[]{:S(2)}, u32[]{:S(2)}) %collective-permute-start.2) | collective-permute-done | bytes 2080 | tf_op jit(solution)/shard_map/ppermute | solution.py:150
  11.6 0.0 collective-permute-start.3
  11.6 0.1 pad.4.clone
  11.7 0.0 copy-start.3
  11.7 3.4 %collective-permute-done.3 = f32[1,512]{1,0:T(1,128)S(1)} collective-permute-done((f32[1,512]{1,0:T(1,128)S(1)}, f32[1,512]{1,0:T(1,128)S(1)}, u32[]{:S(2)}, u32[]{:S(2)}) %collective-permute-start.3) | collective-permute-done | bytes 2080 | tf_op jit(solution)/shard_map/ppermute | solution.py:150
  15.2 0.0 collective-permute-done.1.refs_6_
  15.2 0.0 collective-permute-done.refs_1_
  15.2 1.9 %collective-permute-start.4 = (bf16[256,512]{1,0:T(8,128)(2,1)S(1)}, bf16[256,512]{1,0:T(8,128)(2,1)S(1)}, u32[]{:S(2)}, u32[]{:S(2)}) collective-permute-start(bf16[256,512]{1,0:T(8,128)(2,1)S(1)} %collective-permute-done.refs_1_), channel_id=1, source_target_pairs={{8,0},{16,8},{24,16},{28,24},{20,28},{12,20},{4,12},{0,4},{9,1},{1... | collective-permute-start | bytes 786440 | tf_op jit(solution)/shard_map/ppermute | solution.py:181
  17.1 0.2 collective-permute-start.5
  17.3 0.0 copy-done.3
  17.3 3.7 %collective-permute-start.6 = (f32[1,640]{1,0:T(1,128)S(1)}, f32[1,640]{1,0:T(1,128)S(1)}, u32[]{:S(2)}, u32[]{:S(2)}) collective-permute-start(f32[1,640]{1,0:T(1,128)S(1)} %reshape_maximum_fusion), channel_id=1, source_target_pairs={{0,16},{4,20},{8,24},{12,28},{16,0},{20,4},{24,8},{28,12},{1,17},{... | collective-permute-start | bytes 7688 | tf_op jit(solution)/shard_map/ppermute | solution.py:150
  21.0 0.9 %collective-permute-done.4.refs_2_ = bf16[256,512]{1,0:T(8,128)(2,1)S(1)} collective-permute-done((bf16[256,512]{1,0:T(8,128)(2,1)S(1)}, bf16[256,512]{1,0:T(8,128)(2,1)S(1)}, u32[]{:S(2)}, u32[]{:S(2)}) %collective-permute-start.4) | collective-permute-done | bytes 262176 | tf_op jit(solution)/shard_map/ppermute | solution.py:181
  21.9 1.5 %collective-permute-done.5.refs_5_ = bf16[256,512]{1,0:T(8,128)(2,1)S(1)} collective-permute-done((bf16[256,512]{1,0:T(8,128)(2,1)S(1)}, bf16[256,512]{1,0:T(8,128)(2,1)S(1)}, u32[]{:S(2)}, u32[]{:S(2)}) %collective-permute-start.5) | collective-permute-done | bytes 262176 | tf_op jit(solution)/shard_map/ppermute | solution.py:181
  23.5 1.8 %collective-permute-start.13 = (bf16[256,512]{1,0:T(8,128)(2,1)S(1)}, bf16[256,512]{1,0:T(8,128)(2,1)S(1)}, u32[]{:S(2)}, u32[]{:S(2)}) collective-permute-start(bf16[256,512]{1,0:T(8,128)(2,1)S(1)} %broadcast_select_fusion.refs_11_), channel_id=1, source_target_pairs={{0,2},{1,3},{2,0},{3,1},{4,6},{5,7},{6,4},{7,5},{8,10},{9,11},{10,... | collective-permute-start | bytes 786440 | tf_op jit(solution)/shard_map/ppermute | solution.py:150
  25.2 0.0 collective-permute-done.6
  25.2 0.0 copy-start.2
  25.2 0.7 %collective-permute-start.7 = (bf16[256,512]{1,0:T(8,128)(2,1)S(1)}, bf16[256,512]{1,0:T(8,128)(2,1)S(1)}, u32[]{:S(2)}, u32[]{:S(2)}) collective-permute-start(bf16[256,512]{1,0:T(8,128)(2,1)S(1)} %collective-permute-done.4.refs_2_), channel_id=1, source_target_pairs={{8,0},{16,8},{24,16},{28,24},{20,28},{12,20},{4,12},{0,4},{9,1},{1... | collective-permute-start | bytes 786440 | tf_op jit(solution)/shard_map/ppermute | solution.py:181
  26.0 1.3 %collective-permute-start.8 = (bf16[256,512]{1,0:T(8,128)(2,1)S(1)}, bf16[256,512]{1,0:T(8,128)(2,1)S(1)}, u32[]{:S(2)}, u32[]{:S(2)}) collective-permute-start(bf16[256,512]{1,0:T(8,128)(2,1)S(1)} %collective-permute-done.5.refs_5_), channel_id=1, source_target_pairs={{0,8},{8,16},{16,24},{24,28},{28,20},{20,12},{12,4},{4,0},{1,9},{9... | collective-permute-start | bytes 786440 | tf_op jit(solution)/shard_map/ppermute | solution.py:181
  27.3 0.0 collective-permute-done.10.refs_9_
  27.3 0.0 collective-permute-start.11
  27.3 0.0 collective-permute-done.9.refs_8_
  27.3 0.5 %collective-permute-start.12 = (bf16[256,512]{1,0:T(8,128)(2,1)S(1)}, bf16[256,512]{1,0:T(8,128)(2,1)S(1)}, u32[]{:S(2)}, u32[]{:S(2)}) collective-permute-start(bf16[256,512]{1,0:T(8,128)(2,1)S(1)} %broadcast_select_fusion.refs_11_), channel_id=1, source_target_pairs={{0,1},{1,0},{2,3},{3,2},{4,5},{5,4},{6,7},{7,6},{8,9},{9,8},{10,11... | collective-permute-start | bytes 786440 | tf_op jit(solution)/shard_map/ppermute | solution.py:150
  27.8 2.1 %collective-permute-done.13.refs_13_ = bf16[256,512]{1,0:T(8,128)(2,1)S(1)} collective-permute-done((bf16[256,512]{1,0:T(8,128)(2,1)S(1)}, bf16[256,512]{1,0:T(8,128)(2,1)S(1)}, u32[]{:S(2)}, u32[]{:S(2)}) %collective-permute-start.13) | collective-permute-done | bytes 262176 | tf_op jit(solution)/shard_map/ppermute | solution.py:150
  29.9 0.0 collective-permute-start.14
  29.9 1.7 %collective-permute-done.7.refs_3_ = bf16[256,512]{1,0:T(8,128)(2,1)S(1)} collective-permute-done((bf16[256,512]{1,0:T(8,128)(2,1)S(1)}, bf16[256,512]{1,0:T(8,128)(2,1)S(1)}, u32[]{:S(2)}, u32[]{:S(2)}) %collective-permute-start.7) | collective-permute-done | bytes 262176 | tf_op jit(solution)/shard_map/ppermute | solution.py:181
  31.7 0.3 collective-permute-start.16
  32.0 0.3 collective-permute-done.8.refs_4_
  32.3 0.0 collective-permute-start.15
  32.3 0.0 copy-done.2
  32.4 0.0 slice-start
  32.4 2.9 %collective-permute-done.16.refs_17_ = f32[1,512]{1,0:T(1,128)S(1)} collective-permute-done((f32[1,512]{1,0:T(1,128)S(1)}, f32[1,512]{1,0:T(1,128)S(1)}, u32[]{:S(2)}, u32[]{:S(2)}) %collective-permute-start.16) | collective-permute-done | bytes 2080 | tf_op jit(solution)/shard_map/ppermute | solution.py:150
  35.2 0.0 collective-permute-start.17
  35.2 0.0 collective-permute-done.11.refs_10_
  35.3 0.7 %collective-permute-start.19 = (bf16[128,512]{1,0:T(8,128)(2,1)S(1)}, bf16[128,512]{1,0:T(8,128)(2,1)S(1)}, u32[]{:S(2)}, u32[]{:S(2)}) collective-permute-start(bf16[128,512]{1,0:T(8,128)(2,1)S(1)} %slice.14), channel_id=1, source_target_pairs={{8,0},{16,8},{24,16},{28,24},{20,28},{12,20},{4,12},{0,4},{9,1},{1... | collective-permute-start | bytes 393224 | tf_op jit(solution)/shard_map/ppermute | solution.py:204
  35.9 0.0 collective-permute-done.15.refs_16_
  35.9 1.3 %collective-permute-start.18 = (bf16[128,512]{1,0:T(8,128)(2,1)S(1)}, bf16[128,512]{1,0:T(8,128)(2,1)S(1)}, u32[]{:S(2)}, u32[]{:S(2)}) collective-permute-start(bf16[128,512]{1,0:T(8,128)(2,1)S(1)} %slice.13), channel_id=1, source_target_pairs={{0,8},{8,16},{16,24},{24,28},{28,20},{20,12},{12,4},{4,0},{1,9},{9... | collective-permute-start | bytes 393224 | tf_op jit(solution)/shard_map/ppermute | solution.py:203
  37.3 0.0 slice-done
  37.3 0.0 collective-permute-done.17.refs_18_
  37.3 0.0 collective-permute-done.12.refs_12_
  37.3 0.0 collective-permute-done.14.refs_14_
  37.3 2.1 %shard_map.38 = (f32[512,512]{1,0:T(8,128)S(1)}, bf16[512,256]{1,0:T(8,128)(2,1)S(1)}) custom-call(bf16[256,512]{1,0:T(8,128)(2,1)S(1)} %get-tuple-element.20.refs_0_.refs_7_, bf16[256,512]{1,0:T(8,128)(2,1)S(1)} %collective-permute-done.refs_1_, bf16[256,512]{1,0:T(8,128)(2,1)S(1)} %collective-permute-done.4.refs_2_, ...), custom_call_target="tpu_custom_call" | custom-call | flops 1073741824 | bytes 3145728 | tf_op jit(solution)/shard_map/pallas_call | solution.py:210
  39.5 1.7 %collective-permute-done.19.bottom_ref = bf16[128,512]{1,0:T(8,128)(2,1)S(1)} collective-permute-done((bf16[128,512]{1,0:T(8,128)(2,1)S(1)}, bf16[128,512]{1,0:T(8,128)(2,1)S(1)}, u32[]{:S(2)}, u32[]{:S(2)}) %collective-permute-start.19) | collective-permute-done | bytes 131104 | tf_op jit(solution)/shard_map/ppermute | solution.py:204
  41.2 0.5 collective-permute-done.18.top_ref
  41.6 0.9 %shard_map.39 = (f32[256,512]{1,0:T(8,128)S(1)}, f32[1,512]{1,0:T(1,128)S(1)}) custom-call(f32[512,512]{1,0:T(8,128)S(1)} %get-tuple-element.29.acc_ref, bf16[512,256]{1,0:T(8,128)(2,1)S(1)} %get-tuple-element.30.left_ref, bf16[128,512]{1,0:T(8,128)(2,1)S(1)} %collective-permute-done.18.top_ref, bf16[128,512]{1,0:T(8,128)(2,1)S(1)} %collective-permute-done.19.bottom_ref, ...), custom_call_target="tpu_custom_call" | custom-call | flops 134217728 | bytes 2097152 | tf_op jit(solution)/shard_map/pallas_call | solution.py:234
  42.6 3.5 %collective-permute-start.22 = (f32[1,512]{1,0:T(1,128)S(1)}, f32[1,512]{1,0:T(1,128)S(1)}, u32[]{:S(2)}, u32[]{:S(2)}) collective-permute-start(f32[1,512]{1,0:T(1,128)S(1)} %get-tuple-element.34), channel_id=1, source_target_pairs={{0,12},{4,8},{8,4},{12,0},{16,28},{20,24},{24,20},{28,16},{1,13},{... | collective-permute-start | bytes 6152 | tf_op jit(solution)/shard_map/ppermute | solution.py:265
  46.0 0.0 collective-permute-start.21
  46.0 2.0 %collective-permute-start.20 = (f32[1,512]{1,0:T(1,128)S(1)}, f32[1,512]{1,0:T(1,128)S(1)}, u32[]{:S(2)}, u32[]{:S(2)}) collective-permute-start(f32[1,512]{1,0:T(1,128)S(1)} %get-tuple-element.34), channel_id=1, source_target_pairs={{0,8},{4,0},{8,12},{12,4},{16,24},{20,16},{24,28},{28,20},{1,9},{5... | collective-permute-start | bytes 6152 | tf_op jit(solution)/shard_map/ppermute | solution.py:265
  48.1 0.0 collective-permute-done.22
  48.1 1.6 %collective-permute-done.21 = f32[1,512]{1,0:T(1,128)S(1)} collective-permute-done((f32[1,512]{1,0:T(1,128)S(1)}, f32[1,512]{1,0:T(1,128)S(1)}, u32[]{:S(2)}, u32[]{:S(2)}) %collective-permute-start.21) | collective-permute-done | bytes 2080 | tf_op jit(solution)/shard_map/ppermute | solution.py:265
  49.6 0.0 collective-permute-done.20
  49.6 0.9 %broadcast_multiply_fusion = f32[256,512]{1,0:T(8,128)} fusion(f32[256,512]{1,0:T(8,128)S(1)} %get-tuple-element.33, f32[512]{0:T(512)S(1)} %bitcast.1), kind=kLoop, calls=%fused_computation | loop fusion | flops 131072 | bytes 1050624 | tf_op jit(solution)/shard_map/mul | solution.py:269
  (11 shorter events, 0.1 us)
Async XLA Ops:
  0.0 0.9 %copy-start = (bf16[256,512]{1,0:T(8,128)(2,1)S(1)}, bf16[256,512]{1,0:T(8,128)(2,1)}, u32[]{:S(2)}) copy-start(bf16[256,512]{1,0:T(8,128)(2,1)} %flow_ref.1) | copy-start | bytes 786436
  1.0 0.7 %copy-start.1 = (s32[1,2]{1,0:T(1,128)S(1)}, s32[1,2]{1,0:T(1,128)}, u32[]{:S(2)}) copy-start(s32[1,2]{1,0:T(1,128)} %pattern_ref.1) | copy-start | bytes 28
  2.2 12.9 %collective-permute-start.1 = (bf16[256,512]{1,0:T(8,128)(2,1)S(1)}, bf16[256,512]{1,0:T(8,128)(2,1)S(1)}, u32[]{:S(2)}, u32[]{:S(2)}) collective-permute-start(bf16[256,512]{1,0:T(8,128)(2,1)S(1)} %get-tuple-element.20.refs_0_.refs_7_), channel_id=1, source_target_pairs={{0,8},{8,16},{16,24},{24,28},{28,20},{20,12},{12,4},{4,0},{1,9},{9... | collective-permute-start | bytes 786440 | tf_op jit(solution)/shard_map/ppermute | solution.py:181
  5.3 9.9 %collective-permute-start = (bf16[256,512]{1,0:T(8,128)(2,1)S(1)}, bf16[256,512]{1,0:T(8,128)(2,1)S(1)}, u32[]{:S(2)}, u32[]{:S(2)}) collective-permute-start(bf16[256,512]{1,0:T(8,128)(2,1)S(1)} %get-tuple-element.20.refs_0_.refs_7_), channel_id=1, source_target_pairs={{8,0},{16,8},{24,16},{28,24},{20,28},{12,20},{4,12},{0,4},{9,1},{1... | collective-permute-start | bytes 786440 | tf_op jit(solution)/shard_map/ppermute | solution.py:181
  5.3 6.3 %collective-permute-start.2 = (f32[1,512]{1,0:T(1,128)S(1)}, f32[1,512]{1,0:T(1,128)S(1)}, u32[]{:S(2)}, u32[]{:S(2)}) collective-permute-start(f32[1,512]{1,0:T(1,128)S(1)} %get-tuple-element.21), channel_id=1, source_target_pairs={{0,4},{4,0},{8,12},{12,8},{16,20},{20,16},{24,28},{28,24},{1,5},{5... | collective-permute-start | bytes 6152 | tf_op jit(solution)/shard_map/ppermute | solution.py:150
  7.2 20.1 %collective-permute-start.10 = (bf16[256,512]{1,0:T(8,128)(2,1)S(1)}, bf16[256,512]{1,0:T(8,128)(2,1)S(1)}, u32[]{:S(2)}, u32[]{:S(2)}) collective-permute-start(bf16[256,512]{1,0:T(8,128)(2,1)S(1)} %get-tuple-element.20.refs_0_.refs_7_), channel_id=1, source_target_pairs={{0,2},{1,3},{2,0},{3,1},{4,6},{5,7},{6,4},{7,5},{8,10},{9,11},{10,... | collective-permute-start | bytes 786440 | tf_op jit(solution)/shard_map/ppermute | solution.py:150
  8.8 18.6 %collective-permute-start.9 = (bf16[256,512]{1,0:T(8,128)(2,1)S(1)}, bf16[256,512]{1,0:T(8,128)(2,1)S(1)}, u32[]{:S(2)}, u32[]{:S(2)}) collective-permute-start(bf16[256,512]{1,0:T(8,128)(2,1)S(1)} %get-tuple-element.20.refs_0_.refs_7_), channel_id=1, source_target_pairs={{0,1},{1,0},{2,3},{3,2},{4,5},{5,4},{6,7},{7,6},{8,9},{9,8},{10,11... | collective-permute-start | bytes 786440 | tf_op jit(solution)/shard_map/ppermute | solution.py:150
  11.6 3.6 %collective-permute-start.3 = (f32[1,512]{1,0:T(1,128)S(1)}, f32[1,512]{1,0:T(1,128)S(1)}, u32[]{:S(2)}, u32[]{:S(2)}) collective-permute-start(f32[1,512]{1,0:T(1,128)S(1)} %add.39), channel_id=1, source_target_pairs={{0,8},{4,12},{8,0},{12,4},{16,24},{20,28},{24,16},{28,20},{1,9},{5... | collective-permute-start | bytes 6152 | tf_op jit(solution)/shard_map/ppermute | solution.py:150
  11.7 5.5 %copy-start.3 = (s32[1,2]{1,0:T(1,128)S(1)}, s32[1,2]{1,0:T(1,128)}, u32[]{:S(2)}) copy-start(s32[1,2]{1,0:T(1,128)} %param.5) | copy-start | bytes 28
  15.2 6.7 %collective-permute-start.4 = (bf16[256,512]{1,0:T(8,128)(2,1)S(1)}, bf16[256,512]{1,0:T(8,128)(2,1)S(1)}, u32[]{:S(2)}, u32[]{:S(2)}) collective-permute-start(bf16[256,512]{1,0:T(8,128)(2,1)S(1)} %collective-permute-done.refs_1_), channel_id=1, source_target_pairs={{8,0},{16,8},{24,16},{28,24},{20,28},{12,20},{4,12},{0,4},{9,1},{1... | collective-permute-start | bytes 786440 | tf_op jit(solution)/shard_map/ppermute | solution.py:181
  17.1 6.4 %collective-permute-start.5 = (bf16[256,512]{1,0:T(8,128)(2,1)S(1)}, bf16[256,512]{1,0:T(8,128)(2,1)S(1)}, u32[]{:S(2)}, u32[]{:S(2)}) collective-permute-start(bf16[256,512]{1,0:T(8,128)(2,1)S(1)} %collective-permute-done.1.refs_6_), channel_id=1, source_target_pairs={{0,8},{8,16},{16,24},{24,28},{28,20},{20,12},{12,4},{4,0},{1,9},{9... | collective-permute-start | bytes 786440 | tf_op jit(solution)/shard_map/ppermute | solution.py:181
  17.3 7.9 %collective-permute-start.6 = (f32[1,640]{1,0:T(1,128)S(1)}, f32[1,640]{1,0:T(1,128)S(1)}, u32[]{:S(2)}, u32[]{:S(2)}) collective-permute-start(f32[1,640]{1,0:T(1,128)S(1)} %reshape_maximum_fusion), channel_id=1, source_target_pairs={{0,16},{4,20},{8,24},{12,28},{16,0},{20,4},{24,8},{28,12},{1,17},{... | collective-permute-start | bytes 7688 | tf_op jit(solution)/shard_map/ppermute | solution.py:150
  23.5 6.4 %collective-permute-start.13 = (bf16[256,512]{1,0:T(8,128)(2,1)S(1)}, bf16[256,512]{1,0:T(8,128)(2,1)S(1)}, u32[]{:S(2)}, u32[]{:S(2)}) collective-permute-start(bf16[256,512]{1,0:T(8,128)(2,1)S(1)} %broadcast_select_fusion.refs_11_), channel_id=1, source_target_pairs={{0,2},{1,3},{2,0},{3,1},{4,6},{5,7},{6,4},{7,5},{8,10},{9,11},{10,... | collective-permute-start | bytes 786440 | tf_op jit(solution)/shard_map/ppermute | solution.py:150
  25.2 7.1 %copy-start.2 = (f32[1,640]{1,0:T(1,128)}, f32[1,640]{1,0:T(1,128)S(1)}, u32[]{:S(2)}) copy-start(f32[1,640]{1,0:T(1,128)S(1)} %collective-permute-done.6) | copy-start | bytes 7684
  25.2 6.4 %collective-permute-start.7 = (bf16[256,512]{1,0:T(8,128)(2,1)S(1)}, bf16[256,512]{1,0:T(8,128)(2,1)S(1)}, u32[]{:S(2)}, u32[]{:S(2)}) collective-permute-start(bf16[256,512]{1,0:T(8,128)(2,1)S(1)} %collective-permute-done.4.refs_2_), channel_id=1, source_target_pairs={{8,0},{16,8},{24,16},{28,24},{20,28},{12,20},{4,12},{0,4},{9,1},{1... | collective-permute-start | bytes 786440 | tf_op jit(solution)/shard_map/ppermute | solution.py:181
  26.0 6.4 %collective-permute-start.8 = (bf16[256,512]{1,0:T(8,128)(2,1)S(1)}, bf16[256,512]{1,0:T(8,128)(2,1)S(1)}, u32[]{:S(2)}, u32[]{:S(2)}) collective-permute-start(bf16[256,512]{1,0:T(8,128)(2,1)S(1)} %collective-permute-done.5.refs_5_), channel_id=1, source_target_pairs={{0,8},{8,16},{16,24},{24,28},{28,20},{20,12},{12,4},{4,0},{1,9},{9... | collective-permute-start | bytes 786440 | tf_op jit(solution)/shard_map/ppermute | solution.py:181
  27.3 7.9 %collective-permute-start.11 = (bf16[256,512]{1,0:T(8,128)(2,1)S(1)}, bf16[256,512]{1,0:T(8,128)(2,1)S(1)}, u32[]{:S(2)}, u32[]{:S(2)}) collective-permute-start(bf16[256,512]{1,0:T(8,128)(2,1)S(1)} %collective-permute-done.10.refs_9_), channel_id=1, source_target_pairs={{0,1},{1,0},{2,3},{3,2},{4,5},{5,4},{6,7},{7,6},{8,9},{9,8},{10,11... | collective-permute-start | bytes 786440 | tf_op jit(solution)/shard_map/ppermute | solution.py:150
  27.3 10.0 %collective-permute-start.12 = (bf16[256,512]{1,0:T(8,128)(2,1)S(1)}, bf16[256,512]{1,0:T(8,128)(2,1)S(1)}, u32[]{:S(2)}, u32[]{:S(2)}) collective-permute-start(bf16[256,512]{1,0:T(8,128)(2,1)S(1)} %broadcast_select_fusion.refs_11_), channel_id=1, source_target_pairs={{0,1},{1,0},{2,3},{3,2},{4,5},{5,4},{6,7},{7,6},{8,9},{9,8},{10,11... | collective-permute-start | bytes 786440 | tf_op jit(solution)/shard_map/ppermute | solution.py:150
  29.9 7.4 %collective-permute-start.14 = (bf16[256,512]{1,0:T(8,128)(2,1)S(1)}, bf16[256,512]{1,0:T(8,128)(2,1)S(1)}, u32[]{:S(2)}, u32[]{:S(2)}) collective-permute-start(bf16[256,512]{1,0:T(8,128)(2,1)S(1)} %collective-permute-done.13.refs_13_), channel_id=1, source_target_pairs={{0,1},{1,0},{2,3},{3,2},{4,5},{5,4},{6,7},{7,6},{8,9},{9,8},{10,11... | collective-permute-start | bytes 786440 | tf_op jit(solution)/shard_map/ppermute | solution.py:150
  31.7 3.6 %collective-permute-start.16 = (f32[1,512]{1,0:T(1,128)S(1)}, f32[1,512]{1,0:T(1,128)S(1)}, u32[]{:S(2)}, u32[]{:S(2)}) collective-permute-start(f32[1,512]{1,0:T(1,128)S(1)} %slice_add_fusion.refs_15_.refs_19_.mass_ref), channel_id=1, source_target_pairs={{0,2},{1,3},{2,0},{3,1},{4,6},{5,7},{6,4},{7,5},{8,10},{9,11},{10,... | collective-permute-start | bytes 6152 | tf_op jit(solution)/shard_map/ppermute | solution.py:150
  32.3 3.6 %collective-permute-start.15 = (f32[1,512]{1,0:T(1,128)S(1)}, f32[1,512]{1,0:T(1,128)S(1)}, u32[]{:S(2)}, u32[]{:S(2)}) collective-permute-start(f32[1,512]{1,0:T(1,128)S(1)} %slice_add_fusion.refs_15_.refs_19_.mass_ref), channel_id=1, source_target_pairs={{0,1},{1,0},{2,3},{3,2},{4,5},{5,4},{6,7},{7,6},{8,9},{9,8},{10,11... | collective-permute-start | bytes 6152 | tf_op jit(solution)/shard_map/ppermute | solution.py:150
  32.4 4.9 %slice-start = ((f32[1,640]{1,0:T(1,128)}), f32[1,2]{1,0:T(1,128)S(1)}, s32[]{:S(2)}) async-start(f32[1,640]{1,0:T(1,128)} %copy-done.2), calls=%async_computation | async-start | bytes 1024 | tf_op jit(solution)/shard_map/slice | solution.py:191
  35.2 2.1 %collective-permute-start.17 = (f32[1,512]{1,0:T(1,128)S(1)}, f32[1,512]{1,0:T(1,128)S(1)}, u32[]{:S(2)}, u32[]{:S(2)}) collective-permute-start(f32[1,512]{1,0:T(1,128)S(1)} %collective-permute-done.16.refs_17_), channel_id=1, source_target_pairs={{0,1},{1,0},{2,3},{3,2},{4,5},{5,4},{6,7},{7,6},{8,9},{9,8},{10,11... | collective-permute-start | bytes 6152 | tf_op jit(solution)/shard_map/ppermute | solution.py:150
  35.3 5.9 %collective-permute-start.19 = (bf16[128,512]{1,0:T(8,128)(2,1)S(1)}, bf16[128,512]{1,0:T(8,128)(2,1)S(1)}, u32[]{:S(2)}, u32[]{:S(2)}) collective-permute-start(bf16[128,512]{1,0:T(8,128)(2,1)S(1)} %slice.14), channel_id=1, source_target_pairs={{8,0},{16,8},{24,16},{28,24},{20,28},{12,20},{4,12},{0,4},{9,1},{1... | collective-permute-start | bytes 393224 | tf_op jit(solution)/shard_map/ppermute | solution.py:204
  35.9 5.7 %collective-permute-start.18 = (bf16[128,512]{1,0:T(8,128)(2,1)S(1)}, bf16[128,512]{1,0:T(8,128)(2,1)S(1)}, u32[]{:S(2)}, u32[]{:S(2)}) collective-permute-start(bf16[128,512]{1,0:T(8,128)(2,1)S(1)} %slice.13), channel_id=1, source_target_pairs={{0,8},{8,16},{16,24},{24,28},{28,20},{20,12},{12,4},{4,0},{1,9},{9... | collective-permute-start | bytes 393224 | tf_op jit(solution)/shard_map/ppermute | solution.py:203
  42.6 5.5 %collective-permute-start.22 = (f32[1,512]{1,0:T(1,128)S(1)}, f32[1,512]{1,0:T(1,128)S(1)}, u32[]{:S(2)}, u32[]{:S(2)}) collective-permute-start(f32[1,512]{1,0:T(1,128)S(1)} %get-tuple-element.34), channel_id=1, source_target_pairs={{0,12},{4,8},{8,4},{12,0},{16,28},{20,24},{24,20},{28,16},{1,13},{... | collective-permute-start | bytes 6152 | tf_op jit(solution)/shard_map/ppermute | solution.py:265
  46.0 3.6 %collective-permute-start.21 = (f32[1,512]{1,0:T(1,128)S(1)}, f32[1,512]{1,0:T(1,128)S(1)}, u32[]{:S(2)}, u32[]{:S(2)}) collective-permute-start(f32[1,512]{1,0:T(1,128)S(1)} %get-tuple-element.34), channel_id=1, source_target_pairs={{8,0},{0,4},{12,8},{4,12},{24,16},{16,20},{28,24},{20,28},{9,1},{1... | collective-permute-start | bytes 6152 | tf_op jit(solution)/shard_map/ppermute | solution.py:265
  46.0 3.6 %collective-permute-start.20 = (f32[1,512]{1,0:T(1,128)S(1)}, f32[1,512]{1,0:T(1,128)S(1)}, u32[]{:S(2)}, u32[]{:S(2)}) collective-permute-start(f32[1,512]{1,0:T(1,128)S(1)} %get-tuple-element.34), channel_id=1, source_target_pairs={{0,8},{4,0},{8,12},{12,4},{16,24},{20,16},{24,28},{28,20},{1,9},{5... | collective-permute-start | bytes 6152 | tf_op jit(solution)/shard_map/ppermute | solution.py:265

commit v2 on v1

v2 whole, which is shorter than its diff:
```python
import functools

import jax
import jax.numpy as jnp
from jax import lax
from jax.experimental import pallas as pl
from jax.experimental.pallas import tpu as pltpu
from jax.sharding import PartitionSpec as P

LANES = 128


def ring_order(count):
    return list(range(0, count, 2)) + list(range(count - 1, 0, -2))


def ring_position(index, count):
    return jnp.where(index % 2 == 0, index // 2, count - 1 - index // 2)


def ring_member(position, count):
    position = lax.rem(position + count, count)
    return jnp.where(position < count // 2, 2 * position, 2 * (count - 1 - position) + 1)


def identity(tile):
    rows = lax.broadcasted_iota(jnp.int32, (tile, tile), 0)
    return (rows == lax.broadcasted_iota(jnp.int32, (tile, tile), 1)).astype(jnp.float32)


def lane(note, start, index):
    tail = note[:, start:]
    return jnp.sum(jnp.where(lax.broadcasted_iota(jnp.int32, tail.shape, 1) == index, tail, 0.0), axis=1, keepdims=True)


def mask_rows(note, start, rows_n, tcols, t, tile):
    tail = note[:, start:]
    shape = (rows_n, tail.shape[1])
    wanted = lax.broadcasted_iota(jnp.int32, shape, 0) * tcols + t
    chosen = jnp.where(lax.broadcasted_iota(jnp.int32, shape, 1) == wanted, tail, 0.0)
    return jnp.broadcast_to(jnp.sum(chosen, axis=1, keepdims=True), (rows_n, tile))


def note_kernel(rows_n, flow_hbm, pattern_hbm, keep_hbm, note_ref, flow_ref, pattern_ref, keep_ref, sems):
    pairs = ((flow_hbm, flow_ref), (pattern_hbm, pattern_ref), (keep_hbm, keep_ref))
    copies = [pltpu.make_async_copy(a, b, sems.at[i]) for i, (a, b) in enumerate(pairs)]
    for copy in copies:
        copy.start()
    for copy in copies:
        copy.wait()
    tile, cols_dev = flow_ref.shape
    tcols = cols_dev // tile
    row, col = lax.axis_index("row"), lax.axis_index("col")
    lanes = lax.broadcasted_iota(jnp.int32, (1, note_ref.shape[1] - cols_dev), 1)
    masks = jnp.zeros(lanes.shape, jnp.float32)
    for t in range(tcols):
        cut = slice(t * tile, (t + 1) * tile)
        loop = col * tcols + t == row
        listed = (pattern_ref[0, t] > 0).astype(jnp.float32)
        kept = jnp.logical_or(keep_ref[0, t] > 0, loop).astype(jnp.float32)
        sums = jnp.sum(flow_ref[:, cut].astype(jnp.float32), axis=0, keepdims=True)
        note_ref[:, cut] = sums * listed + loop.astype(jnp.float32)
        masks = jnp.where(lanes == row * tcols + t, listed, masks)
        masks = jnp.where(lanes == (rows_n + row) * tcols + t, kept, masks)
    note_ref[:, cols_dev:] = masks


def store_normalized(place, block, flag, inverse, is_diagonal):
    place[...] = (block[...].astype(jnp.float32) * (inverse * flag)).astype(jnp.bfloat16)

    @pl.when(is_diagonal)
    def _():
        base = block[...].astype(jnp.float32) * flag + identity(block.shape[0])
        place[...] = (base * inverse).astype(jnp.bfloat16)


def square_kernel(rows_n, cols_n, last, *refs):
    blocks, refs = refs[: rows_n - 1], refs[rows_n - 1 :]
    own_cols, refs = refs[:cols_n], refs[cols_n:]
    mate_cols, refs = refs[:cols_n], refs[cols_n:]
    notes, refs = refs[:cols_n], refs[cols_n:]
    acc_ref, left_last_ref, left, right, flags = refs
    step = pl.program_id(0)
    row, col = lax.axis_index("row"), lax.axis_index("col")
    position = ring_position(row, rows_n)
    mate = row ^ (rows_n // 2)
    tile, cols_dev = own_cols[0].shape
    tcols = cols_dev // tile
    width = acc_ref.shape[1]

    @pl.when(step == 0)
    def _():
        for q in range(cols_n):
            for t in range(tcols):
                flags[q * tcols + t] = mask_rows(notes[q], cols_dev, rows_n, tcols, t, tile)
        for q in range(cols_n):
            for t in range(tcols):
                cut = slice(t * tile, (t + 1) * tile)
                inverse = 1.0 / notes[q][:, cut]
                k = (col ^ q) * tcols + t
                slot = lax.rem(ring_position(k, rows_n) - position + rows_n, rows_n)
                lanes = pl.ds(pl.multiple_of(slot * tile, tile), tile)
                for half, cols, r in ((0, own_cols, row), (1, mate_cols, mate)):
                    flag = flags[q * tcols + t, pl.ds(r, 1), :]
                    place = left.at[half * tile : (half + 1) * tile, lanes]
                    store_normalized(place, cols[q].at[:, cut], flag, inverse, k == r)
        left_last_ref[...] = left[:, last * tile : (last + 1) * tile]

    slots = [s for s in range(rows_n) if s != last]
    for slot, block in zip(slots, blocks):
        r = ring_member(position + slot, rows_n)
        for t in range(width // tile):
            cut = slice(t * tile, (t + 1) * tile)
            tile_col = step * (width // tile) + t
            lanes = pl.ds(pl.multiple_of(tile_col * tile, tile), tile)
            place = right.at[slot * tile : (slot + 1) * tile, cut]
            flag = flags[tile_col, pl.ds(r, 1), :]
            store_normalized(place, block.at[:, cut], flag, 1.0 / notes[0][:, lanes], col * tcols + tile_col == r)
    group = 4
    pieces = [(a, min(a + group, last)) for a in range(0, last, group)]
    pieces += [(a, min(a + group, rows_n)) for a in range(last + 1, rows_n, group)]
    for number, (a, b) in enumerate(pieces):
        span = slice(a * tile, b * tile)
        product = jnp.dot(left[:, span], right[span, :], preferred_element_type=jnp.float32)
        acc_ref[...] = product if number == 0 else acc_ref[...] + product


def inflate_kernel(rows_n, last, acc_ref, left_ref, top_ref, bottom_ref, note_ref, out_ref, tot_ref, right):
    step = pl.program_id(0)
    row, col = lax.axis_index("row"), lax.axis_index("col")
    r = ring_member(ring_position(row, rows_n) + last, rows_n)
    tile, width = out_ref.shape
    per_step = width // tile
    tcols = per_step * pl.num_programs(0)
    cols_dev = tcols * tile
    half = top_ref.shape[0]
    for t in range(per_step):
        cut = slice(t * tile, (t + 1) * tile)
        tile_col = step * per_step + t
        flag = lane(note_ref, cols_dev, r * tcols + tile_col)
        inverse = 1.0 / note_ref[:, pl.ds(pl.multiple_of(tile_col * tile, tile), tile)]
        right[0:half, cut] = (top_ref[:, cut].astype(jnp.float32) * (inverse * flag)).astype(jnp.bfloat16)
        right[half:tile, cut] = (bottom_ref[:, cut].astype(jnp.float32) * (inverse * flag)).astype(jnp.bfloat16)

        @pl.when(col * tcols + tile_col == r)
        def _():
            eye = identity(tile)
            top = top_ref[:, cut].astype(jnp.float32) * flag + eye[0:half]
            bottom = bottom_ref[:, cut].astype(jnp.float32) * flag + eye[half:tile]
            right[0:half, cut] = (top * inverse).astype(jnp.bfloat16)
            right[half:tile, cut] = (bottom * inverse).astype(jnp.bfloat16)

    for t in range(per_step):
        cut = slice(t * tile, (t + 1) * tile)
        tile_col = step * per_step + t
        product = acc_ref[:, cut] + jnp.dot(left_ref[...], right[:, cut], preferred_element_type=jnp.float32)
        mine = product[0:tile] * lane(note_ref, cols_dev, (rows_n + row) * tcols + tile_col)
        mine = mine * mine
        out_ref[:, cut] = mine
        mate = row ^ (rows_n // 2)
        other = product[tile : 2 * tile] * lane(note_ref, cols_dev, (rows_n + mate) * tcols + tile_col)
        tot_ref[:, cut] = jnp.sum(mine + other * other, axis=0, keepdims=True)


def whole():
    return pl.BlockSpec(memory_space=pltpu.VMEM)


def fixed(shape):
    return pl.BlockSpec(shape, lambda j: (0, 0), memory_space=pltpu.VMEM)


def body(rows_n, cols_n, flow, pattern, keep):
    tile, cols_dev = flow.shape
    tcols = pattern.shape[1]
    row = lax.axis_index("row")
    position = ring_position(row, rows_n)
    half_ring, quarter = rows_n // 2, rows_n // 4
    width = min(cols_dev, 2 * tile)
    grid = (cols_dev // width,)
    small = rows_n * tile <= 2048

    order = ring_order(rows_n)
    up = [(order[i], order[(i + 1) % rows_n]) for i in range(rows_n)]
    down = [(b, a) for a, b in up]

    def send(value, axis, count, bit):
        return lax.ppermute(value, axis, [(i, i ^ bit) for i in range(count)])

    def send_row(value, bit):
        return send(value, "row", rows_n, bit)

    def finish_cols(own, other):
        held = {0: own, cols_n // 2: other}
        bit = cols_n // 4
        while bit:
            held.update({q ^ bit: send(v, "col", cols_n, bit) for q, v in list(held.items())})
            bit //= 2
        return [held[q] for q in range(cols_n)]

    def send_far_col(value):
        return send(value, "col", cols_n, cols_n // 2)

    lanes = -(-2 * rows_n * tcols // LANES) * LANES
    note = pl.pallas_call(
        functools.partial(note_kernel, rows_n),
        out_shape=jax.ShapeDtypeStruct((1, cols_dev + lanes), jnp.float32),
        in_specs=[pl.BlockSpec(memory_space=pltpu.HBM)] * 3,
        out_specs=whole(),
        scratch_shapes=[
            pltpu.VMEM(flow.shape, flow.dtype),
            pltpu.SMEM(pattern.shape, pattern.dtype),
            pltpu.SMEM(keep.shape, keep.dtype),
            pltpu.SemaphoreType.DMA((3,)),
        ],
        compiler_params=pltpu.CompilerParams(vmem_limit_bytes=8 * tile * cols_dev * 2),
    )(flow, pattern, keep)

    ring = {0: flow}
    behind = ahead = flow
    bit_count = rows_n.bit_length() - 1
    other_mate = None
    def send_both(value, bit):
        pairs = [(r * cols_n + c, (r ^ bit) * cols_n + (c ^ (cols_n // 2))) for r in range(rows_n) for c in range(cols_n)]
        return lax.ppermute(value, ("row", "col"), pairs)

    for s in range(1, half_ring):
        behind, ahead = lax.ppermute(behind, "row", up), lax.ppermute(ahead, "row", down)
        if s == 1:
            note = note + send_row(note, 1)
            mine = send_far_col(flow)
        elif s == 2:
            near, far = note + send_row(note, 2), send_far_col(note) + send_both(note, 2)
            note = jnp.concatenate([near, far], axis=0)
        elif s <= bit_count:
            note = note + send_row(note, 1 << (s - 1))
        if s == quarter + 1:
            other_mate = send_far_col(mate)
        if s <= bit_count:
            if s == 1:
                behind, ahead, note, mine = lax.optimization_barrier((behind, ahead, note, mine))
            else:
                behind, ahead, note = lax.optimization_barrier((behind, ahead, note))
        else:
            behind, ahead = lax.optimization_barrier((behind, ahead))
        ring[s], ring[rows_n - s] = ahead, behind
        if s == quarter:
            mate = jnp.where(position % half_ring < quarter, ahead, behind)
    beside_note = send(note, "col", cols_n, 1)
    half = tile // 2
    top = lax.ppermute(behind[:half], "row", up)
    bottom = lax.ppermute(ahead[half:], "row", down)
    notes = [note[:1], beside_note[:1], note[1:], beside_note[1:]]
    note = note[:1]
    own_cols = finish_cols(flow, mine)
    mate_cols = finish_cols(mate, other_mate)

    blocks = [ring[o] for o in range(rows_n) if o != half_ring]
    col_block = pl.BlockSpec((tile, width), lambda j: (0, j), memory_space=pltpu.VMEM)
    wide_block = pl.BlockSpec((2 * tile, width), lambda j: (0, j), memory_space=pltpu.VMEM)
    half_block = pl.BlockSpec((half, width), lambda j: (0, j), memory_space=pltpu.VMEM)
    acc, left_last = pl.pallas_call(
        functools.partial(square_kernel, rows_n, cols_n, half_ring),
        grid=grid,
        out_shape=(
            jax.ShapeDtypeStruct((2 * tile, cols_dev), jnp.float32),
            jax.ShapeDtypeStruct((2 * tile, tile), jnp.bfloat16),
        ),
        in_specs=[col_block] * len(blocks) + [fixed(v.shape) for v in own_cols + mate_cols + notes],
        out_specs=(wide_block, fixed((2 * tile, tile))),
        scratch_shapes=[
            pltpu.VMEM((2 * tile, rows_n * tile), jnp.bfloat16),
            pltpu.VMEM((rows_n * tile, width), jnp.bfloat16),
            pltpu.VMEM((cols_n * tcols, rows_n, tile), jnp.float32),
        ],
        cost_estimate=pl.CostEstimate(
            flops=4 * tile * tile * rows_n * cols_dev, bytes_accessed=24 * tile * cols_dev, transcendentals=0
        ),
        compiler_params=pltpu.CompilerParams(vmem_limit_bytes=(20 if small else 60) * 1024 * 1024),
    )(*blocks, *own_cols, *mate_cols, *notes)

    inflated, totals = pl.pallas_call(
        functools.partial(inflate_kernel, rows_n, half_ring),
        grid=grid,
        out_shape=(
            jax.ShapeDtypeStruct((tile, cols_dev), jnp.float32),
            jax.ShapeDtypeStruct((1, cols_dev), jnp.float32),
        ),
        in_specs=[wide_block, fixed((2 * tile, tile)), half_block, half_block, fixed(note.shape)],
        out_specs=(col_block, pl.BlockSpec((1, width), lambda j: (0, j), memory_space=pltpu.VMEM)),
        scratch_shapes=[pltpu.VMEM((tile, width), jnp.bfloat16)],
        cost_estimate=pl.CostEstimate(
            flops=4 * tile * tile * cols_dev, bytes_accessed=16 * tile * cols_dev, transcendentals=0
        ),
        compiler_params=pltpu.CompilerParams(vmem_limit_bytes=16 * 1024 * 1024),
    )(acc, left_last, top, bottom, note)

    bit = 1
    while bit < half_ring:
        totals = totals + send_row(totals, bit)
        bit *= 2
    return inflated * (rows_n * tile / totals)


def solution(mesh):
    return jax.shard_map(
        functools.partial(body, mesh.shape["row"], mesh.shape["col"]),
        mesh=mesh,
        in_specs=(P("row", "col"), P("row", "col"), P("row", "col")),
        out_specs=P("row", "col"),
        check_vma=False,
    )
```

time: 50.6 us -> 45.9 us (0.907)
  waiting for transfers between devices: 19.4 us -> 12.5 us
  starting transfers between devices: 24.6 us -> 26.3 us
  local copies, waits for them, and re-layouts: 1.72 us -> 2.33 us
    ppermute x12 -> x13, starting transfers between devices: 9.8 us -> 14.5 us  [send(): return lax.ppermute(value, axis, [(i, i ^ bit) for i in range(count)])]
    ppermute x3 -> x1, starting transfers between devices: 5.49 us -> 0.91 us  [send_both(): return lax.ppermute(value, ('row', 'col'), pairs)]
    ppermute x3, waiting for transfers between devices: 2.64 us -> 0.01 us  [body(): lax.ppermute(ahead, 'row', down)]
    ppermute x3, waiting for transfers between devices: 1.88 us -> 0.01 us  [body(): lax.ppermute(behind, 'row', up)]
    ppermute x1, starting transfers between devices: 0.69 us -> 2.31 us  [body(): bottom = lax.ppermute(ahead[half:], 'row', down)]
    ppermute x1, waiting for transfers between devices: 1.68 us -> 0.1 us  [body(): bottom = lax.ppermute(ahead[half:], 'row', down)]
    unnamed x8, local copies, waits for them, and re-layouts: 1.61 us -> 2.3 us
    ppermute x3, starting transfers between devices: 2.62 us -> 1.99 us  [body(): lax.ppermute(ahead, 'row', down)]
  transfers between devices with their start and end apart: 23 -> 22, of which waited for: 11 -> 9; matrix products, arithmetic and copies ran while one was open for 0% -> 0% of each run, Pallas kernels for 4% -> 7%
where the time goes in v2:
time: 45.9 us; the launch traced here: 45.7 us
  starting transfers between devices  26.3 us (57%)
  waiting for transfers between devices  12.5 us (27%)
  Pallas kernels  3.54 us (8%)
  local copies, waits for them, and re-layouts  2.33 us (5%)
  other arithmetic  0.93 us (2%)
    ppermute x13, starting transfers between devices, send(): return lax.ppermute(value, axis, [(i, i ^ bit) for i in range(count)])  14.5 us
    ppermute x13, waiting for transfers between devices, send(): return lax.ppermute(value, axis, [(i, i ^ bit) for i in range(count)])  10.6 us
    ppermute x3, starting transfers between devices, body(): lax.ppermute(behind, 'row', up)  5.19 us
    pallas_call x1, Pallas kernels, body(): pl.pallas_call(functools.partial(square_kernel, rows_n, cols_n, half_ring...  2.33 us
    ppermute x1, starting transfers between devices, body(): bottom = lax.ppermute(ahead[half:], 'row', down)  2.31 us
    unnamed x8, local copies, waits for them, and re-layouts  2.3 us
    ppermute x3, starting transfers between devices, body(): lax.ppermute(ahead, 'row', down)  1.99 us
    ppermute x1, starting transfers between devices, body(): top = lax.ppermute(behind[:half], 'row', up)  1.45 us
  transfers between devices with their start and end apart: 22, of which 9 were waited for; matrix products, arithmetic and copies ran while one was open for 0% of the time, Pallas kernels for 7%

profile of v2, /device:TPU:0, one launch (start us, length us, event | category | flops | bytes accessed | tf_op | source)
XLA Modules:
  0.0 45.7 jit_solution(1707682002335726572)
XLA Ops:
  0.0 3.0 %collective-permute-start = (bf16[256,512]{1,0:T(8,128)(2,1)}, bf16[256,512]{1,0:T(8,128)(2,1)S(1)}, u32[]{:S(2)}, u32[]{:S(2)}) collective-permute-start(bf16[256,512]{1,0:T(8,128)(2,1)} %refs_7_.1), channel_id=1, source_target_pairs={{0,8},{8,16},{16,24},{24,28},{28,20},{20,12},{12,4},{4,0},{1,9},{9... | collective-permute-start | bytes 786440 | tf_op jit(solution)/shard_map/ppermute | solution.py:228
  3.0 0.0 collective-permute-start.1
  3.0 2.0 %collective-permute-start.3 = (bf16[256,512]{1,0:T(8,128)(2,1)}, bf16[256,512]{1,0:T(8,128)(2,1)S(1)}, u32[]{:S(2)}, u32[]{:S(2)}) collective-permute-start(bf16[256,512]{1,0:T(8,128)(2,1)} %refs_7_.1), channel_id=1, source_target_pairs={{0,2},{1,3},{2,0},{3,1},{4,6},{5,7},{6,4},{7,5},{8,10},{9,11},{10,... | collective-permute-start | bytes 786440 | tf_op jit(solution)/shard_map/ppermute | solution.py:188
  5.0 0.0 copy-start
  5.0 1.0 %copy-done = bf16[256,512]{1,0:T(8,128)(2,1)S(1)} copy-done((bf16[256,512]{1,0:T(8,128)(2,1)S(1)}, bf16[256,512]{1,0:T(8,128)(2,1)}, u32[]{:S(2)}) %copy-start) | copy-done | bytes 262168
  6.0 0.0 copy-start.2
  6.0 0.7 %copy-done.2 = s32[1,2]{1,0:T(1,128)S(1)} copy-done((s32[1,2]{1,0:T(1,128)S(1)}, s32[1,2]{1,0:T(1,128)}, u32[]{:S(2)}) %copy-start.2) | copy-done | bytes 32
  6.6 0.0 copy-start.3
  6.6 0.7 %copy-done.3 = s32[1,2]{1,0:T(1,128)S(1)} copy-done((s32[1,2]{1,0:T(1,128)S(1)}, s32[1,2]{1,0:T(1,128)}, u32[]{:S(2)}) %copy-start.3) | copy-done | bytes 32
  7.3 0.6 %shard_map.37 = f32[1,640]{1,0:T(1,128)S(1)} custom-call(bf16[256,512]{1,0:T(8,128)(2,1)S(1)} %copy-done, s32[1,2]{1,0:T(1,128)S(1)} %copy-done.2, s32[1,2]{1,0:T(1,128)S(1)} %copy-done.3), custom_call_target="tpu_custom_call" | custom-call | tf_op jit(solution)/shard_map/pallas_call | solution.py:205
  7.9 1.6 %collective-permute-start.2 = (f32[1,640]{1,0:T(1,128)S(1)}, f32[1,640]{1,0:T(1,128)S(1)}, u32[]{:S(2)}, u32[]{:S(2)}) collective-permute-start(f32[1,640]{1,0:T(1,128)S(1)} %shard_map.37), channel_id=1, source_target_pairs={{0,4},{4,0},{8,12},{12,8},{16,20},{20,16},{24,28},{28,24},{1,5},{5... | collective-permute-start | bytes 7688 | tf_op jit(solution)/shard_map/ppermute | solution.py:188
  9.5 2.1 %collective-permute-done.2 = f32[1,640]{1,0:T(1,128)S(1)} collective-permute-done((f32[1,640]{1,0:T(1,128)S(1)}, f32[1,640]{1,0:T(1,128)S(1)}, u32[]{:S(2)}, u32[]{:S(2)}) %collective-permute-start.2) | collective-permute-done | bytes 2592 | tf_op jit(solution)/shard_map/ppermute | solution.py:188
  11.6 0.0 collective-permute-done.refs_6_
  11.6 0.0 collective-permute-done.1.refs_1_
  11.6 0.0 collective-permute-done.3.refs_9_
  11.6 1.6 %collective-permute-start.4 = (bf16[256,512]{1,0:T(8,128)(2,1)S(1)}, bf16[256,512]{1,0:T(8,128)(2,1)S(1)}, u32[]{:S(2)}, u32[]{:S(2)}) collective-permute-start(bf16[256,512]{1,0:T(8,128)(2,1)S(1)} %collective-permute-done.refs_6_), channel_id=1, source_target_pairs={{0,8},{8,16},{16,24},{24,28},{28,20},{20,12},{12,4},{4,0},{1,9},{9... | collective-permute-start | bytes 786440 | tf_op jit(solution)/shard_map/ppermute | solution.py:228
  13.3 0.4 collective-permute-start.5
  13.7 1.6 %collective-permute-start.6 = (f32[1,640]{1,0:T(1,128)S(1)}, f32[1,640]{1,0:T(1,128)S(1)}, u32[]{:S(2)}, u32[]{:S(2)}) collective-permute-start(f32[1,640]{1,0:T(1,128)S(1)} %add.26), channel_id=1, source_target_pairs={{0,8},{4,12},{8,0},{12,4},{16,24},{20,28},{24,16},{28,20},{1,9},{5... | collective-permute-start | bytes 7688 | tf_op jit(solution)/shard_map/ppermute | solution.py:188
  15.3 1.0 %collective-permute-start.7 = (f32[1,640]{1,0:T(1,128)S(1)}, f32[1,640]{1,0:T(1,128)S(1)}, u32[]{:S(2)}, u32[]{:S(2)}) collective-permute-start(f32[1,640]{1,0:T(1,128)S(1)} %add.26), channel_id=1, source_target_pairs={{0,2},{1,3},{2,0},{3,1},{4,6},{5,7},{6,4},{7,5},{8,10},{9,11},{10,... | collective-permute-start | bytes 7688 | tf_op jit(solution)/shard_map/ppermute | solution.py:188
  16.3 0.9 %collective-permute-start.8 = (f32[1,640]{1,0:T(1,128)S(1)}, f32[1,640]{1,0:T(1,128)S(1)}, u32[]{:S(2)}, u32[]{:S(2)}) collective-permute-start(f32[1,640]{1,0:T(1,128)S(1)} %add.26), channel_id=1, source_target_pairs={{0,10},{1,11},{2,8},{3,9},{4,14},{5,15},{6,12},{7,13},{8,2},{9,3},... | collective-permute-start | bytes 7688 | tf_op jit(solution)/shard_map/ppermute | solution.py:225
  17.2 2.5 %collective-permute-done.6 = f32[1,640]{1,0:T(1,128)S(1)} collective-permute-done((f32[1,640]{1,0:T(1,128)S(1)}, f32[1,640]{1,0:T(1,128)S(1)}, u32[]{:S(2)}, u32[]{:S(2)}) %collective-permute-start.6) | collective-permute-done | bytes 2592 | tf_op jit(solution)/shard_map/ppermute | solution.py:188
  19.7 0.0 collective-permute-done.7
  19.7 1.1 %collective-permute-done.8 = f32[1,640]{1,0:T(1,128)S(1)} collective-permute-done((f32[1,640]{1,0:T(1,128)S(1)}, f32[1,640]{1,0:T(1,128)S(1)}, u32[]{:S(2)}, u32[]{:S(2)}) %collective-permute-start.8) | collective-permute-done | bytes 2592 | tf_op jit(solution)/shard_map/ppermute | solution.py:225
  20.8 0.0 copy-start.1
  20.8 0.0 collective-permute-done.4.refs_5_
  20.8 0.0 collective-permute-done.5.refs_2_
  20.8 1.5 %collective-permute-start.10 = (bf16[256,512]{1,0:T(8,128)(2,1)S(1)}, bf16[256,512]{1,0:T(8,128)(2,1)S(1)}, u32[]{:S(2)}, u32[]{:S(2)}) collective-permute-start(bf16[256,512]{1,0:T(8,128)(2,1)S(1)} %collective-permute-done.5.refs_2_), channel_id=1, source_target_pairs={{8,0},{16,8},{24,16},{28,24},{20,28},{12,20},{4,12},{0,4},{9,1},{1... | collective-permute-start | bytes 786440 | tf_op jit(solution)/shard_map/ppermute | solution.py:228
  22.4 0.5 %collective-permute-start.9 = (bf16[256,512]{1,0:T(8,128)(2,1)S(1)}, bf16[256,512]{1,0:T(8,128)(2,1)S(1)}, u32[]{:S(2)}, u32[]{:S(2)}) collective-permute-start(bf16[256,512]{1,0:T(8,128)(2,1)S(1)} %collective-permute-done.4.refs_5_), channel_id=1, source_target_pairs={{0,8},{8,16},{16,24},{24,28},{28,20},{20,12},{12,4},{4,0},{1,9},{9... | collective-permute-start | bytes 786440 | tf_op jit(solution)/shard_map/ppermute | solution.py:228
  23.0 1.1 %collective-permute-start.15 = (bf16[256,512]{1,0:T(8,128)(2,1)S(1)}, bf16[256,512]{1,0:T(8,128)(2,1)S(1)}, u32[]{:S(2)}, u32[]{:S(2)}) collective-permute-start(bf16[256,512]{1,0:T(8,128)(2,1)S(1)} %broadcast_select_fusion.refs_11_), channel_id=1, source_target_pairs={{0,2},{1,3},{2,0},{3,1},{4,6},{5,7},{6,4},{7,5},{8,10},{9,11},{10,... | collective-permute-start | bytes 786440 | tf_op jit(solution)/shard_map/ppermute | solution.py:188
  24.0 0.0 copy-done.1
  24.0 0.0 collective-permute-start.12
  24.0 2.6 %collective-permute-start.11 = (f32[2,640]{1,0:T(2,128)S(1)}, f32[2,640]{1,0:T(2,128)S(1)}, u32[]{:S(2)}, u32[]{:S(2)}) collective-permute-start(f32[2,640]{1,0:T(2,128)S(1)} %pad_maximum_fusion), channel_id=1, source_target_pairs={{0,16},{4,20},{8,24},{12,28},{16,0},{20,4},{24,8},{28,12},{1,17},{... | collective-permute-start | bytes 15368 | tf_op jit(solution)/shard_map/ppermute | solution.py:188
  26.7 1.9 %collective-permute-done.11 = f32[2,640]{1,0:T(2,128)S(1)} collective-permute-done((f32[2,640]{1,0:T(2,128)S(1)}, f32[2,640]{1,0:T(2,128)S(1)}, u32[]{:S(2)}, u32[]{:S(2)}) %collective-permute-start.11) | collective-permute-done | bytes 5152 | tf_op jit(solution)/shard_map/ppermute | solution.py:188
  28.6 0.0 collective-permute-start.13
  28.6 0.0 collective-permute-done.10.refs_3_
  28.6 0.6 %collective-permute-start.14 = (bf16[256,512]{1,0:T(8,128)(2,1)S(1)}, bf16[256,512]{1,0:T(8,128)(2,1)S(1)}, u32[]{:S(2)}, u32[]{:S(2)}) collective-permute-start(bf16[256,512]{1,0:T(8,128)(2,1)S(1)} %broadcast_select_fusion.refs_11_), channel_id=1, source_target_pairs={{0,1},{1,0},{2,3},{3,2},{4,5},{5,4},{6,7},{7,6},{8,9},{9,8},{10,11... | collective-permute-start | bytes 786440 | tf_op jit(solution)/shard_map/ppermute | solution.py:188
  29.1 0.0 collective-permute-done.9.refs_4_
  29.1 0.1 collective-permute-start.17
  29.2 0.2 collective-permute-done.15.refs_13_
  29.4 0.3 collective-permute-start.16
  29.7 0.0 collective-permute-done.12.refs_8_
  29.7 1.5 %collective-permute-start.18 = (bf16[128,512]{1,0:T(8,128)(2,1)S(1)}, bf16[128,512]{1,0:T(8,128)(2,1)S(1)}, u32[]{:S(2)}, u32[]{:S(2)}) collective-permute-start(bf16[128,512]{1,0:T(8,128)(2,1)S(1)} %slice.23), channel_id=1, source_target_pairs={{0,8},{8,16},{16,24},{24,28},{28,20},{20,12},{12,4},{4,0},{1,9},{9... | collective-permute-start | bytes 393224 | tf_op jit(solution)/shard_map/ppermute | solution.py:251
  31.2 0.0 collective-permute-done.17
  31.2 2.3 %collective-permute-start.19 = (bf16[128,512]{1,0:T(8,128)(2,1)S(1)}, bf16[128,512]{1,0:T(8,128)(2,1)S(1)}, u32[]{:S(2)}, u32[]{:S(2)}) collective-permute-start(bf16[128,512]{1,0:T(8,128)(2,1)S(1)} %slice.24), channel_id=1, source_target_pairs={{8,0},{16,8},{24,16},{28,24},{20,28},{12,20},{4,12},{0,4},{9,1},{1... | collective-permute-start | bytes 393224 | tf_op jit(solution)/shard_map/ppermute | solution.py:252
  33.5 0.0 collective-permute-done.13.refs_10_
  33.5 0.0 collective-permute-done.14.refs_12_
  33.5 0.0 collective-permute-done.16.refs_14_
  33.5 2.3 %shard_map.38 = (f32[512,512]{1,0:T(8,128)S(1)}, bf16[512,256]{1,0:T(8,128)(2,1)S(1)}) custom-call(bf16[256,512]{1,0:T(8,128)(2,1)S(1)} %copy-done.1, bf16[256,512]{1,0:T(8,128)(2,1)S(1)} %collective-permute-done.1.refs_1_, bf16[256,512]{1,0:T(8,128)(2,1)S(1)} %collective-permute-done.5.refs_2_, bf16[256,512]{1,0:T(8,128)(2,1)S(1)} %collective-permute-done.10.refs_3_, ...), custom_call_target="tpu_custom_call" | custom-call | flops 1073741824 | bytes 3145728 | tf_op jit(solution)/shard_map/pallas_call | solution.py:262
  35.8 0.7 %collective-permute-done.18.top_ref = bf16[128,512]{1,0:T(8,128)(2,1)S(1)} collective-permute-done((bf16[128,512]{1,0:T(8,128)(2,1)S(1)}, bf16[128,512]{1,0:T(8,128)(2,1)S(1)}, u32[]{:S(2)}, u32[]{:S(2)}) %collective-permute-start.18) | collective-permute-done | bytes 131104 | tf_op jit(solution)/shard_map/ppermute | solution.py:251
  36.5 0.1 collective-permute-done.19.bottom_ref
  36.6 0.6 %shard_map.39 = (f32[256,512]{1,0:T(8,128)S(1)}, f32[1,512]{1,0:T(1,128)S(1)}) custom-call(f32[512,512]{1,0:T(8,128)S(1)} %get-tuple-element.29.acc_ref, bf16[512,256]{1,0:T(8,128)(2,1)S(1)} %get-tuple-element.30.left_ref, bf16[128,512]{1,0:T(8,128)(2,1)S(1)} %collective-permute-done.18.top_ref, bf16[128,512]{1,0:T(8,128)(2,1)S(1)} %collective-permute-done.19.bottom_ref, ...), custom_call_target="tpu_custom_call" | custom-call | flops 134217728 | bytes 2097152 | tf_op jit(solution)/shard_map/pallas_call | solution.py:282
  37.2 2.5 %collective-permute-start.20 = (f32[1,512]{1,0:T(1,128)S(1)}, f32[1,512]{1,0:T(1,128)S(1)}, u32[]{:S(2)}, u32[]{:S(2)}) collective-permute-start(f32[1,512]{1,0:T(1,128)S(1)} %get-tuple-element.32), channel_id=1, source_target_pairs={{0,4},{4,0},{8,12},{12,8},{16,20},{20,16},{24,28},{28,24},{1,5},{5... | collective-permute-start | bytes 6152 | tf_op jit(solution)/shard_map/ppermute | solution.py:188
  39.7 1.6 %collective-permute-done.20 = f32[1,512]{1,0:T(1,128)S(1)} collective-permute-done((f32[1,512]{1,0:T(1,128)S(1)}, f32[1,512]{1,0:T(1,128)S(1)}, u32[]{:S(2)}, u32[]{:S(2)}) %collective-permute-start.20) | collective-permute-done | bytes 2080 | tf_op jit(solution)/shard_map/ppermute | solution.py:188
  41.3 1.2 %collective-permute-start.21 = (f32[1,512]{1,0:T(1,128)S(1)}, f32[1,512]{1,0:T(1,128)S(1)}, u32[]{:S(2)}, u32[]{:S(2)}) collective-permute-start(f32[1,512]{1,0:T(1,128)S(1)} %add.32), channel_id=1, source_target_pairs={{0,8},{4,12},{8,0},{12,4},{16,24},{20,28},{24,16},{28,20},{1,9},{5... | collective-permute-start | bytes 6152 | tf_op jit(solution)/shard_map/ppermute | solution.py:188
  42.5 2.4 %collective-permute-done.21 = f32[1,512]{1,0:T(1,128)S(1)} collective-permute-done((f32[1,512]{1,0:T(1,128)S(1)}, f32[1,512]{1,0:T(1,128)S(1)}, u32[]{:S(2)}, u32[]{:S(2)}) %collective-permute-start.21) | collective-permute-done | bytes 2080 | tf_op jit(solution)/shard_map/ppermute | solution.py:188
  44.9 0.9 %broadcast_multiply_fusion = f32[256,512]{1,0:T(8,128)} fusion(f32[256,512]{1,0:T(8,128)S(1)} %get-tuple-element.31, f32[512]{0:T(512)S(1)} %bitcast.1), kind=kLoop, calls=%fused_computation | loop fusion | flops 131072 | bytes 1050624 | tf_op jit(solution)/shard_map/mul | solution.py:302
  (12 shorter events, 0.1 us)
Async XLA Ops:
  0.0 11.6 %collective-permute-start = (bf16[256,512]{1,0:T(8,128)(2,1)}, bf16[256,512]{1,0:T(8,128)(2,1)S(1)}, u32[]{:S(2)}, u32[]{:S(2)}) collective-permute-start(bf16[256,512]{1,0:T(8,128)(2,1)} %refs_7_.1), channel_id=1, source_target_pairs={{0,8},{8,16},{16,24},{24,28},{28,20},{20,12},{12,4},{4,0},{1,9},{9... | collective-permute-start | bytes 786440 | tf_op jit(solution)/shard_map/ppermute | solution.py:228
  3.0 8.6 %collective-permute-start.1 = (bf16[256,512]{1,0:T(8,128)(2,1)}, bf16[256,512]{1,0:T(8,128)(2,1)S(1)}, u32[]{:S(2)}, u32[]{:S(2)}) collective-permute-start(bf16[256,512]{1,0:T(8,128)(2,1)} %refs_7_.1), channel_id=1, source_target_pairs={{8,0},{16,8},{24,16},{28,24},{20,28},{12,20},{4,12},{0,4},{9,1},{1... | collective-permute-start | bytes 786440 | tf_op jit(solution)/shard_map/ppermute | solution.py:228
  3.0 8.6 %collective-permute-start.3 = (bf16[256,512]{1,0:T(8,128)(2,1)}, bf16[256,512]{1,0:T(8,128)(2,1)S(1)}, u32[]{:S(2)}, u32[]{:S(2)}) collective-permute-start(bf16[256,512]{1,0:T(8,128)(2,1)} %refs_7_.1), channel_id=1, source_target_pairs={{0,2},{1,3},{2,0},{3,1},{4,6},{5,7},{6,4},{7,5},{8,10},{9,11},{10,... | collective-permute-start | bytes 786440 | tf_op jit(solution)/shard_map/ppermute | solution.py:188
  5.0 1.0 %copy-start = (bf16[256,512]{1,0:T(8,128)(2,1)S(1)}, bf16[256,512]{1,0:T(8,128)(2,1)}, u32[]{:S(2)}) copy-start(bf16[256,512]{1,0:T(8,128)(2,1)} %refs_7_.1) | copy-start | bytes 786436
  6.0 0.7 %copy-start.2 = (s32[1,2]{1,0:T(1,128)S(1)}, s32[1,2]{1,0:T(1,128)}, u32[]{:S(2)}) copy-start(s32[1,2]{1,0:T(1,128)} %pattern_hbm.1) | copy-start | bytes 28
  6.6 0.7 %copy-start.3 = (s32[1,2]{1,0:T(1,128)S(1)}, s32[1,2]{1,0:T(1,128)}, u32[]{:S(2)}) copy-start(s32[1,2]{1,0:T(1,128)} %keep_hbm.1) | copy-start | bytes 28
  7.9 3.7 %collective-permute-start.2 = (f32[1,640]{1,0:T(1,128)S(1)}, f32[1,640]{1,0:T(1,128)S(1)}, u32[]{:S(2)}, u32[]{:S(2)}) collective-permute-start(f32[1,640]{1,0:T(1,128)S(1)} %shard_map.37), channel_id=1, source_target_pairs={{0,4},{4,0},{8,12},{12,8},{16,20},{20,16},{24,28},{28,24},{1,5},{5... | collective-permute-start | bytes 7688 | tf_op jit(solution)/shard_map/ppermute | solution.py:188
  11.6 9.2 %collective-permute-start.4 = (bf16[256,512]{1,0:T(8,128)(2,1)S(1)}, bf16[256,512]{1,0:T(8,128)(2,1)S(1)}, u32[]{:S(2)}, u32[]{:S(2)}) collective-permute-start(bf16[256,512]{1,0:T(8,128)(2,1)S(1)} %collective-permute-done.refs_6_), channel_id=1, source_target_pairs={{0,8},{8,16},{16,24},{24,28},{28,20},{20,12},{12,4},{4,0},{1,9},{9... | collective-permute-start | bytes 786440 | tf_op jit(solution)/shard_map/ppermute | solution.py:228
  13.3 7.6 %collective-permute-start.5 = (bf16[256,512]{1,0:T(8,128)(2,1)S(1)}, bf16[256,512]{1,0:T(8,128)(2,1)S(1)}, u32[]{:S(2)}, u32[]{:S(2)}) collective-permute-start(bf16[256,512]{1,0:T(8,128)(2,1)S(1)} %collective-permute-done.1.refs_1_), channel_id=1, source_target_pairs={{8,0},{16,8},{24,16},{28,24},{20,28},{12,20},{4,12},{0,4},{9,1},{1... | collective-permute-start | bytes 786440 | tf_op jit(solution)/shard_map/ppermute | solution.py:228
  13.7 5.9 %collective-permute-start.6 = (f32[1,640]{1,0:T(1,128)S(1)}, f32[1,640]{1,0:T(1,128)S(1)}, u32[]{:S(2)}, u32[]{:S(2)}) collective-permute-start(f32[1,640]{1,0:T(1,128)S(1)} %add.26), channel_id=1, source_target_pairs={{0,8},{4,12},{8,0},{12,4},{16,24},{20,28},{24,16},{28,20},{1,9},{5... | collective-permute-start | bytes 7688 | tf_op jit(solution)/shard_map/ppermute | solution.py:188
  15.3 4.4 %collective-permute-start.7 = (f32[1,640]{1,0:T(1,128)S(1)}, f32[1,640]{1,0:T(1,128)S(1)}, u32[]{:S(2)}, u32[]{:S(2)}) collective-permute-start(f32[1,640]{1,0:T(1,128)S(1)} %add.26), channel_id=1, source_target_pairs={{0,2},{1,3},{2,0},{3,1},{4,6},{5,7},{6,4},{7,5},{8,10},{9,11},{10,... | collective-permute-start | bytes 7688 | tf_op jit(solution)/shard_map/ppermute | solution.py:188
  16.3 4.5 %collective-permute-start.8 = (f32[1,640]{1,0:T(1,128)S(1)}, f32[1,640]{1,0:T(1,128)S(1)}, u32[]{:S(2)}, u32[]{:S(2)}) collective-permute-start(f32[1,640]{1,0:T(1,128)S(1)} %add.26), channel_id=1, source_target_pairs={{0,10},{1,11},{2,8},{3,9},{4,14},{5,15},{6,12},{7,13},{8,2},{9,3},... | collective-permute-start | bytes 7688 | tf_op jit(solution)/shard_map/ppermute | solution.py:225
  20.8 3.2 %copy-start.1 = (bf16[256,512]{1,0:T(8,128)(2,1)S(1)}, bf16[256,512]{1,0:T(8,128)(2,1)}, u32[]{:S(2)}) copy-start(bf16[256,512]{1,0:T(8,128)(2,1)} %refs_7_.1) | copy-start | bytes 786436
  20.8 7.7 %collective-permute-start.10 = (bf16[256,512]{1,0:T(8,128)(2,1)S(1)}, bf16[256,512]{1,0:T(8,128)(2,1)S(1)}, u32[]{:S(2)}, u32[]{:S(2)}) collective-permute-start(bf16[256,512]{1,0:T(8,128)(2,1)S(1)} %collective-permute-done.5.refs_2_), channel_id=1, source_target_pairs={{8,0},{16,8},{24,16},{28,24},{20,28},{12,20},{4,12},{0,4},{9,1},{1... | collective-permute-start | bytes 786440 | tf_op jit(solution)/shard_map/ppermute | solution.py:228
  22.4 6.8 %collective-permute-start.9 = (bf16[256,512]{1,0:T(8,128)(2,1)S(1)}, bf16[256,512]{1,0:T(8,128)(2,1)S(1)}, u32[]{:S(2)}, u32[]{:S(2)}) collective-permute-start(bf16[256,512]{1,0:T(8,128)(2,1)S(1)} %collective-permute-done.4.refs_5_), channel_id=1, source_target_pairs={{0,8},{8,16},{16,24},{24,28},{28,20},{20,12},{12,4},{4,0},{1,9},{9... | collective-permute-start | bytes 786440 | tf_op jit(solution)/shard_map/ppermute | solution.py:228
  23.0 6.4 %collective-permute-start.15 = (bf16[256,512]{1,0:T(8,128)(2,1)S(1)}, bf16[256,512]{1,0:T(8,128)(2,1)S(1)}, u32[]{:S(2)}, u32[]{:S(2)}) collective-permute-start(bf16[256,512]{1,0:T(8,128)(2,1)S(1)} %broadcast_select_fusion.refs_11_), channel_id=1, source_target_pairs={{0,2},{1,3},{2,0},{3,1},{4,6},{5,7},{6,4},{7,5},{8,10},{9,11},{10,... | collective-permute-start | bytes 786440 | tf_op jit(solution)/shard_map/ppermute | solution.py:188
  24.0 5.7 %collective-permute-start.12 = (bf16[256,512]{1,0:T(8,128)(2,1)S(1)}, bf16[256,512]{1,0:T(8,128)(2,1)S(1)}, u32[]{:S(2)}, u32[]{:S(2)}) collective-permute-start(bf16[256,512]{1,0:T(8,128)(2,1)S(1)} %copy-done.1), channel_id=1, source_target_pairs={{0,1},{1,0},{2,3},{3,2},{4,5},{5,4},{6,7},{7,6},{8,9},{9,8},{10,11... | collective-permute-start | bytes 786440 | tf_op jit(solution)/shard_map/ppermute | solution.py:188
  24.0 4.5 %collective-permute-start.11 = (f32[2,640]{1,0:T(2,128)S(1)}, f32[2,640]{1,0:T(2,128)S(1)}, u32[]{:S(2)}, u32[]{:S(2)}) collective-permute-start(f32[2,640]{1,0:T(2,128)S(1)} %pad_maximum_fusion), channel_id=1, source_target_pairs={{0,16},{4,20},{8,24},{12,28},{16,0},{20,4},{24,8},{28,12},{1,17},{... | collective-permute-start | bytes 15368 | tf_op jit(solution)/shard_map/ppermute | solution.py:188
  28.6 4.9 %collective-permute-start.13 = (bf16[256,512]{1,0:T(8,128)(2,1)S(1)}, bf16[256,512]{1,0:T(8,128)(2,1)S(1)}, u32[]{:S(2)}, u32[]{:S(2)}) collective-permute-start(bf16[256,512]{1,0:T(8,128)(2,1)S(1)} %collective-permute-done.3.refs_9_), channel_id=1, source_target_pairs={{0,1},{1,0},{2,3},{3,2},{4,5},{5,4},{6,7},{7,6},{8,9},{9,8},{10,11... | collective-permute-start | bytes 786440 | tf_op jit(solution)/shard_map/ppermute | solution.py:188
  28.6 4.9 %collective-permute-start.14 = (bf16[256,512]{1,0:T(8,128)(2,1)S(1)}, bf16[256,512]{1,0:T(8,128)(2,1)S(1)}, u32[]{:S(2)}, u32[]{:S(2)}) collective-permute-start(bf16[256,512]{1,0:T(8,128)(2,1)S(1)} %broadcast_select_fusion.refs_11_), channel_id=1, source_target_pairs={{0,1},{1,0},{2,3},{3,2},{4,5},{5,4},{6,7},{7,6},{8,9},{9,8},{10,11... | collective-permute-start | bytes 786440 | tf_op jit(solution)/shard_map/ppermute | solution.py:188
  29.1 2.0 %collective-permute-start.17 = (f32[2,640]{1,0:T(2,128)S(1)}, f32[2,640]{1,0:T(2,128)S(1)}, u32[]{:S(2)}, u32[]{:S(2)}) collective-permute-start(f32[2,640]{1,0:T(2,128)S(1)} %add.29), channel_id=1, source_target_pairs={{0,1},{1,0},{2,3},{3,2},{4,5},{5,4},{6,7},{7,6},{8,9},{9,8},{10,11... | collective-permute-start | bytes 15368 | tf_op jit(solution)/shard_map/ppermute | solution.py:188
  29.4 4.1 %collective-permute-start.16 = (bf16[256,512]{1,0:T(8,128)(2,1)S(1)}, bf16[256,512]{1,0:T(8,128)(2,1)S(1)}, u32[]{:S(2)}, u32[]{:S(2)}) collective-permute-start(bf16[256,512]{1,0:T(8,128)(2,1)S(1)} %collective-permute-done.15.refs_13_), channel_id=1, source_target_pairs={{0,1},{1,0},{2,3},{3,2},{4,5},{5,4},{6,7},{7,6},{8,9},{9,8},{10,11... | collective-permute-start | bytes 786440 | tf_op jit(solution)/shard_map/ppermute | solution.py:188
  29.7 6.8 %collective-permute-start.18 = (bf16[128,512]{1,0:T(8,128)(2,1)S(1)}, bf16[128,512]{1,0:T(8,128)(2,1)S(1)}, u32[]{:S(2)}, u32[]{:S(2)}) collective-permute-start(bf16[128,512]{1,0:T(8,128)(2,1)S(1)} %slice.23), channel_id=1, source_target_pairs={{0,8},{8,16},{16,24},{24,28},{28,20},{20,12},{12,4},{4,0},{1,9},{9... | collective-permute-start | bytes 393224 | tf_op jit(solution)/shard_map/ppermute | solution.py:251
  31.2 5.4 %collective-permute-start.19 = (bf16[128,512]{1,0:T(8,128)(2,1)S(1)}, bf16[128,512]{1,0:T(8,128)(2,1)S(1)}, u32[]{:S(2)}, u32[]{:S(2)}) collective-permute-start(bf16[128,512]{1,0:T(8,128)(2,1)S(1)} %slice.24), channel_id=1, source_target_pairs={{8,0},{16,8},{24,16},{28,24},{20,28},{12,20},{4,12},{0,4},{9,1},{1... | collective-permute-start | bytes 393224 | tf_op jit(solution)/shard_map/ppermute | solution.py:252
  37.2 4.1 %collective-permute-start.20 = (f32[1,512]{1,0:T(1,128)S(1)}, f32[1,512]{1,0:T(1,128)S(1)}, u32[]{:S(2)}, u32[]{:S(2)}) collective-permute-start(f32[1,512]{1,0:T(1,128)S(1)} %get-tuple-element.32), channel_id=1, source_target_pairs={{0,4},{4,0},{8,12},{12,8},{16,20},{20,16},{24,28},{28,24},{1,5},{5... | collective-permute-start | bytes 6152 | tf_op jit(solution)/shard_map/ppermute | solution.py:188
  41.3 3.6 %collective-permute-start.21 = (f32[1,512]{1,0:T(1,128)S(1)}, f32[1,512]{1,0:T(1,128)S(1)}, u32[]{:S(2)}, u32[]{:S(2)}) collective-permute-start(f32[1,512]{1,0:T(1,128)S(1)} %add.32), channel_id=1, source_target_pairs={{0,8},{4,12},{8,0},{12,4},{16,24},{20,28},{24,16},{28,20},{1,9},{5... | collective-permute-start | bytes 6152 | tf_op jit(solution)/shard_map/ppermute | solution.py:188

commit v3 on v2

--- a/solution.py
+++ b/solution.py
@@ -216,36 +216,30 @@
         compiler_params=pltpu.CompilerParams(vmem_limit_bytes=8 * tile * cols_dev * 2),
     )(flow, pattern, keep)
 
-    ring = {0: flow}
-    behind = ahead = flow
-    bit_count = rows_n.bit_length() - 1
-    other_mate = None
     def send_both(value, bit):
         pairs = [(r * cols_n + c, (r ^ bit) * cols_n + (c ^ (cols_n // 2))) for r in range(rows_n) for c in range(cols_n)]
         return lax.ppermute(value, ("row", "col"), pairs)
 
+    ring = {0: flow}
+    behind = ahead = flow
+    bits = [1 << b for b in range(rows_n.bit_length() - 1)]
+    bits[:2] = bits[1::-1]
     for s in range(1, half_ring):
         behind, ahead = lax.ppermute(behind, "row", up), lax.ppermute(ahead, "row", down)
+        if s == 2:
+            near, far = note + send_row(note, bits[1]), send_far_col(note) + send_both(note, bits[1])
+            note = jnp.concatenate([near, far], axis=0)
+        elif s <= len(bits):
+            note = note + send_row(note, bits[s - 1])
         if s == 1:
-            note = note + send_row(note, 1)
             mine = send_far_col(flow)
-        elif s == 2:
-            near, far = note + send_row(note, 2), send_far_col(note) + send_both(note, 2)
-            note = jnp.concatenate([near, far], axis=0)
-        elif s <= bit_count:
-            note = note + send_row(note, 1 << (s - 1))
-        if s == quarter + 1:
-            other_mate = send_far_col(mate)
-        if s <= bit_count:
-            if s == 1:
-                behind, ahead, note, mine = lax.optimization_barrier((behind, ahead, note, mine))
-            else:
-                behind, ahead, note = lax.optimization_barrier((behind, ahead, note))
+            behind, ahead, note, mine = lax.optimization_barrier((behind, ahead, note, mine))
         else:
-            behind, ahead = lax.optimization_barrier((behind, ahead))
+            behind, ahead, note = lax.optimization_barrier((behind, ahead, note))
         ring[s], ring[rows_n - s] = ahead, behind
         if s == quarter:
             mate = jnp.where(position % half_ring < quarter, ahead, behind)
+            other_mate = send_far_col(mate)
     beside_note = send(note, "col", cols_n, 1)
     half = tile // 2
     top = lax.ppermute(behind[:half], "row", up)

time: 45.9 us -> 45.4 us (0.989)
  starting transfers between devices: 26.3 us -> 24.6 us
  waiting for transfers between devices: 12.5 us -> 13.8 us
    ppermute x1, starting transfers between devices: 2.31 us -> 1.13 us  [body(): bottom = lax.ppermute(ahead[half:], 'row', down)]
    ppermute x1, waiting for transfers between devices: 0.1 us -> 1.2 us  [body(): bottom = lax.ppermute(ahead[half:], 'row', down)]
    ppermute x3, starting transfers between devices: 1.99 us -> 1.04 us  [body(): lax.ppermute(ahead, 'row', down)]
    ppermute x3, starting transfers between devices: 5.19 us -> 6.15 us  [body(): lax.ppermute(behind, 'row', up)]
    ppermute x1, waiting for transfers between devices: 1.11 us -> 1.93 us  [send_both(): return lax.ppermute(value, ('row', 'col'), pairs)]
    ppermute x13, starting transfers between devices: 14.5 us -> 13.7 us  [send(): return lax.ppermute(value, axis, [(i, i ^ bit) for i in range(count)])]
    ppermute x13, waiting for transfers between devices: 10.6 us -> 9.95 us  [send(): return lax.ppermute(value, axis, [(i, i ^ bit) for i in range(count)])]
  transfers between devices with their start and end apart: 22 -> 22, of which waited for: 9 -> 10; matrix products, arithmetic and copies ran while one was open for 0% -> 0% of each run, Pallas kernels for 7% -> 7%
where the time goes in v3:
time: 45.4 us; the launch traced here: 45.3 us
  starting transfers between devices  24.6 us (54%)
  waiting for transfers between devices  13.8 us (30%)
  Pallas kernels  3.54 us (8%)
  local copies, waits for them, and re-layouts  2.33 us (5%)
  other arithmetic  0.93 us (2%)
    ppermute x13, starting transfers between devices, send(): return lax.ppermute(value, axis, [(i, i ^ bit) for i in range(count)])  13.7 us
    ppermute x13, waiting for transfers between devices, send(): return lax.ppermute(value, axis, [(i, i ^ bit) for i in range(count)])  9.95 us
    ppermute x3, starting transfers between devices, body(): lax.ppermute(behind, 'row', up)  6.15 us
    pallas_call x1, Pallas kernels, body(): pl.pallas_call(functools.partial(square_kernel, rows_n, cols_n, half_ring...  2.33 us
    unnamed x8, local copies, waits for them, and re-layouts  2.3 us
    ppermute x1, waiting for transfers between devices, send_both(): return lax.ppermute(value, ('row', 'col'), pairs)  1.93 us
    ppermute x1, starting transfers between devices, body(): top = lax.ppermute(behind[:half], 'row', up)  1.63 us
    ppermute x1, waiting for transfers between devices, body(): bottom = lax.ppermute(ahead[half:], 'row', down)  1.2 us
  transfers between devices with their start and end apart: 22, of which 10 were waited for; matrix products, arithmetic and copies ran while one was open for 0% of the time, Pallas kernels for 7%

profile of v3, /device:TPU:0, one launch (start us, length us, event | category | flops | bytes accessed | tf_op | source)
XLA Modules:
  0.0 45.3 jit_solution(16352456536517690838)
XLA Ops:
  0.0 3.0 %collective-permute-start = (bf16[256,512]{1,0:T(8,128)(2,1)}, bf16[256,512]{1,0:T(8,128)(2,1)S(1)}, u32[]{:S(2)}, u32[]{:S(2)}) collective-permute-start(bf16[256,512]{1,0:T(8,128)(2,1)} %refs_7_.1), channel_id=1, source_target_pairs={{0,8},{8,16},{16,24},{24,28},{28,20},{20,12},{12,4},{4,0},{1,9},{9... | collective-permute-start | bytes 786440 | tf_op jit(solution)/shard_map/ppermute | solution.py:228
  3.0 0.0 collective-permute-start.1
  3.0 2.0 %collective-permute-start.3 = (bf16[256,512]{1,0:T(8,128)(2,1)}, bf16[256,512]{1,0:T(8,128)(2,1)S(1)}, u32[]{:S(2)}, u32[]{:S(2)}) collective-permute-start(bf16[256,512]{1,0:T(8,128)(2,1)} %refs_7_.1), channel_id=1, source_target_pairs={{0,2},{1,3},{2,0},{3,1},{4,6},{5,7},{6,4},{7,5},{8,10},{9,11},{10,... | collective-permute-start | bytes 786440 | tf_op jit(solution)/shard_map/ppermute | solution.py:188
  5.0 0.0 copy-start
  5.0 1.0 %copy-done = bf16[256,512]{1,0:T(8,128)(2,1)S(1)} copy-done((bf16[256,512]{1,0:T(8,128)(2,1)S(1)}, bf16[256,512]{1,0:T(8,128)(2,1)}, u32[]{:S(2)}) %copy-start) | copy-done | bytes 262168
  6.0 0.0 copy-start.2
  6.0 0.7 %copy-done.2 = s32[1,2]{1,0:T(1,128)S(1)} copy-done((s32[1,2]{1,0:T(1,128)S(1)}, s32[1,2]{1,0:T(1,128)}, u32[]{:S(2)}) %copy-start.2) | copy-done | bytes 32
  6.6 0.0 copy-start.3
  6.6 0.7 %copy-done.3 = s32[1,2]{1,0:T(1,128)S(1)} copy-done((s32[1,2]{1,0:T(1,128)S(1)}, s32[1,2]{1,0:T(1,128)}, u32[]{:S(2)}) %copy-start.3) | copy-done | bytes 32
  7.3 0.6 %shard_map.37 = f32[1,640]{1,0:T(1,128)S(1)} custom-call(bf16[256,512]{1,0:T(8,128)(2,1)S(1)} %copy-done, s32[1,2]{1,0:T(1,128)S(1)} %copy-done.2, s32[1,2]{1,0:T(1,128)S(1)} %copy-done.3), custom_call_target="tpu_custom_call" | custom-call | tf_op jit(solution)/shard_map/pallas_call | solution.py:205
  7.9 1.6 %collective-permute-start.2 = (f32[1,640]{1,0:T(1,128)S(1)}, f32[1,640]{1,0:T(1,128)S(1)}, u32[]{:S(2)}, u32[]{:S(2)}) collective-permute-start(f32[1,640]{1,0:T(1,128)S(1)} %shard_map.37), channel_id=1, source_target_pairs={{0,8},{4,12},{8,0},{12,4},{16,24},{20,28},{24,16},{28,20},{1,9},{5... | collective-permute-start | bytes 7688 | tf_op jit(solution)/shard_map/ppermute | solution.py:188
  9.6 2.0 %collective-permute-done.2 = f32[1,640]{1,0:T(1,128)S(1)} collective-permute-done((f32[1,640]{1,0:T(1,128)S(1)}, f32[1,640]{1,0:T(1,128)S(1)}, u32[]{:S(2)}, u32[]{:S(2)}) %collective-permute-start.2) | collective-permute-done | bytes 2592 | tf_op jit(solution)/shard_map/ppermute | solution.py:188
  11.6 0.0 collective-permute-done.refs_6_
  11.6 0.0 collective-permute-done.1.refs_1_
  11.6 0.0 collective-permute-done.3.refs_9_
  11.6 1.6 %collective-permute-start.4 = (bf16[256,512]{1,0:T(8,128)(2,1)S(1)}, bf16[256,512]{1,0:T(8,128)(2,1)S(1)}, u32[]{:S(2)}, u32[]{:S(2)}) collective-permute-start(bf16[256,512]{1,0:T(8,128)(2,1)S(1)} %collective-permute-done.refs_6_), channel_id=1, source_target_pairs={{0,8},{8,16},{16,24},{24,28},{28,20},{20,12},{12,4},{4,0},{1,9},{9... | collective-permute-start | bytes 786440 | tf_op jit(solution)/shard_map/ppermute | solution.py:228
  13.3 0.4 collective-permute-start.5
  13.7 1.5 %collective-permute-start.6 = (f32[1,640]{1,0:T(1,128)S(1)}, f32[1,640]{1,0:T(1,128)S(1)}, u32[]{:S(2)}, u32[]{:S(2)}) collective-permute-start(f32[1,640]{1,0:T(1,128)S(1)} %add.26), channel_id=1, source_target_pairs={{0,4},{4,0},{8,12},{12,8},{16,20},{20,16},{24,28},{28,24},{1,5},{5... | collective-permute-start | bytes 7688 | tf_op jit(solution)/shard_map/ppermute | solution.py:188
  15.2 1.0 %collective-permute-start.7 = (f32[1,640]{1,0:T(1,128)S(1)}, f32[1,640]{1,0:T(1,128)S(1)}, u32[]{:S(2)}, u32[]{:S(2)}) collective-permute-start(f32[1,640]{1,0:T(1,128)S(1)} %add.26), channel_id=1, source_target_pairs={{0,2},{1,3},{2,0},{3,1},{4,6},{5,7},{6,4},{7,5},{8,10},{9,11},{10,... | collective-permute-start | bytes 7688 | tf_op jit(solution)/shard_map/ppermute | solution.py:188
  16.2 1.0 %collective-permute-start.8 = (f32[1,640]{1,0:T(1,128)S(1)}, f32[1,640]{1,0:T(1,128)S(1)}, u32[]{:S(2)}, u32[]{:S(2)}) collective-permute-start(f32[1,640]{1,0:T(1,128)S(1)} %add.26), channel_id=1, source_target_pairs={{0,6},{1,7},{2,4},{3,5},{4,2},{5,3},{6,0},{7,1},{8,14},{9,15},{10,... | collective-permute-start | bytes 7688 | tf_op jit(solution)/shard_map/ppermute | solution.py:221
  17.2 1.0 %collective-permute-done.6 = f32[1,640]{1,0:T(1,128)S(1)} collective-permute-done((f32[1,640]{1,0:T(1,128)S(1)}, f32[1,640]{1,0:T(1,128)S(1)}, u32[]{:S(2)}, u32[]{:S(2)}) %collective-permute-start.6) | collective-permute-done | bytes 2592 | tf_op jit(solution)/shard_map/ppermute | solution.py:188
  18.2 0.6 %collective-permute-done.7 = f32[1,640]{1,0:T(1,128)S(1)} collective-permute-done((f32[1,640]{1,0:T(1,128)S(1)}, f32[1,640]{1,0:T(1,128)S(1)}, u32[]{:S(2)}, u32[]{:S(2)}) %collective-permute-start.7) | collective-permute-done | bytes 2592 | tf_op jit(solution)/shard_map/ppermute | solution.py:188
  18.8 1.9 %collective-permute-done.8 = f32[1,640]{1,0:T(1,128)S(1)} collective-permute-done((f32[1,640]{1,0:T(1,128)S(1)}, f32[1,640]{1,0:T(1,128)S(1)}, u32[]{:S(2)}, u32[]{:S(2)}) %collective-permute-start.8) | collective-permute-done | bytes 2592 | tf_op jit(solution)/shard_map/ppermute | solution.py:221
  20.7 0.0 copy-start.1
  20.8 0.0 collective-permute-done.4.refs_5_
  20.8 0.0 collective-permute-done.5.refs_2_
  20.8 0.6 %collective-permute-start.10 = (bf16[256,512]{1,0:T(8,128)(2,1)S(1)}, bf16[256,512]{1,0:T(8,128)(2,1)S(1)}, u32[]{:S(2)}, u32[]{:S(2)}) collective-permute-start(bf16[256,512]{1,0:T(8,128)(2,1)S(1)} %collective-permute-done.5.refs_2_), channel_id=1, source_target_pairs={{8,0},{16,8},{24,16},{28,24},{20,28},{12,20},{4,12},{0,4},{9,1},{1... | collective-permute-start | bytes 786440 | tf_op jit(solution)/shard_map/ppermute | solution.py:228
  21.4 1.5 %collective-permute-start.9 = (bf16[256,512]{1,0:T(8,128)(2,1)S(1)}, bf16[256,512]{1,0:T(8,128)(2,1)S(1)}, u32[]{:S(2)}, u32[]{:S(2)}) collective-permute-start(bf16[256,512]{1,0:T(8,128)(2,1)S(1)} %collective-permute-done.4.refs_5_), channel_id=1, source_target_pairs={{0,8},{8,16},{16,24},{24,28},{28,20},{20,12},{12,4},{4,0},{1,9},{9... | collective-permute-start | bytes 786440 | tf_op jit(solution)/shard_map/ppermute | solution.py:228
  22.9 1.1 %collective-permute-start.15 = (bf16[256,512]{1,0:T(8,128)(2,1)S(1)}, bf16[256,512]{1,0:T(8,128)(2,1)S(1)}, u32[]{:S(2)}, u32[]{:S(2)}) collective-permute-start(bf16[256,512]{1,0:T(8,128)(2,1)S(1)} %broadcast_select_fusion.refs_11_), channel_id=1, source_target_pairs={{0,2},{1,3},{2,0},{3,1},{4,6},{5,7},{6,4},{7,5},{8,10},{9,11},{10,... | collective-permute-start | bytes 786440 | tf_op jit(solution)/shard_map/ppermute | solution.py:188
  24.0 0.0 copy-done.1
  24.0 0.0 collective-permute-start.12
  24.0 2.6 %collective-permute-start.11 = (f32[2,640]{1,0:T(2,128)S(1)}, f32[2,640]{1,0:T(2,128)S(1)}, u32[]{:S(2)}, u32[]{:S(2)}) collective-permute-start(f32[2,640]{1,0:T(2,128)S(1)} %pad_maximum_fusion), channel_id=1, source_target_pairs={{0,16},{4,20},{8,24},{12,28},{16,0},{20,4},{24,8},{28,12},{1,17},{... | collective-permute-start | bytes 15368 | tf_op jit(solution)/shard_map/ppermute | solution.py:188
  26.5 1.9 %collective-permute-done.11 = f32[2,640]{1,0:T(2,128)S(1)} collective-permute-done((f32[2,640]{1,0:T(2,128)S(1)}, f32[2,640]{1,0:T(2,128)S(1)}, u32[]{:S(2)}, u32[]{:S(2)}) %collective-permute-start.11) | collective-permute-done | bytes 5152 | tf_op jit(solution)/shard_map/ppermute | solution.py:188
  28.5 0.0 collective-permute-start.13
  28.5 0.0 collective-permute-done.10.refs_3_
  28.5 0.6 %collective-permute-start.14 = (bf16[256,512]{1,0:T(8,128)(2,1)S(1)}, bf16[256,512]{1,0:T(8,128)(2,1)S(1)}, u32[]{:S(2)}, u32[]{:S(2)}) collective-permute-start(bf16[256,512]{1,0:T(8,128)(2,1)S(1)} %broadcast_select_fusion.refs_11_), channel_id=1, source_target_pairs={{0,1},{1,0},{2,3},{3,2},{4,5},{5,4},{6,7},{7,6},{8,9},{9,8},{10,11... | collective-permute-start | bytes 786440 | tf_op jit(solution)/shard_map/ppermute | solution.py:188
  29.1 0.0 collective-permute-done.9.refs_4_
  29.1 0.1 collective-permute-start.17
  29.1 0.2 collective-permute-done.15.refs_13_
  29.3 0.2 collective-permute-start.16
  29.6 0.0 collective-permute-done.12.refs_8_
  29.6 1.6 %collective-permute-start.18 = (bf16[128,512]{1,0:T(8,128)(2,1)S(1)}, bf16[128,512]{1,0:T(8,128)(2,1)S(1)}, u32[]{:S(2)}, u32[]{:S(2)}) collective-permute-start(bf16[128,512]{1,0:T(8,128)(2,1)S(1)} %slice.23), channel_id=1, source_target_pairs={{0,8},{8,16},{16,24},{24,28},{28,20},{20,12},{12,4},{4,0},{1,9},{9... | collective-permute-start | bytes 393224 | tf_op jit(solution)/shard_map/ppermute | solution.py:245
  31.2 0.0 collective-permute-done.17
  31.3 1.1 %collective-permute-start.19 = (bf16[128,512]{1,0:T(8,128)(2,1)S(1)}, bf16[128,512]{1,0:T(8,128)(2,1)S(1)}, u32[]{:S(2)}, u32[]{:S(2)}) collective-permute-start(bf16[128,512]{1,0:T(8,128)(2,1)S(1)} %slice.24), channel_id=1, source_target_pairs={{8,0},{16,8},{24,16},{28,24},{20,28},{12,20},{4,12},{0,4},{9,1},{1... | collective-permute-start | bytes 393224 | tf_op jit(solution)/shard_map/ppermute | solution.py:246
  32.4 0.0 collective-permute-done.13.refs_10_
  32.4 0.0 collective-permute-done.14.refs_12_
  32.4 0.0 collective-permute-done.16.refs_14_
  32.4 2.3 %shard_map.38 = (f32[512,512]{1,0:T(8,128)S(1)}, bf16[512,256]{1,0:T(8,128)(2,1)S(1)}) custom-call(bf16[256,512]{1,0:T(8,128)(2,1)S(1)} %copy-done.1, bf16[256,512]{1,0:T(8,128)(2,1)S(1)} %collective-permute-done.1.refs_1_, bf16[256,512]{1,0:T(8,128)(2,1)S(1)} %collective-permute-done.5.refs_2_, bf16[256,512]{1,0:T(8,128)(2,1)S(1)} %collective-permute-done.10.refs_3_, ...), custom_call_target="tpu_custom_call" | custom-call | flops 1073741824 | bytes 3145728 | tf_op jit(solution)/shard_map/pallas_call | solution.py:256
  34.8 0.7 %collective-permute-done.18.top_ref = bf16[128,512]{1,0:T(8,128)(2,1)S(1)} collective-permute-done((bf16[128,512]{1,0:T(8,128)(2,1)S(1)}, bf16[128,512]{1,0:T(8,128)(2,1)S(1)}, u32[]{:S(2)}, u32[]{:S(2)}) %collective-permute-start.18) | collective-permute-done | bytes 131104 | tf_op jit(solution)/shard_map/ppermute | solution.py:245
  35.4 1.2 %collective-permute-done.19.bottom_ref = bf16[128,512]{1,0:T(8,128)(2,1)S(1)} collective-permute-done((bf16[128,512]{1,0:T(8,128)(2,1)S(1)}, bf16[128,512]{1,0:T(8,128)(2,1)S(1)}, u32[]{:S(2)}, u32[]{:S(2)}) %collective-permute-start.19) | collective-permute-done | bytes 131104 | tf_op jit(solution)/shard_map/ppermute | solution.py:246
  36.6 0.6 %shard_map.39 = (f32[256,512]{1,0:T(8,128)S(1)}, f32[1,512]{1,0:T(1,128)S(1)}) custom-call(f32[512,512]{1,0:T(8,128)S(1)} %get-tuple-element.29.acc_ref, bf16[512,256]{1,0:T(8,128)(2,1)S(1)} %get-tuple-element.30.left_ref, bf16[128,512]{1,0:T(8,128)(2,1)S(1)} %collective-permute-done.18.top_ref, bf16[128,512]{1,0:T(8,128)(2,1)S(1)} %collective-permute-done.19.bottom_ref, ...), custom_call_target="tpu_custom_call" | custom-call | flops 134217728 | bytes 2097152 | tf_op jit(solution)/shard_map/pallas_call | solution.py:276
  37.2 1.4 %collective-permute-start.20 = (f32[1,512]{1,0:T(1,128)S(1)}, f32[1,512]{1,0:T(1,128)S(1)}, u32[]{:S(2)}, u32[]{:S(2)}) collective-permute-start(f32[1,512]{1,0:T(1,128)S(1)} %get-tuple-element.32), channel_id=1, source_target_pairs={{0,4},{4,0},{8,12},{12,8},{16,20},{20,16},{24,28},{28,24},{1,5},{5... | collective-permute-start | bytes 6152 | tf_op jit(solution)/shard_map/ppermute | solution.py:188
  38.6 2.2 %collective-permute-done.20 = f32[1,512]{1,0:T(1,128)S(1)} collective-permute-done((f32[1,512]{1,0:T(1,128)S(1)}, f32[1,512]{1,0:T(1,128)S(1)}, u32[]{:S(2)}, u32[]{:S(2)}) %collective-permute-start.20) | collective-permute-done | bytes 2080 | tf_op jit(solution)/shard_map/ppermute | solution.py:188
  40.8 1.6 %collective-permute-start.21 = (f32[1,512]{1,0:T(1,128)S(1)}, f32[1,512]{1,0:T(1,128)S(1)}, u32[]{:S(2)}, u32[]{:S(2)}) collective-permute-start(f32[1,512]{1,0:T(1,128)S(1)} %add.32), channel_id=1, source_target_pairs={{0,8},{4,12},{8,0},{12,4},{16,24},{20,28},{24,16},{28,20},{1,9},{5... | collective-permute-start | bytes 6152 | tf_op jit(solution)/shard_map/ppermute | solution.py:188
  42.4 2.0 %collective-permute-done.21 = f32[1,512]{1,0:T(1,128)S(1)} collective-permute-done((f32[1,512]{1,0:T(1,128)S(1)}, f32[1,512]{1,0:T(1,128)S(1)}, u32[]{:S(2)}, u32[]{:S(2)}) %collective-permute-start.21) | collective-permute-done | bytes 2080 | tf_op jit(solution)/shard_map/ppermute | solution.py:188
  44.4 0.9 %broadcast_multiply_fusion = f32[256,512]{1,0:T(8,128)} fusion(f32[256,512]{1,0:T(8,128)S(1)} %get-tuple-element.31, f32[512]{0:T(512)S(1)} %bitcast.1), kind=kLoop, calls=%fused_computation | loop fusion | flops 131072 | bytes 1050624 | tf_op jit(solution)/shard_map/mul | solution.py:296
  (12 shorter events, 0.1 us)
Async XLA Ops:
  0.0 11.6 %collective-permute-start = (bf16[256,512]{1,0:T(8,128)(2,1)}, bf16[256,512]{1,0:T(8,128)(2,1)S(1)}, u32[]{:S(2)}, u32[]{:S(2)}) collective-permute-start(bf16[256,512]{1,0:T(8,128)(2,1)} %refs_7_.1), channel_id=1, source_target_pairs={{0,8},{8,16},{16,24},{24,28},{28,20},{20,12},{12,4},{4,0},{1,9},{9... | collective-permute-start | bytes 786440 | tf_op jit(solution)/shard_map/ppermute | solution.py:228
  3.0 8.6 %collective-permute-start.1 = (bf16[256,512]{1,0:T(8,128)(2,1)}, bf16[256,512]{1,0:T(8,128)(2,1)S(1)}, u32[]{:S(2)}, u32[]{:S(2)}) collective-permute-start(bf16[256,512]{1,0:T(8,128)(2,1)} %refs_7_.1), channel_id=1, source_target_pairs={{8,0},{16,8},{24,16},{28,24},{20,28},{12,20},{4,12},{0,4},{9,1},{1... | collective-permute-start | bytes 786440 | tf_op jit(solution)/shard_map/ppermute | solution.py:228
  3.0 8.6 %collective-permute-start.3 = (bf16[256,512]{1,0:T(8,128)(2,1)}, bf16[256,512]{1,0:T(8,128)(2,1)S(1)}, u32[]{:S(2)}, u32[]{:S(2)}) collective-permute-start(bf16[256,512]{1,0:T(8,128)(2,1)} %refs_7_.1), channel_id=1, source_target_pairs={{0,2},{1,3},{2,0},{3,1},{4,6},{5,7},{6,4},{7,5},{8,10},{9,11},{10,... | collective-permute-start | bytes 786440 | tf_op jit(solution)/shard_map/ppermute | solution.py:188
  5.0 1.0 %copy-start = (bf16[256,512]{1,0:T(8,128)(2,1)S(1)}, bf16[256,512]{1,0:T(8,128)(2,1)}, u32[]{:S(2)}) copy-start(bf16[256,512]{1,0:T(8,128)(2,1)} %refs_7_.1) | copy-start | bytes 786436
  6.0 0.7 %copy-start.2 = (s32[1,2]{1,0:T(1,128)S(1)}, s32[1,2]{1,0:T(1,128)}, u32[]{:S(2)}) copy-start(s32[1,2]{1,0:T(1,128)} %pattern_hbm.1) | copy-start | bytes 28
  6.6 0.7 %copy-start.3 = (s32[1,2]{1,0:T(1,128)S(1)}, s32[1,2]{1,0:T(1,128)}, u32[]{:S(2)}) copy-start(s32[1,2]{1,0:T(1,128)} %keep_hbm.1) | copy-start | bytes 28
  7.9 3.7 %collective-permute-start.2 = (f32[1,640]{1,0:T(1,128)S(1)}, f32[1,640]{1,0:T(1,128)S(1)}, u32[]{:S(2)}, u32[]{:S(2)}) collective-permute-start(f32[1,640]{1,0:T(1,128)S(1)} %shard_map.37), channel_id=1, source_target_pairs={{0,8},{4,12},{8,0},{12,4},{16,24},{20,28},{24,16},{28,20},{1,9},{5... | collective-permute-start | bytes 7688 | tf_op jit(solution)/shard_map/ppermute | solution.py:188
  11.6 9.1 %collective-permute-start.4 = (bf16[256,512]{1,0:T(8,128)(2,1)S(1)}, bf16[256,512]{1,0:T(8,128)(2,1)S(1)}, u32[]{:S(2)}, u32[]{:S(2)}) collective-permute-start(bf16[256,512]{1,0:T(8,128)(2,1)S(1)} %collective-permute-done.refs_6_), channel_id=1, source_target_pairs={{0,8},{8,16},{16,24},{24,28},{28,20},{20,12},{12,4},{4,0},{1,9},{9... | collective-permute-start | bytes 786440 | tf_op jit(solution)/shard_map/ppermute | solution.py:228
  13.3 7.5 %collective-permute-start.5 = (bf16[256,512]{1,0:T(8,128)(2,1)S(1)}, bf16[256,512]{1,0:T(8,128)(2,1)S(1)}, u32[]{:S(2)}, u32[]{:S(2)}) collective-permute-start(bf16[256,512]{1,0:T(8,128)(2,1)S(1)} %collective-permute-done.1.refs_1_), channel_id=1, source_target_pairs={{8,0},{16,8},{24,16},{28,24},{20,28},{12,20},{4,12},{0,4},{9,1},{1... | collective-permute-start | bytes 786440 | tf_op jit(solution)/shard_map/ppermute | solution.py:228
  13.7 4.5 %collective-permute-start.6 = (f32[1,640]{1,0:T(1,128)S(1)}, f32[1,640]{1,0:T(1,128)S(1)}, u32[]{:S(2)}, u32[]{:S(2)}) collective-permute-start(f32[1,640]{1,0:T(1,128)S(1)} %add.26), channel_id=1, source_target_pairs={{0,4},{4,0},{8,12},{12,8},{16,20},{20,16},{24,28},{28,24},{1,5},{5... | collective-permute-start | bytes 7688 | tf_op jit(solution)/shard_map/ppermute | solution.py:188
  15.2 3.6 %collective-permute-start.7 = (f32[1,640]{1,0:T(1,128)S(1)}, f32[1,640]{1,0:T(1,128)S(1)}, u32[]{:S(2)}, u32[]{:S(2)}) collective-permute-start(f32[1,640]{1,0:T(1,128)S(1)} %add.26), channel_id=1, source_target_pairs={{0,2},{1,3},{2,0},{3,1},{4,6},{5,7},{6,4},{7,5},{8,10},{9,11},{10,... | collective-permute-start | bytes 7688 | tf_op jit(solution)/shard_map/ppermute | solution.py:188
  16.2 4.5 %collective-permute-start.8 = (f32[1,640]{1,0:T(1,128)S(1)}, f32[1,640]{1,0:T(1,128)S(1)}, u32[]{:S(2)}, u32[]{:S(2)}) collective-permute-start(f32[1,640]{1,0:T(1,128)S(1)} %add.26), channel_id=1, source_target_pairs={{0,6},{1,7},{2,4},{3,5},{4,2},{5,3},{6,0},{7,1},{8,14},{9,15},{10,... | collective-permute-start | bytes 7688 | tf_op jit(solution)/shard_map/ppermute | solution.py:221
  20.7 3.2 %copy-start.1 = (bf16[256,512]{1,0:T(8,128)(2,1)S(1)}, bf16[256,512]{1,0:T(8,128)(2,1)}, u32[]{:S(2)}) copy-start(bf16[256,512]{1,0:T(8,128)(2,1)} %refs_7_.1) | copy-start | bytes 786436
  20.8 7.7 %collective-permute-start.10 = (bf16[256,512]{1,0:T(8,128)(2,1)S(1)}, bf16[256,512]{1,0:T(8,128)(2,1)S(1)}, u32[]{:S(2)}, u32[]{:S(2)}) collective-permute-start(bf16[256,512]{1,0:T(8,128)(2,1)S(1)} %collective-permute-done.5.refs_2_), channel_id=1, source_target_pairs={{8,0},{16,8},{24,16},{28,24},{20,28},{12,20},{4,12},{0,4},{9,1},{1... | collective-permute-start | bytes 786440 | tf_op jit(solution)/shard_map/ppermute | solution.py:228
  21.4 7.7 %collective-permute-start.9 = (bf16[256,512]{1,0:T(8,128)(2,1)S(1)}, bf16[256,512]{1,0:T(8,128)(2,1)S(1)}, u32[]{:S(2)}, u32[]{:S(2)}) collective-permute-start(bf16[256,512]{1,0:T(8,128)(2,1)S(1)} %collective-permute-done.4.refs_5_), channel_id=1, source_target_pairs={{0,8},{8,16},{16,24},{24,28},{28,20},{20,12},{12,4},{4,0},{1,9},{9... | collective-permute-start | bytes 786440 | tf_op jit(solution)/shard_map/ppermute | solution.py:228
  22.9 6.4 %collective-permute-start.15 = (bf16[256,512]{1,0:T(8,128)(2,1)S(1)}, bf16[256,512]{1,0:T(8,128)(2,1)S(1)}, u32[]{:S(2)}, u32[]{:S(2)}) collective-permute-start(bf16[256,512]{1,0:T(8,128)(2,1)S(1)} %broadcast_select_fusion.refs_11_), channel_id=1, source_target_pairs={{0,2},{1,3},{2,0},{3,1},{4,6},{5,7},{6,4},{7,5},{8,10},{9,11},{10,... | collective-permute-start | bytes 786440 | tf_op jit(solution)/shard_map/ppermute | solution.py:188
  24.0 5.7 %collective-permute-start.12 = (bf16[256,512]{1,0:T(8,128)(2,1)S(1)}, bf16[256,512]{1,0:T(8,128)(2,1)S(1)}, u32[]{:S(2)}, u32[]{:S(2)}) collective-permute-start(bf16[256,512]{1,0:T(8,128)(2,1)S(1)} %copy-done.1), channel_id=1, source_target_pairs={{0,1},{1,0},{2,3},{3,2},{4,5},{5,4},{6,7},{7,6},{8,9},{9,8},{10,11... | collective-permute-start | bytes 786440 | tf_op jit(solution)/shard_map/ppermute | solution.py:188
  24.0 4.5 %collective-permute-start.11 = (f32[2,640]{1,0:T(2,128)S(1)}, f32[2,640]{1,0:T(2,128)S(1)}, u32[]{:S(2)}, u32[]{:S(2)}) collective-permute-start(f32[2,640]{1,0:T(2,128)S(1)} %pad_maximum_fusion), channel_id=1, source_target_pairs={{0,16},{4,20},{8,24},{12,28},{16,0},{20,4},{24,8},{28,12},{1,17},{... | collective-permute-start | bytes 15368 | tf_op jit(solution)/shard_map/ppermute | solution.py:188
  28.5 3.9 %collective-permute-start.13 = (bf16[256,512]{1,0:T(8,128)(2,1)S(1)}, bf16[256,512]{1,0:T(8,128)(2,1)S(1)}, u32[]{:S(2)}, u32[]{:S(2)}) collective-permute-start(bf16[256,512]{1,0:T(8,128)(2,1)S(1)} %collective-permute-done.3.refs_9_), channel_id=1, source_target_pairs={{0,1},{1,0},{2,3},{3,2},{4,5},{5,4},{6,7},{7,6},{8,9},{9,8},{10,11... | collective-permute-start | bytes 786440 | tf_op jit(solution)/shard_map/ppermute | solution.py:188
  28.5 3.9 %collective-permute-start.14 = (bf16[256,512]{1,0:T(8,128)(2,1)S(1)}, bf16[256,512]{1,0:T(8,128)(2,1)S(1)}, u32[]{:S(2)}, u32[]{:S(2)}) collective-permute-start(bf16[256,512]{1,0:T(8,128)(2,1)S(1)} %broadcast_select_fusion.refs_11_), channel_id=1, source_target_pairs={{0,1},{1,0},{2,3},{3,2},{4,5},{5,4},{6,7},{7,6},{8,9},{9,8},{10,11... | collective-permute-start | bytes 786440 | tf_op jit(solution)/shard_map/ppermute | solution.py:188
  29.1 2.2 %collective-permute-start.17 = (f32[2,640]{1,0:T(2,128)S(1)}, f32[2,640]{1,0:T(2,128)S(1)}, u32[]{:S(2)}, u32[]{:S(2)}) collective-permute-start(f32[2,640]{1,0:T(2,128)S(1)} %add.29), channel_id=1, source_target_pairs={{0,1},{1,0},{2,3},{3,2},{4,5},{5,4},{6,7},{7,6},{8,9},{9,8},{10,11... | collective-permute-start | bytes 15368 | tf_op jit(solution)/shard_map/ppermute | solution.py:188
  29.3 3.1 %collective-permute-start.16 = (bf16[256,512]{1,0:T(8,128)(2,1)S(1)}, bf16[256,512]{1,0:T(8,128)(2,1)S(1)}, u32[]{:S(2)}, u32[]{:S(2)}) collective-permute-start(bf16[256,512]{1,0:T(8,128)(2,1)S(1)} %collective-permute-done.15.refs_13_), channel_id=1, source_target_pairs={{0,1},{1,0},{2,3},{3,2},{4,5},{5,4},{6,7},{7,6},{8,9},{9,8},{10,11... | collective-permute-start | bytes 786440 | tf_op jit(solution)/shard_map/ppermute | solution.py:188
  29.6 5.8 %collective-permute-start.18 = (bf16[128,512]{1,0:T(8,128)(2,1)S(1)}, bf16[128,512]{1,0:T(8,128)(2,1)S(1)}, u32[]{:S(2)}, u32[]{:S(2)}) collective-permute-start(bf16[128,512]{1,0:T(8,128)(2,1)S(1)} %slice.23), channel_id=1, source_target_pairs={{0,8},{8,16},{16,24},{24,28},{28,20},{20,12},{12,4},{4,0},{1,9},{9... | collective-permute-start | bytes 393224 | tf_op jit(solution)/shard_map/ppermute | solution.py:245
  31.3 5.4 %collective-permute-start.19 = (bf16[128,512]{1,0:T(8,128)(2,1)S(1)}, bf16[128,512]{1,0:T(8,128)(2,1)S(1)}, u32[]{:S(2)}, u32[]{:S(2)}) collective-permute-start(bf16[128,512]{1,0:T(8,128)(2,1)S(1)} %slice.24), channel_id=1, source_target_pairs={{8,0},{16,8},{24,16},{28,24},{20,28},{12,20},{4,12},{0,4},{9,1},{1... | collective-permute-start | bytes 393224 | tf_op jit(solution)/shard_map/ppermute | solution.py:246
  37.2 3.7 %collective-permute-start.20 = (f32[1,512]{1,0:T(1,128)S(1)}, f32[1,512]{1,0:T(1,128)S(1)}, u32[]{:S(2)}, u32[]{:S(2)}) collective-permute-start(f32[1,512]{1,0:T(1,128)S(1)} %get-tuple-element.32), channel_id=1, source_target_pairs={{0,4},{4,0},{8,12},{12,8},{16,20},{20,16},{24,28},{28,24},{1,5},{5... | collective-permute-start | bytes 6152 | tf_op jit(solution)/shard_map/ppermute | solution.py:188
  40.8 3.6 %collective-permute-start.21 = (f32[1,512]{1,0:T(1,128)S(1)}, f32[1,512]{1,0:T(1,128)S(1)}, u32[]{:S(2)}, u32[]{:S(2)}) collective-permute-start(f32[1,512]{1,0:T(1,128)S(1)} %add.32), channel_id=1, source_target_pairs={{0,8},{4,12},{8,0},{12,4},{16,24},{20,28},{24,16},{28,20},{1,9},{5... | collective-permute-start | bytes 6152 | tf_op jit(solution)/shard_map/ppermute | solution.py:188

commit v4 on v3

--- a/solution.py
+++ b/solution.py
@@ -227,7 +227,8 @@
     for s in range(1, half_ring):
         behind, ahead = lax.ppermute(behind, "row", up), lax.ppermute(ahead, "row", down)
         if s == 2:
-            near, far = note + send_row(note, bits[1]), send_far_col(note) + send_both(note, bits[1])
+            far = send_both(note, bits[1]) + send_far_col(note)
+            near = note + send_row(note, bits[1])
             note = jnp.concatenate([near, far], axis=0)
         elif s <= len(bits):
             note = note + send_row(note, bits[s - 1])
@@ -291,8 +292,13 @@
 
     bit = 1
     while bit < half_ring:
-        totals = totals + send_row(totals, bit)
-        bit *= 2
+        if 2 * bit < half_ring:
+            across = send_row(totals, 3 * bit)
+            totals = (totals + across) + (send_row(totals, bit) + send_row(totals, 2 * bit))
+            bit *= 4
+        else:
+            totals = totals + send_row(totals, bit)
+            bit *= 2
     return inflated * (rows_n * tile / totals)
 
 

time: 45.4 us -> 44.2 us (0.974)
  waiting for transfers between devices: 13.8 us -> 10.6 us
  starting transfers between devices: 24.6 us -> 26.5 us
    ppermute x13 -> x14, waiting for transfers between devices: 9.95 us -> 8.14 us  [send(): return lax.ppermute(value, axis, [(i, i ^ bit) for i in range(count)])]
    ppermute x13 -> x14, starting transfers between devices: 13.7 us -> 14.7 us  [send(): return lax.ppermute(value, axis, [(i, i ^ bit) for i in range(count)])]
    ppermute x1, starting transfers between devices: 1.13 us -> 2.09 us  [body(): bottom = lax.ppermute(ahead[half:], 'row', down)]
    ppermute x3, starting transfers between devices: 6.15 us -> 5.19 us  [body(): lax.ppermute(behind, 'row', up)]
    ppermute x1, waiting for transfers between devices: 1.2 us -> 0.25 us  [body(): bottom = lax.ppermute(ahead[half:], 'row', down)]
    ppermute x3, starting transfers between devices: 1.04 us -> 1.94 us  [body(): lax.ppermute(ahead, 'row', down)]
  transfers between devices with their start and end apart: 22 -> 23, of which waited for: 10 -> 11; matrix products, arithmetic and copies ran while one was open for 0% -> 0% of each run, Pallas kernels for 7% -> 7%
where the time goes in v4:
time: 44.2 us; the launch traced here: 44.1 us
  starting transfers between devices  26.5 us (60%)
  waiting for transfers between devices  10.6 us (24%)
  Pallas kernels  3.54 us (8%)
  local copies, waits for them, and re-layouts  2.33 us (5%)
  other arithmetic  0.93 us (2%)
    ppermute x14, starting transfers between devices, send(): return lax.ppermute(value, axis, [(i, i ^ bit) for i in range(count)])  14.7 us
    ppermute x14, waiting for transfers between devices, send(): return lax.ppermute(value, axis, [(i, i ^ bit) for i in range(count)])  8.14 us
    ppermute x3, starting transfers between devices, body(): lax.ppermute(behind, 'row', up)  5.19 us
    pallas_call x1, Pallas kernels, body(): pl.pallas_call(functools.partial(square_kernel, rows_n, cols_n, half_ring...  2.33 us
    unnamed x8, local copies, waits for them, and re-layouts  2.3 us
    ppermute x1, starting transfers between devices, body(): bottom = lax.ppermute(ahead[half:], 'row', down)  2.09 us
    ppermute x3, starting transfers between devices, body(): lax.ppermute(ahead, 'row', down)  1.94 us
    ppermute x1, starting transfers between devices, body(): top = lax.ppermute(behind[:half], 'row', up)  1.63 us
  transfers between devices with their start and end apart: 23, of which 11 were waited for; matrix products, arithmetic and copies ran while one was open for 0% of the time, Pallas kernels for 7%

profile of v4, /device:TPU:0, one launch (start us, length us, event | category | flops | bytes accessed | tf_op | source)
XLA Modules:
  0.0 44.1 jit_solution(3541814052386297242)
XLA Ops:
  0.0 3.0 %collective-permute-start = (bf16[256,512]{1,0:T(8,128)(2,1)}, bf16[256,512]{1,0:T(8,128)(2,1)S(1)}, u32[]{:S(2)}, u32[]{:S(2)}) collective-permute-start(bf16[256,512]{1,0:T(8,128)(2,1)} %refs_7_.1), channel_id=1, source_target_pairs={{0,8},{8,16},{16,24},{24,28},{28,20},{20,12},{12,4},{4,0},{1,9},{9... | collective-permute-start | bytes 786440 | tf_op jit(solution)/shard_map/ppermute | solution.py:228
  3.0 0.0 collective-permute-start.1
  3.0 2.0 %collective-permute-start.3 = (bf16[256,512]{1,0:T(8,128)(2,1)}, bf16[256,512]{1,0:T(8,128)(2,1)S(1)}, u32[]{:S(2)}, u32[]{:S(2)}) collective-permute-start(bf16[256,512]{1,0:T(8,128)(2,1)} %refs_7_.1), channel_id=1, source_target_pairs={{0,2},{1,3},{2,0},{3,1},{4,6},{5,7},{6,4},{7,5},{8,10},{9,11},{10,... | collective-permute-start | bytes 786440 | tf_op jit(solution)/shard_map/ppermute | solution.py:188
  5.0 0.0 copy-start
  5.0 1.0 %copy-done = bf16[256,512]{1,0:T(8,128)(2,1)S(1)} copy-done((bf16[256,512]{1,0:T(8,128)(2,1)S(1)}, bf16[256,512]{1,0:T(8,128)(2,1)}, u32[]{:S(2)}) %copy-start) | copy-done | bytes 262168
  6.0 0.0 copy-start.2
  6.0 0.7 %copy-done.2 = s32[1,2]{1,0:T(1,128)S(1)} copy-done((s32[1,2]{1,0:T(1,128)S(1)}, s32[1,2]{1,0:T(1,128)}, u32[]{:S(2)}) %copy-start.2) | copy-done | bytes 32
  6.6 0.0 copy-start.3
  6.6 0.7 %copy-done.3 = s32[1,2]{1,0:T(1,128)S(1)} copy-done((s32[1,2]{1,0:T(1,128)S(1)}, s32[1,2]{1,0:T(1,128)}, u32[]{:S(2)}) %copy-start.3) | copy-done | bytes 32
  7.3 0.6 %shard_map.37 = f32[1,640]{1,0:T(1,128)S(1)} custom-call(bf16[256,512]{1,0:T(8,128)(2,1)S(1)} %copy-done, s32[1,2]{1,0:T(1,128)S(1)} %copy-done.2, s32[1,2]{1,0:T(1,128)S(1)} %copy-done.3), custom_call_target="tpu_custom_call" | custom-call | tf_op jit(solution)/shard_map/pallas_call | solution.py:205
  7.9 1.6 %collective-permute-start.2 = (f32[1,640]{1,0:T(1,128)S(1)}, f32[1,640]{1,0:T(1,128)S(1)}, u32[]{:S(2)}, u32[]{:S(2)}) collective-permute-start(f32[1,640]{1,0:T(1,128)S(1)} %shard_map.37), channel_id=1, source_target_pairs={{0,8},{4,12},{8,0},{12,4},{16,24},{20,28},{24,16},{28,20},{1,9},{5... | collective-permute-start | bytes 7688 | tf_op jit(solution)/shard_map/ppermute | solution.py:188
  9.6 2.0 %collective-permute-done.2 = f32[1,640]{1,0:T(1,128)S(1)} collective-permute-done((f32[1,640]{1,0:T(1,128)S(1)}, f32[1,640]{1,0:T(1,128)S(1)}, u32[]{:S(2)}, u32[]{:S(2)}) %collective-permute-start.2) | collective-permute-done | bytes 2592 | tf_op jit(solution)/shard_map/ppermute | solution.py:188
  11.6 0.0 collective-permute-done.refs_6_
  11.6 0.0 collective-permute-done.1.refs_1_
  11.6 0.0 collective-permute-done.3.refs_9_
  11.6 1.6 %collective-permute-start.4 = (bf16[256,512]{1,0:T(8,128)(2,1)S(1)}, bf16[256,512]{1,0:T(8,128)(2,1)S(1)}, u32[]{:S(2)}, u32[]{:S(2)}) collective-permute-start(bf16[256,512]{1,0:T(8,128)(2,1)S(1)} %collective-permute-done.refs_6_), channel_id=1, source_target_pairs={{0,8},{8,16},{16,24},{24,28},{28,20},{20,12},{12,4},{4,0},{1,9},{9... | collective-permute-start | bytes 786440 | tf_op jit(solution)/shard_map/ppermute | solution.py:228
  13.3 0.4 %collective-permute-start.5 = (bf16[256,512]{1,0:T(8,128)(2,1)S(1)}, bf16[256,512]{1,0:T(8,128)(2,1)S(1)}, u32[]{:S(2)}, u32[]{:S(2)}) collective-permute-start(bf16[256,512]{1,0:T(8,128)(2,1)S(1)} %collective-permute-done.1.refs_1_), channel_id=1, source_target_pairs={{8,0},{16,8},{24,16},{28,24},{20,28},{12,20},{4,12},{0,4},{9,1},{1... | collective-permute-start | bytes 786440 | tf_op jit(solution)/shard_map/ppermute | solution.py:228
  13.7 1.5 %collective-permute-start.6 = (f32[1,640]{1,0:T(1,128)S(1)}, f32[1,640]{1,0:T(1,128)S(1)}, u32[]{:S(2)}, u32[]{:S(2)}) collective-permute-start(f32[1,640]{1,0:T(1,128)S(1)} %add.29), channel_id=1, source_target_pairs={{0,4},{4,0},{8,12},{12,8},{16,20},{20,16},{24,28},{28,24},{1,5},{5... | collective-permute-start | bytes 7688 | tf_op jit(solution)/shard_map/ppermute | solution.py:188
  15.2 1.0 %collective-permute-start.7 = (f32[1,640]{1,0:T(1,128)S(1)}, f32[1,640]{1,0:T(1,128)S(1)}, u32[]{:S(2)}, u32[]{:S(2)}) collective-permute-start(f32[1,640]{1,0:T(1,128)S(1)} %add.29), channel_id=1, source_target_pairs={{0,6},{1,7},{2,4},{3,5},{4,2},{5,3},{6,0},{7,1},{8,14},{9,15},{10,... | collective-permute-start | bytes 7688 | tf_op jit(solution)/shard_map/ppermute | solution.py:221
  16.2 1.0 %collective-permute-start.8 = (f32[1,640]{1,0:T(1,128)S(1)}, f32[1,640]{1,0:T(1,128)S(1)}, u32[]{:S(2)}, u32[]{:S(2)}) collective-permute-start(f32[1,640]{1,0:T(1,128)S(1)} %add.29), channel_id=1, source_target_pairs={{0,2},{1,3},{2,0},{3,1},{4,6},{5,7},{6,4},{7,5},{8,10},{9,11},{10,... | collective-permute-start | bytes 7688 | tf_op jit(solution)/shard_map/ppermute | solution.py:188
  17.2 1.0 %collective-permute-done.6 = f32[1,640]{1,0:T(1,128)S(1)} collective-permute-done((f32[1,640]{1,0:T(1,128)S(1)}, f32[1,640]{1,0:T(1,128)S(1)}, u32[]{:S(2)}, u32[]{:S(2)}) %collective-permute-start.6) | collective-permute-done | bytes 2592 | tf_op jit(solution)/shard_map/ppermute | solution.py:188
  18.2 1.5 %collective-permute-done.7 = f32[1,640]{1,0:T(1,128)S(1)} collective-permute-done((f32[1,640]{1,0:T(1,128)S(1)}, f32[1,640]{1,0:T(1,128)S(1)}, u32[]{:S(2)}, u32[]{:S(2)}) %collective-permute-start.7) | collective-permute-done | bytes 2592 | tf_op jit(solution)/shard_map/ppermute | solution.py:221
  19.7 0.1 collective-permute-done.8
  19.8 0.0 copy-start.1
  19.8 0.0 collective-permute-done.4.refs_5_
  19.8 0.1 collective-permute-done.5.refs_2_
  19.9 1.5 %collective-permute-start.10 = (bf16[256,512]{1,0:T(8,128)(2,1)S(1)}, bf16[256,512]{1,0:T(8,128)(2,1)S(1)}, u32[]{:S(2)}, u32[]{:S(2)}) collective-permute-start(bf16[256,512]{1,0:T(8,128)(2,1)S(1)} %collective-permute-done.5.refs_2_), channel_id=1, source_target_pairs={{8,0},{16,8},{24,16},{28,24},{20,28},{12,20},{4,12},{0,4},{9,1},{1... | collective-permute-start | bytes 786440 | tf_op jit(solution)/shard_map/ppermute | solution.py:228
  21.4 0.5 %collective-permute-start.9 = (bf16[256,512]{1,0:T(8,128)(2,1)S(1)}, bf16[256,512]{1,0:T(8,128)(2,1)S(1)}, u32[]{:S(2)}, u32[]{:S(2)}) collective-permute-start(bf16[256,512]{1,0:T(8,128)(2,1)S(1)} %collective-permute-done.4.refs_5_), channel_id=1, source_target_pairs={{0,8},{8,16},{16,24},{24,28},{28,20},{20,12},{12,4},{4,0},{1,9},{9... | collective-permute-start | bytes 786440 | tf_op jit(solution)/shard_map/ppermute | solution.py:228
  21.9 1.1 %collective-permute-start.15 = (bf16[256,512]{1,0:T(8,128)(2,1)S(1)}, bf16[256,512]{1,0:T(8,128)(2,1)S(1)}, u32[]{:S(2)}, u32[]{:S(2)}) collective-permute-start(bf16[256,512]{1,0:T(8,128)(2,1)S(1)} %broadcast_select_fusion.refs_11_), channel_id=1, source_target_pairs={{0,2},{1,3},{2,0},{3,1},{4,6},{5,7},{6,4},{7,5},{8,10},{9,11},{10,... | collective-permute-start | bytes 786440 | tf_op jit(solution)/shard_map/ppermute | solution.py:188
  23.0 0.0 copy-done.1
  23.0 0.0 collective-permute-start.12
  23.0 2.6 %collective-permute-start.11 = (f32[2,640]{1,0:T(2,128)S(1)}, f32[2,640]{1,0:T(2,128)S(1)}, u32[]{:S(2)}, u32[]{:S(2)}) collective-permute-start(f32[2,640]{1,0:T(2,128)S(1)} %pad_maximum_fusion), channel_id=1, source_target_pairs={{0,16},{4,20},{8,24},{12,28},{16,0},{20,4},{24,8},{28,12},{1,17},{... | collective-permute-start | bytes 15368 | tf_op jit(solution)/shard_map/ppermute | solution.py:188
  25.6 1.9 %collective-permute-done.11 = f32[2,640]{1,0:T(2,128)S(1)} collective-permute-done((f32[2,640]{1,0:T(2,128)S(1)}, f32[2,640]{1,0:T(2,128)S(1)}, u32[]{:S(2)}, u32[]{:S(2)}) %collective-permute-start.11) | collective-permute-done | bytes 5152 | tf_op jit(solution)/shard_map/ppermute | solution.py:188
  27.5 0.0 collective-permute-start.13
  27.6 0.0 collective-permute-done.10.refs_3_
  27.6 0.6 %collective-permute-start.14 = (bf16[256,512]{1,0:T(8,128)(2,1)S(1)}, bf16[256,512]{1,0:T(8,128)(2,1)S(1)}, u32[]{:S(2)}, u32[]{:S(2)}) collective-permute-start(bf16[256,512]{1,0:T(8,128)(2,1)S(1)} %broadcast_select_fusion.refs_11_), channel_id=1, source_target_pairs={{0,1},{1,0},{2,3},{3,2},{4,5},{5,4},{6,7},{7,6},{8,9},{9,8},{10,11... | collective-permute-start | bytes 786440 | tf_op jit(solution)/shard_map/ppermute | solution.py:188
  28.1 0.0 collective-permute-done.9.refs_4_
  28.1 0.1 collective-permute-start.17
  28.2 0.2 collective-permute-done.15.refs_13_
  28.4 0.3 collective-permute-start.16
  28.7 0.0 collective-permute-done.12.refs_8_
  28.7 1.6 %collective-permute-start.18 = (bf16[128,512]{1,0:T(8,128)(2,1)S(1)}, bf16[128,512]{1,0:T(8,128)(2,1)S(1)}, u32[]{:S(2)}, u32[]{:S(2)}) collective-permute-start(bf16[128,512]{1,0:T(8,128)(2,1)S(1)} %slice.23), channel_id=1, source_target_pairs={{0,8},{8,16},{16,24},{24,28},{28,20},{20,12},{12,4},{4,0},{1,9},{9... | collective-permute-start | bytes 393224 | tf_op jit(solution)/shard_map/ppermute | solution.py:246
  30.3 0.0 collective-permute-done.17
  30.3 2.1 %collective-permute-start.19 = (bf16[128,512]{1,0:T(8,128)(2,1)S(1)}, bf16[128,512]{1,0:T(8,128)(2,1)S(1)}, u32[]{:S(2)}, u32[]{:S(2)}) collective-permute-start(bf16[128,512]{1,0:T(8,128)(2,1)S(1)} %slice.24), channel_id=1, source_target_pairs={{8,0},{16,8},{24,16},{28,24},{20,28},{12,20},{4,12},{0,4},{9,1},{1... | collective-permute-start | bytes 393224 | tf_op jit(solution)/shard_map/ppermute | solution.py:247
  32.4 0.0 collective-permute-done.13.refs_10_
  32.4 0.0 collective-permute-done.14.refs_12_
  32.4 0.0 collective-permute-done.16.refs_14_
  32.4 2.3 %shard_map.38 = (f32[512,512]{1,0:T(8,128)S(1)}, bf16[512,256]{1,0:T(8,128)(2,1)S(1)}) custom-call(bf16[256,512]{1,0:T(8,128)(2,1)S(1)} %copy-done.1, bf16[256,512]{1,0:T(8,128)(2,1)S(1)} %collective-permute-done.1.refs_1_, bf16[256,512]{1,0:T(8,128)(2,1)S(1)} %collective-permute-done.5.refs_2_, bf16[256,512]{1,0:T(8,128)(2,1)S(1)} %collective-permute-done.10.refs_3_, ...), custom_call_target="tpu_custom_call" | custom-call | flops 1073741824 | bytes 3145728 | tf_op jit(solution)/shard_map/pallas_call | solution.py:257
  34.8 0.7 %collective-permute-done.18.top_ref = bf16[128,512]{1,0:T(8,128)(2,1)S(1)} collective-permute-done((bf16[128,512]{1,0:T(8,128)(2,1)S(1)}, bf16[128,512]{1,0:T(8,128)(2,1)S(1)}, u32[]{:S(2)}, u32[]{:S(2)}) %collective-permute-start.18) | collective-permute-done | bytes 131104 | tf_op jit(solution)/shard_map/ppermute | solution.py:246
  35.4 0.2 collective-permute-done.19.bottom_ref
  35.7 0.6 %shard_map.39 = (f32[256,512]{1,0:T(8,128)S(1)}, f32[1,512]{1,0:T(1,128)S(1)}) custom-call(f32[512,512]{1,0:T(8,128)S(1)} %get-tuple-element.29.acc_ref, bf16[512,256]{1,0:T(8,128)(2,1)S(1)} %get-tuple-element.30.left_ref, bf16[128,512]{1,0:T(8,128)(2,1)S(1)} %collective-permute-done.18.top_ref, bf16[128,512]{1,0:T(8,128)(2,1)S(1)} %collective-permute-done.19.bottom_ref, ...), custom_call_target="tpu_custom_call" | custom-call | flops 134217728 | bytes 2097152 | tf_op jit(solution)/shard_map/pallas_call | solution.py:277
  36.3 3.3 %collective-permute-start.20 = (f32[1,512]{1,0:T(1,128)S(1)}, f32[1,512]{1,0:T(1,128)S(1)}, u32[]{:S(2)}, u32[]{:S(2)}) collective-permute-start(f32[1,512]{1,0:T(1,128)S(1)} %get-tuple-element.32), channel_id=1, source_target_pairs={{0,12},{4,8},{8,4},{12,0},{16,28},{20,24},{24,20},{28,16},{1,13},{... | collective-permute-start | bytes 6152 | tf_op jit(solution)/shard_map/ppermute | solution.py:188
  39.6 0.0 collective-permute-start.21
  39.6 0.6 %collective-permute-start.22 = (f32[1,512]{1,0:T(1,128)S(1)}, f32[1,512]{1,0:T(1,128)S(1)}, u32[]{:S(2)}, u32[]{:S(2)}) collective-permute-start(f32[1,512]{1,0:T(1,128)S(1)} %get-tuple-element.32), channel_id=1, source_target_pairs={{0,8},{4,12},{8,0},{12,4},{16,24},{20,28},{24,16},{28,20},{1,9},{5... | collective-permute-start | bytes 6152 | tf_op jit(solution)/shard_map/ppermute | solution.py:188
  40.2 0.9 %collective-permute-done.20 = f32[1,512]{1,0:T(1,128)S(1)} collective-permute-done((f32[1,512]{1,0:T(1,128)S(1)}, f32[1,512]{1,0:T(1,128)S(1)}, u32[]{:S(2)}, u32[]{:S(2)}) %collective-permute-start.20) | collective-permute-done | bytes 2080 | tf_op jit(solution)/shard_map/ppermute | solution.py:188
  41.2 2.0 %collective-permute-done.21 = f32[1,512]{1,0:T(1,128)S(1)} collective-permute-done((f32[1,512]{1,0:T(1,128)S(1)}, f32[1,512]{1,0:T(1,128)S(1)}, u32[]{:S(2)}, u32[]{:S(2)}) %collective-permute-start.21) | collective-permute-done | bytes 2080 | tf_op jit(solution)/shard_map/ppermute | solution.py:188
  43.2 0.0 collective-permute-done.22
  43.2 0.9 %broadcast_multiply_fusion = f32[256,512]{1,0:T(8,128)} fusion(f32[256,512]{1,0:T(8,128)S(1)} %get-tuple-element.31, f32[512]{0:T(512)S(1)} %bitcast.1), kind=kLoop, calls=%fused_computation | loop fusion | flops 131072 | bytes 1050624 | tf_op jit(solution)/shard_map/mul | solution.py:302
  (11 shorter events, 0.1 us)
Async XLA Ops:
  0.0 11.6 %collective-permute-start = (bf16[256,512]{1,0:T(8,128)(2,1)}, bf16[256,512]{1,0:T(8,128)(2,1)S(1)}, u32[]{:S(2)}, u32[]{:S(2)}) collective-permute-start(bf16[256,512]{1,0:T(8,128)(2,1)} %refs_7_.1), channel_id=1, source_target_pairs={{0,8},{8,16},{16,24},{24,28},{28,20},{20,12},{12,4},{4,0},{1,9},{9... | collective-permute-start | bytes 786440 | tf_op jit(solution)/shard_map/ppermute | solution.py:228
  3.0 8.6 %collective-permute-start.1 = (bf16[256,512]{1,0:T(8,128)(2,1)}, bf16[256,512]{1,0:T(8,128)(2,1)S(1)}, u32[]{:S(2)}, u32[]{:S(2)}) collective-permute-start(bf16[256,512]{1,0:T(8,128)(2,1)} %refs_7_.1), channel_id=1, source_target_pairs={{8,0},{16,8},{24,16},{28,24},{20,28},{12,20},{4,12},{0,4},{9,1},{1... | collective-permute-start | bytes 786440 | tf_op jit(solution)/shard_map/ppermute | solution.py:228
  3.0 8.6 %collective-permute-start.3 = (bf16[256,512]{1,0:T(8,128)(2,1)}, bf16[256,512]{1,0:T(8,128)(2,1)S(1)}, u32[]{:S(2)}, u32[]{:S(2)}) collective-permute-start(bf16[256,512]{1,0:T(8,128)(2,1)} %refs_7_.1), channel_id=1, source_target_pairs={{0,2},{1,3},{2,0},{3,1},{4,6},{5,7},{6,4},{7,5},{8,10},{9,11},{10,... | collective-permute-start | bytes 786440 | tf_op jit(solution)/shard_map/ppermute | solution.py:188
  5.0 1.0 %copy-start = (bf16[256,512]{1,0:T(8,128)(2,1)S(1)}, bf16[256,512]{1,0:T(8,128)(2,1)}, u32[]{:S(2)}) copy-start(bf16[256,512]{1,0:T(8,128)(2,1)} %refs_7_.1) | copy-start | bytes 786436
  6.0 0.7 %copy-start.2 = (s32[1,2]{1,0:T(1,128)S(1)}, s32[1,2]{1,0:T(1,128)}, u32[]{:S(2)}) copy-start(s32[1,2]{1,0:T(1,128)} %pattern_hbm.1) | copy-start | bytes 28
  6.6 0.7 %copy-start.3 = (s32[1,2]{1,0:T(1,128)S(1)}, s32[1,2]{1,0:T(1,128)}, u32[]{:S(2)}) copy-start(s32[1,2]{1,0:T(1,128)} %keep_hbm.1) | copy-start | bytes 28
  7.9 3.7 %collective-permute-start.2 = (f32[1,640]{1,0:T(1,128)S(1)}, f32[1,640]{1,0:T(1,128)S(1)}, u32[]{:S(2)}, u32[]{:S(2)}) collective-permute-start(f32[1,640]{1,0:T(1,128)S(1)} %shard_map.37), channel_id=1, source_target_pairs={{0,8},{4,12},{8,0},{12,4},{16,24},{20,28},{24,16},{28,20},{1,9},{5... | collective-permute-start | bytes 7688 | tf_op jit(solution)/shard_map/ppermute | solution.py:188
  11.6 8.2 %collective-permute-start.4 = (bf16[256,512]{1,0:T(8,128)(2,1)S(1)}, bf16[256,512]{1,0:T(8,128)(2,1)S(1)}, u32[]{:S(2)}, u32[]{:S(2)}) collective-permute-start(bf16[256,512]{1,0:T(8,128)(2,1)S(1)} %collective-permute-done.refs_6_), channel_id=1, source_target_pairs={{0,8},{8,16},{16,24},{24,28},{28,20},{20,12},{12,4},{4,0},{1,9},{9... | collective-permute-start | bytes 786440 | tf_op jit(solution)/shard_map/ppermute | solution.py:228
  13.3 6.6 %collective-permute-start.5 = (bf16[256,512]{1,0:T(8,128)(2,1)S(1)}, bf16[256,512]{1,0:T(8,128)(2,1)S(1)}, u32[]{:S(2)}, u32[]{:S(2)}) collective-permute-start(bf16[256,512]{1,0:T(8,128)(2,1)S(1)} %collective-permute-done.1.refs_1_), channel_id=1, source_target_pairs={{8,0},{16,8},{24,16},{28,24},{20,28},{12,20},{4,12},{0,4},{9,1},{1... | collective-permute-start | bytes 786440 | tf_op jit(solution)/shard_map/ppermute | solution.py:228
  13.7 4.5 %collective-permute-start.6 = (f32[1,640]{1,0:T(1,128)S(1)}, f32[1,640]{1,0:T(1,128)S(1)}, u32[]{:S(2)}, u32[]{:S(2)}) collective-permute-start(f32[1,640]{1,0:T(1,128)S(1)} %add.29), channel_id=1, source_target_pairs={{0,4},{4,0},{8,12},{12,8},{16,20},{20,16},{24,28},{28,24},{1,5},{5... | collective-permute-start | bytes 7688 | tf_op jit(solution)/shard_map/ppermute | solution.py:188
  15.2 4.5 %collective-permute-start.7 = (f32[1,640]{1,0:T(1,128)S(1)}, f32[1,640]{1,0:T(1,128)S(1)}, u32[]{:S(2)}, u32[]{:S(2)}) collective-permute-start(f32[1,640]{1,0:T(1,128)S(1)} %add.29), channel_id=1, source_target_pairs={{0,6},{1,7},{2,4},{3,5},{4,2},{5,3},{6,0},{7,1},{8,14},{9,15},{10,... | collective-permute-start | bytes 7688 | tf_op jit(solution)/shard_map/ppermute | solution.py:221
  16.2 3.6 %collective-permute-start.8 = (f32[1,640]{1,0:T(1,128)S(1)}, f32[1,640]{1,0:T(1,128)S(1)}, u32[]{:S(2)}, u32[]{:S(2)}) collective-permute-start(f32[1,640]{1,0:T(1,128)S(1)} %add.29), channel_id=1, source_target_pairs={{0,2},{1,3},{2,0},{3,1},{4,6},{5,7},{6,4},{7,5},{8,10},{9,11},{10,... | collective-permute-start | bytes 7688 | tf_op jit(solution)/shard_map/ppermute | solution.py:188
  19.8 3.2 %copy-start.1 = (bf16[256,512]{1,0:T(8,128)(2,1)S(1)}, bf16[256,512]{1,0:T(8,128)(2,1)}, u32[]{:S(2)}) copy-start(bf16[256,512]{1,0:T(8,128)(2,1)} %refs_7_.1) | copy-start | bytes 786436
  19.9 7.7 %collective-permute-start.10 = (bf16[256,512]{1,0:T(8,128)(2,1)S(1)}, bf16[256,512]{1,0:T(8,128)(2,1)S(1)}, u32[]{:S(2)}, u32[]{:S(2)}) collective-permute-start(bf16[256,512]{1,0:T(8,128)(2,1)S(1)} %collective-permute-done.5.refs_2_), channel_id=1, source_target_pairs={{8,0},{16,8},{24,16},{28,24},{20,28},{12,20},{4,12},{0,4},{9,1},{1... | collective-permute-start | bytes 786440 | tf_op jit(solution)/shard_map/ppermute | solution.py:228
  21.4 6.8 %collective-permute-start.9 = (bf16[256,512]{1,0:T(8,128)(2,1)S(1)}, bf16[256,512]{1,0:T(8,128)(2,1)S(1)}, u32[]{:S(2)}, u32[]{:S(2)}) collective-permute-start(bf16[256,512]{1,0:T(8,128)(2,1)S(1)} %collective-permute-done.4.refs_5_), channel_id=1, source_target_pairs={{0,8},{8,16},{16,24},{24,28},{28,20},{20,12},{12,4},{4,0},{1,9},{9... | collective-permute-start | bytes 786440 | tf_op jit(solution)/shard_map/ppermute | solution.py:228
  21.9 6.4 %collective-permute-start.15 = (bf16[256,512]{1,0:T(8,128)(2,1)S(1)}, bf16[256,512]{1,0:T(8,128)(2,1)S(1)}, u32[]{:S(2)}, u32[]{:S(2)}) collective-permute-start(bf16[256,512]{1,0:T(8,128)(2,1)S(1)} %broadcast_select_fusion.refs_11_), channel_id=1, source_target_pairs={{0,2},{1,3},{2,0},{3,1},{4,6},{5,7},{6,4},{7,5},{8,10},{9,11},{10,... | collective-permute-start | bytes 786440 | tf_op jit(solution)/shard_map/ppermute | solution.py:188
  23.0 5.7 %collective-permute-start.12 = (bf16[256,512]{1,0:T(8,128)(2,1)S(1)}, bf16[256,512]{1,0:T(8,128)(2,1)S(1)}, u32[]{:S(2)}, u32[]{:S(2)}) collective-permute-start(bf16[256,512]{1,0:T(8,128)(2,1)S(1)} %copy-done.1), channel_id=1, source_target_pairs={{0,1},{1,0},{2,3},{3,2},{4,5},{5,4},{6,7},{7,6},{8,9},{9,8},{10,11... | collective-permute-start | bytes 786440 | tf_op jit(solution)/shard_map/ppermute | solution.py:188
  23.0 4.5 %collective-permute-start.11 = (f32[2,640]{1,0:T(2,128)S(1)}, f32[2,640]{1,0:T(2,128)S(1)}, u32[]{:S(2)}, u32[]{:S(2)}) collective-permute-start(f32[2,640]{1,0:T(2,128)S(1)} %pad_maximum_fusion), channel_id=1, source_target_pairs={{0,16},{4,20},{8,24},{12,28},{16,0},{20,4},{24,8},{28,12},{1,17},{... | collective-permute-start | bytes 15368 | tf_op jit(solution)/shard_map/ppermute | solution.py:188
  27.5 4.9 %collective-permute-start.13 = (bf16[256,512]{1,0:T(8,128)(2,1)S(1)}, bf16[256,512]{1,0:T(8,128)(2,1)S(1)}, u32[]{:S(2)}, u32[]{:S(2)}) collective-permute-start(bf16[256,512]{1,0:T(8,128)(2,1)S(1)} %collective-permute-done.3.refs_9_), channel_id=1, source_target_pairs={{0,1},{1,0},{2,3},{3,2},{4,5},{5,4},{6,7},{7,6},{8,9},{9,8},{10,11... | collective-permute-start | bytes 786440 | tf_op jit(solution)/shard_map/ppermute | solution.py:188
  27.6 4.9 %collective-permute-start.14 = (bf16[256,512]{1,0:T(8,128)(2,1)S(1)}, bf16[256,512]{1,0:T(8,128)(2,1)S(1)}, u32[]{:S(2)}, u32[]{:S(2)}) collective-permute-start(bf16[256,512]{1,0:T(8,128)(2,1)S(1)} %broadcast_select_fusion.refs_11_), channel_id=1, source_target_pairs={{0,1},{1,0},{2,3},{3,2},{4,5},{5,4},{6,7},{7,6},{8,9},{9,8},{10,11... | collective-permute-start | bytes 786440 | tf_op jit(solution)/shard_map/ppermute | solution.py:188
  28.1 2.2 %collective-permute-start.17 = (f32[2,640]{1,0:T(2,128)S(1)}, f32[2,640]{1,0:T(2,128)S(1)}, u32[]{:S(2)}, u32[]{:S(2)}) collective-permute-start(f32[2,640]{1,0:T(2,128)S(1)} %add.32), channel_id=1, source_target_pairs={{0,1},{1,0},{2,3},{3,2},{4,5},{5,4},{6,7},{7,6},{8,9},{9,8},{10,11... | collective-permute-start | bytes 15368 | tf_op jit(solution)/shard_map/ppermute | solution.py:188
  28.4 4.1 %collective-permute-start.16 = (bf16[256,512]{1,0:T(8,128)(2,1)S(1)}, bf16[256,512]{1,0:T(8,128)(2,1)S(1)}, u32[]{:S(2)}, u32[]{:S(2)}) collective-permute-start(bf16[256,512]{1,0:T(8,128)(2,1)S(1)} %collective-permute-done.15.refs_13_), channel_id=1, source_target_pairs={{0,1},{1,0},{2,3},{3,2},{4,5},{5,4},{6,7},{7,6},{8,9},{9,8},{10,11... | collective-permute-start | bytes 786440 | tf_op jit(solution)/shard_map/ppermute | solution.py:188
  28.7 6.7 %collective-permute-start.18 = (bf16[128,512]{1,0:T(8,128)(2,1)S(1)}, bf16[128,512]{1,0:T(8,128)(2,1)S(1)}, u32[]{:S(2)}, u32[]{:S(2)}) collective-permute-start(bf16[128,512]{1,0:T(8,128)(2,1)S(1)} %slice.23), channel_id=1, source_target_pairs={{0,8},{8,16},{16,24},{24,28},{28,20},{20,12},{12,4},{4,0},{1,9},{9... | collective-permute-start | bytes 393224 | tf_op jit(solution)/shard_map/ppermute | solution.py:246
  30.3 5.4 %collective-permute-start.19 = (bf16[128,512]{1,0:T(8,128)(2,1)S(1)}, bf16[128,512]{1,0:T(8,128)(2,1)S(1)}, u32[]{:S(2)}, u32[]{:S(2)}) collective-permute-start(bf16[128,512]{1,0:T(8,128)(2,1)S(1)} %slice.24), channel_id=1, source_target_pairs={{8,0},{16,8},{24,16},{28,24},{20,28},{12,20},{4,12},{0,4},{9,1},{1... | collective-permute-start | bytes 393224 | tf_op jit(solution)/shard_map/ppermute | solution.py:247
  36.3 4.9 %collective-permute-start.20 = (f32[1,512]{1,0:T(1,128)S(1)}, f32[1,512]{1,0:T(1,128)S(1)}, u32[]{:S(2)}, u32[]{:S(2)}) collective-permute-start(f32[1,512]{1,0:T(1,128)S(1)} %get-tuple-element.32), channel_id=1, source_target_pairs={{0,12},{4,8},{8,4},{12,0},{16,28},{20,24},{24,20},{28,16},{1,13},{... | collective-permute-start | bytes 6152 | tf_op jit(solution)/shard_map/ppermute | solution.py:188
  39.6 3.6 %collective-permute-start.21 = (f32[1,512]{1,0:T(1,128)S(1)}, f32[1,512]{1,0:T(1,128)S(1)}, u32[]{:S(2)}, u32[]{:S(2)}) collective-permute-start(f32[1,512]{1,0:T(1,128)S(1)} %get-tuple-element.32), channel_id=1, source_target_pairs={{0,4},{4,0},{8,12},{12,8},{16,20},{20,16},{24,28},{28,24},{1,5},{5... | collective-permute-start | bytes 6152 | tf_op jit(solution)/shard_map/ppermute | solution.py:188
  39.6 3.6 %collective-permute-start.22 = (f32[1,512]{1,0:T(1,128)S(1)}, f32[1,512]{1,0:T(1,128)S(1)}, u32[]{:S(2)}, u32[]{:S(2)}) collective-permute-start(f32[1,512]{1,0:T(1,128)S(1)} %get-tuple-element.32), channel_id=1, source_target_pairs={{0,8},{4,12},{8,0},{12,4},{16,24},{20,28},{24,16},{28,20},{1,9},{5... | collective-permute-start | bytes 6152 | tf_op jit(solution)/shard_map/ppermute | solution.py:188

commit v5 on v4

--- a/solution.py
+++ b/solution.py
@@ -160,6 +160,19 @@
         mate = row ^ (rows_n // 2)
         other = product[tile : 2 * tile] * lane(note_ref, cols_dev, (rows_n + mate) * tcols + tile_col)
         tot_ref[:, cut] = jnp.sum(mine + other * other, axis=0, keepdims=True)
+
+
+def scale_kernel(order_total, parts, inflated_ref, totals_ref, out_hbm, scaled, sems):
+    factor = order_total / totals_ref[...]
+    size = inflated_ref.shape[0] // parts
+    copies = []
+    for part in range(parts):
+        rows = pl.ds(part * size, size)
+        scaled[rows, :] = inflated_ref[rows, :] * factor
+        copies.append(pltpu.make_async_copy(scaled.at[rows, :], out_hbm.at[rows, :], sems.at[part]))
+        copies[-1].start()
+    for copy in copies:
+        copy.wait()
 
 
 def whole():
@@ -299,7 +312,15 @@
         else:
             totals = totals + send_row(totals, bit)
             bit *= 2
-    return inflated * (rows_n * tile / totals)
+    parts = 4
+    return pl.pallas_call(
+        functools.partial(scale_kernel, float(rows_n * tile), parts),
+        out_shape=jax.ShapeDtypeStruct((tile, cols_dev), jnp.float32),
+        in_specs=[whole(), whole()],
+        out_specs=pl.BlockSpec(memory_space=pl.ANY),
+        scratch_shapes=[pltpu.VMEM((tile, cols_dev), jnp.float32), pltpu.SemaphoreType.DMA((parts,))],
+        compiler_params=pltpu.CompilerParams(vmem_limit_bytes=8 * 4 * tile * cols_dev),
+    )(inflated, totals)
 
 
 def solution(mesh):

time: 44.2 us -> 44.2 us (level)
  other arithmetic: 0.93 us -> 0.07 us
  Pallas kernels: 3.54 us -> 4.38 us
    mul x1 -> x0, other arithmetic: 0.86 us -> none  [body(): return inflated * (rows_n * tile / totals)]
    pallas_call x0 -> x1, Pallas kernels: none -> 0.84 us  [body(): pl.pallas_call(functools.partial(scale_kernel, float(rows_n * tile), part...]
where the time goes in v5:
time: 44.2 us; the launch traced here: 44 us
  starting transfers between devices  26.5 us (60%)
  waiting for transfers between devices  10.6 us (24%)
  Pallas kernels  4.38 us (10%)
  local copies, waits for them, and re-layouts  2.33 us (5%)
    ppermute x14, starting transfers between devices, send(): return lax.ppermute(value, axis, [(i, i ^ bit) for i in range(count)])  14.7 us
    ppermute x14, waiting for transfers between devices, send(): return lax.ppermute(value, axis, [(i, i ^ bit) for i in range(count)])  8.14 us
    ppermute x3, starting transfers between devices, body(): lax.ppermute(behind, 'row', up)  5.19 us
    pallas_call x1, Pallas kernels, body(): pl.pallas_call(functools.partial(square_kernel, rows_n, cols_n, half_ring...  2.33 us
    unnamed x8, local copies, waits for them, and re-layouts  2.3 us
    ppermute x1, starting transfers between devices, body(): bottom = lax.ppermute(ahead[half:], 'row', down)  2.09 us
    ppermute x3, starting transfers between devices, body(): lax.ppermute(ahead, 'row', down)  1.94 us
    ppermute x1, starting transfers between devices, body(): top = lax.ppermute(behind[:half], 'row', up)  1.63 us
  transfers between devices with their start and end apart: 23, of which 11 were waited for; matrix products, arithmetic and copies ran while one was open for 0% of the time, Pallas kernels for 7%

profile of v5, /device:TPU:0, one launch (start us, length us, event | category | flops | bytes accessed | tf_op | source)
XLA Modules:
  0.0 44.0 jit_solution(3976035206817426907)
XLA Ops:
  0.0 3.0 %collective-permute-start = (bf16[256,512]{1,0:T(8,128)(2,1)}, bf16[256,512]{1,0:T(8,128)(2,1)S(1)}, u32[]{:S(2)}, u32[]{:S(2)}) collective-permute-start(bf16[256,512]{1,0:T(8,128)(2,1)} %refs_7_.1), channel_id=1, source_target_pairs={{0,8},{8,16},{16,24},{24,28},{28,20},{20,12},{12,4},{4,0},{1,9},{9... | collective-permute-start | bytes 786440 | tf_op jit(solution)/shard_map/ppermute | solution.py:241
  3.0 0.0 collective-permute-start.1
  3.0 2.0 %collective-permute-start.3 = (bf16[256,512]{1,0:T(8,128)(2,1)}, bf16[256,512]{1,0:T(8,128)(2,1)S(1)}, u32[]{:S(2)}, u32[]{:S(2)}) collective-permute-start(bf16[256,512]{1,0:T(8,128)(2,1)} %refs_7_.1), channel_id=1, source_target_pairs={{0,2},{1,3},{2,0},{3,1},{4,6},{5,7},{6,4},{7,5},{8,10},{9,11},{10,... | collective-permute-start | bytes 786440 | tf_op jit(solution)/shard_map/ppermute | solution.py:201
  5.0 0.0 copy-start
  5.0 1.0 %copy-done = bf16[256,512]{1,0:T(8,128)(2,1)S(1)} copy-done((bf16[256,512]{1,0:T(8,128)(2,1)S(1)}, bf16[256,512]{1,0:T(8,128)(2,1)}, u32[]{:S(2)}) %copy-start) | copy-done | bytes 262168
  6.0 0.0 copy-start.2
  6.0 0.7 %copy-done.2 = s32[1,2]{1,0:T(1,128)S(1)} copy-done((s32[1,2]{1,0:T(1,128)S(1)}, s32[1,2]{1,0:T(1,128)}, u32[]{:S(2)}) %copy-start.2) | copy-done | bytes 32
  6.6 0.0 copy-start.3
  6.6 0.7 %copy-done.3 = s32[1,2]{1,0:T(1,128)S(1)} copy-done((s32[1,2]{1,0:T(1,128)S(1)}, s32[1,2]{1,0:T(1,128)}, u32[]{:S(2)}) %copy-start.3) | copy-done | bytes 32
  7.3 0.6 %shard_map.37 = f32[1,640]{1,0:T(1,128)S(1)} custom-call(bf16[256,512]{1,0:T(8,128)(2,1)S(1)} %copy-done, s32[1,2]{1,0:T(1,128)S(1)} %copy-done.2, s32[1,2]{1,0:T(1,128)S(1)} %copy-done.3), custom_call_target="tpu_custom_call" | custom-call | tf_op jit(solution)/shard_map/pallas_call | solution.py:218
  7.9 1.6 %collective-permute-start.2 = (f32[1,640]{1,0:T(1,128)S(1)}, f32[1,640]{1,0:T(1,128)S(1)}, u32[]{:S(2)}, u32[]{:S(2)}) collective-permute-start(f32[1,640]{1,0:T(1,128)S(1)} %shard_map.37), channel_id=1, source_target_pairs={{0,8},{4,12},{8,0},{12,4},{16,24},{20,28},{24,16},{28,20},{1,9},{5... | collective-permute-start | bytes 7688 | tf_op jit(solution)/shard_map/ppermute | solution.py:201
  9.6 2.0 %collective-permute-done.2 = f32[1,640]{1,0:T(1,128)S(1)} collective-permute-done((f32[1,640]{1,0:T(1,128)S(1)}, f32[1,640]{1,0:T(1,128)S(1)}, u32[]{:S(2)}, u32[]{:S(2)}) %collective-permute-start.2) | collective-permute-done | bytes 2592 | tf_op jit(solution)/shard_map/ppermute | solution.py:201
  11.6 0.0 collective-permute-done.refs_6_
  11.6 0.0 collective-permute-done.1.refs_1_
  11.6 0.0 collective-permute-done.3.refs_9_
  11.6 1.6 %collective-permute-start.4 = (bf16[256,512]{1,0:T(8,128)(2,1)S(1)}, bf16[256,512]{1,0:T(8,128)(2,1)S(1)}, u32[]{:S(2)}, u32[]{:S(2)}) collective-permute-start(bf16[256,512]{1,0:T(8,128)(2,1)S(1)} %collective-permute-done.refs_6_), channel_id=1, source_target_pairs={{0,8},{8,16},{16,24},{24,28},{28,20},{20,12},{12,4},{4,0},{1,9},{9... | collective-permute-start | bytes 786440 | tf_op jit(solution)/shard_map/ppermute | solution.py:241
  13.3 0.4 %collective-permute-start.5 = (bf16[256,512]{1,0:T(8,128)(2,1)S(1)}, bf16[256,512]{1,0:T(8,128)(2,1)S(1)}, u32[]{:S(2)}, u32[]{:S(2)}) collective-permute-start(bf16[256,512]{1,0:T(8,128)(2,1)S(1)} %collective-permute-done.1.refs_1_), channel_id=1, source_target_pairs={{8,0},{16,8},{24,16},{28,24},{20,28},{12,20},{4,12},{0,4},{9,1},{1... | collective-permute-start | bytes 786440 | tf_op jit(solution)/shard_map/ppermute | solution.py:241
  13.7 1.5 %collective-permute-start.6 = (f32[1,640]{1,0:T(1,128)S(1)}, f32[1,640]{1,0:T(1,128)S(1)}, u32[]{:S(2)}, u32[]{:S(2)}) collective-permute-start(f32[1,640]{1,0:T(1,128)S(1)} %add.29), channel_id=1, source_target_pairs={{0,4},{4,0},{8,12},{12,8},{16,20},{20,16},{24,28},{28,24},{1,5},{5... | collective-permute-start | bytes 7688 | tf_op jit(solution)/shard_map/ppermute | solution.py:201
  15.2 1.0 %collective-permute-start.7 = (f32[1,640]{1,0:T(1,128)S(1)}, f32[1,640]{1,0:T(1,128)S(1)}, u32[]{:S(2)}, u32[]{:S(2)}) collective-permute-start(f32[1,640]{1,0:T(1,128)S(1)} %add.29), channel_id=1, source_target_pairs={{0,6},{1,7},{2,4},{3,5},{4,2},{5,3},{6,0},{7,1},{8,14},{9,15},{10,... | collective-permute-start | bytes 7688 | tf_op jit(solution)/shard_map/ppermute | solution.py:234
  16.2 1.0 %collective-permute-start.8 = (f32[1,640]{1,0:T(1,128)S(1)}, f32[1,640]{1,0:T(1,128)S(1)}, u32[]{:S(2)}, u32[]{:S(2)}) collective-permute-start(f32[1,640]{1,0:T(1,128)S(1)} %add.29), channel_id=1, source_target_pairs={{0,2},{1,3},{2,0},{3,1},{4,6},{5,7},{6,4},{7,5},{8,10},{9,11},{10,... | collective-permute-start | bytes 7688 | tf_op jit(solution)/shard_map/ppermute | solution.py:201
  17.2 1.0 %collective-permute-done.6 = f32[1,640]{1,0:T(1,128)S(1)} collective-permute-done((f32[1,640]{1,0:T(1,128)S(1)}, f32[1,640]{1,0:T(1,128)S(1)}, u32[]{:S(2)}, u32[]{:S(2)}) %collective-permute-start.6) | collective-permute-done | bytes 2592 | tf_op jit(solution)/shard_map/ppermute | solution.py:201
  18.2 1.5 %collective-permute-done.7 = f32[1,640]{1,0:T(1,128)S(1)} collective-permute-done((f32[1,640]{1,0:T(1,128)S(1)}, f32[1,640]{1,0:T(1,128)S(1)}, u32[]{:S(2)}, u32[]{:S(2)}) %collective-permute-start.7) | collective-permute-done | bytes 2592 | tf_op jit(solution)/shard_map/ppermute | solution.py:234
  19.7 0.1 collective-permute-done.8
  19.8 0.0 copy-start.1
  19.8 0.0 collective-permute-done.4.refs_5_
  19.8 0.1 collective-permute-done.5.refs_2_
  19.9 1.5 %collective-permute-start.10 = (bf16[256,512]{1,0:T(8,128)(2,1)S(1)}, bf16[256,512]{1,0:T(8,128)(2,1)S(1)}, u32[]{:S(2)}, u32[]{:S(2)}) collective-permute-start(bf16[256,512]{1,0:T(8,128)(2,1)S(1)} %collective-permute-done.5.refs_2_), channel_id=1, source_target_pairs={{8,0},{16,8},{24,16},{28,24},{20,28},{12,20},{4,12},{0,4},{9,1},{1... | collective-permute-start | bytes 786440 | tf_op jit(solution)/shard_map/ppermute | solution.py:241
  21.4 0.5 %collective-permute-start.9 = (bf16[256,512]{1,0:T(8,128)(2,1)S(1)}, bf16[256,512]{1,0:T(8,128)(2,1)S(1)}, u32[]{:S(2)}, u32[]{:S(2)}) collective-permute-start(bf16[256,512]{1,0:T(8,128)(2,1)S(1)} %collective-permute-done.4.refs_5_), channel_id=1, source_target_pairs={{0,8},{8,16},{16,24},{24,28},{28,20},{20,12},{12,4},{4,0},{1,9},{9... | collective-permute-start | bytes 786440 | tf_op jit(solution)/shard_map/ppermute | solution.py:241
  21.9 1.1 %collective-permute-start.15 = (bf16[256,512]{1,0:T(8,128)(2,1)S(1)}, bf16[256,512]{1,0:T(8,128)(2,1)S(1)}, u32[]{:S(2)}, u32[]{:S(2)}) collective-permute-start(bf16[256,512]{1,0:T(8,128)(2,1)S(1)} %broadcast_select_fusion.refs_11_), channel_id=1, source_target_pairs={{0,2},{1,3},{2,0},{3,1},{4,6},{5,7},{6,4},{7,5},{8,10},{9,11},{10,... | collective-permute-start | bytes 786440 | tf_op jit(solution)/shard_map/ppermute | solution.py:201
  23.0 0.0 copy-done.1
  23.0 0.0 collective-permute-start.12
  23.0 2.6 %collective-permute-start.11 = (f32[2,640]{1,0:T(2,128)S(1)}, f32[2,640]{1,0:T(2,128)S(1)}, u32[]{:S(2)}, u32[]{:S(2)}) collective-permute-start(f32[2,640]{1,0:T(2,128)S(1)} %pad_maximum_fusion), channel_id=1, source_target_pairs={{0,16},{4,20},{8,24},{12,28},{16,0},{20,4},{24,8},{28,12},{1,17},{... | collective-permute-start | bytes 15368 | tf_op jit(solution)/shard_map/ppermute | solution.py:201
  25.6 1.9 %collective-permute-done.11 = f32[2,640]{1,0:T(2,128)S(1)} collective-permute-done((f32[2,640]{1,0:T(2,128)S(1)}, f32[2,640]{1,0:T(2,128)S(1)}, u32[]{:S(2)}, u32[]{:S(2)}) %collective-permute-start.11) | collective-permute-done | bytes 5152 | tf_op jit(solution)/shard_map/ppermute | solution.py:201
  27.5 0.0 collective-permute-start.13
  27.6 0.0 collective-permute-done.10.refs_3_
  27.6 0.6 %collective-permute-start.14 = (bf16[256,512]{1,0:T(8,128)(2,1)S(1)}, bf16[256,512]{1,0:T(8,128)(2,1)S(1)}, u32[]{:S(2)}, u32[]{:S(2)}) collective-permute-start(bf16[256,512]{1,0:T(8,128)(2,1)S(1)} %broadcast_select_fusion.refs_11_), channel_id=1, source_target_pairs={{0,1},{1,0},{2,3},{3,2},{4,5},{5,4},{6,7},{7,6},{8,9},{9,8},{10,11... | collective-permute-start | bytes 786440 | tf_op jit(solution)/shard_map/ppermute | solution.py:201
  28.1 0.0 collective-permute-done.9.refs_4_
  28.1 0.1 collective-permute-start.17
  28.2 0.2 collective-permute-done.15.refs_13_
  28.4 0.3 collective-permute-start.16
  28.7 0.0 collective-permute-done.12.refs_8_
  28.7 1.6 %collective-permute-start.18 = (bf16[128,512]{1,0:T(8,128)(2,1)S(1)}, bf16[128,512]{1,0:T(8,128)(2,1)S(1)}, u32[]{:S(2)}, u32[]{:S(2)}) collective-permute-start(bf16[128,512]{1,0:T(8,128)(2,1)S(1)} %slice.23), channel_id=1, source_target_pairs={{0,8},{8,16},{16,24},{24,28},{28,20},{20,12},{12,4},{4,0},{1,9},{9... | collective-permute-start | bytes 393224 | tf_op jit(solution)/shard_map/ppermute | solution.py:259
  30.3 0.0 collective-permute-done.17
  30.3 2.1 %collective-permute-start.19 = (bf16[128,512]{1,0:T(8,128)(2,1)S(1)}, bf16[128,512]{1,0:T(8,128)(2,1)S(1)}, u32[]{:S(2)}, u32[]{:S(2)}) collective-permute-start(bf16[128,512]{1,0:T(8,128)(2,1)S(1)} %slice.24), channel_id=1, source_target_pairs={{8,0},{16,8},{24,16},{28,24},{20,28},{12,20},{4,12},{0,4},{9,1},{1... | collective-permute-start | bytes 393224 | tf_op jit(solution)/shard_map/ppermute | solution.py:260
  32.4 0.0 collective-permute-done.13.refs_10_
  32.4 0.0 collective-permute-done.14.refs_12_
  32.4 0.0 collective-permute-done.16.refs_14_
  32.4 2.3 %shard_map.38 = (f32[512,512]{1,0:T(8,128)S(1)}, bf16[512,256]{1,0:T(8,128)(2,1)S(1)}) custom-call(bf16[256,512]{1,0:T(8,128)(2,1)S(1)} %copy-done.1, bf16[256,512]{1,0:T(8,128)(2,1)S(1)} %collective-permute-done.1.refs_1_, bf16[256,512]{1,0:T(8,128)(2,1)S(1)} %collective-permute-done.5.refs_2_, bf16[256,512]{1,0:T(8,128)(2,1)S(1)} %collective-permute-done.10.refs_3_, ...), custom_call_target="tpu_custom_call" | custom-call | flops 1073741824 | bytes 3145728 | tf_op jit(solution)/shard_map/pallas_call | solution.py:270
  34.8 0.7 %collective-permute-done.18.top_ref = bf16[128,512]{1,0:T(8,128)(2,1)S(1)} collective-permute-done((bf16[128,512]{1,0:T(8,128)(2,1)S(1)}, bf16[128,512]{1,0:T(8,128)(2,1)S(1)}, u32[]{:S(2)}, u32[]{:S(2)}) %collective-permute-start.18) | collective-permute-done | bytes 131104 | tf_op jit(solution)/shard_map/ppermute | solution.py:259
  35.4 0.2 collective-permute-done.19.bottom_ref
  35.7 0.6 %shard_map.39 = (f32[256,512]{1,0:T(8,128)S(1)}, f32[1,512]{1,0:T(1,128)S(1)}) custom-call(f32[512,512]{1,0:T(8,128)S(1)} %get-tuple-element.29.acc_ref, bf16[512,256]{1,0:T(8,128)(2,1)S(1)} %get-tuple-element.30.left_ref, bf16[128,512]{1,0:T(8,128)(2,1)S(1)} %collective-permute-done.18.top_ref, bf16[128,512]{1,0:T(8,128)(2,1)S(1)} %collective-permute-done.19.bottom_ref, ...), custom_call_target="tpu_custom_call" | custom-call | flops 134217728 | bytes 2097152 | tf_op jit(solution)/shard_map/pallas_call | solution.py:290
  36.3 3.3 %collective-permute-start.20 = (f32[1,512]{1,0:T(1,128)S(1)}, f32[1,512]{1,0:T(1,128)S(1)}, u32[]{:S(2)}, u32[]{:S(2)}) collective-permute-start(f32[1,512]{1,0:T(1,128)S(1)} %get-tuple-element.32), channel_id=1, source_target_pairs={{0,12},{4,8},{8,4},{12,0},{16,28},{20,24},{24,20},{28,16},{1,13},{... | collective-permute-start | bytes 6152 | tf_op jit(solution)/shard_map/ppermute | solution.py:201
  39.6 0.0 collective-permute-start.21
  39.6 0.6 %collective-permute-start.22 = (f32[1,512]{1,0:T(1,128)S(1)}, f32[1,512]{1,0:T(1,128)S(1)}, u32[]{:S(2)}, u32[]{:S(2)}) collective-permute-start(f32[1,512]{1,0:T(1,128)S(1)} %get-tuple-element.32), channel_id=1, source_target_pairs={{0,8},{4,12},{8,0},{12,4},{16,24},{20,28},{24,16},{28,20},{1,9},{5... | collective-permute-start | bytes 6152 | tf_op jit(solution)/shard_map/ppermute | solution.py:201
  40.2 0.9 %collective-permute-done.20 = f32[1,512]{1,0:T(1,128)S(1)} collective-permute-done((f32[1,512]{1,0:T(1,128)S(1)}, f32[1,512]{1,0:T(1,128)S(1)}, u32[]{:S(2)}, u32[]{:S(2)}) %collective-permute-start.20) | collective-permute-done | bytes 2080 | tf_op jit(solution)/shard_map/ppermute | solution.py:201
  41.2 2.0 %collective-permute-done.21 = f32[1,512]{1,0:T(1,128)S(1)} collective-permute-done((f32[1,512]{1,0:T(1,128)S(1)}, f32[1,512]{1,0:T(1,128)S(1)}, u32[]{:S(2)}, u32[]{:S(2)}) %collective-permute-start.21) | collective-permute-done | bytes 2080 | tf_op jit(solution)/shard_map/ppermute | solution.py:201
  43.2 0.0 collective-permute-done.22
  43.2 0.8 %shard_map.40 = f32[256,512]{1,0:T(8,128)} custom-call(f32[256,512]{1,0:T(8,128)S(1)} %get-tuple-element.31.inflated_ref, f32[1,512]{1,0:T(1,128)S(1)} %add_add_fusion.totals_ref), custom_call_target="tpu_custom_call" | custom-call | tf_op jit(solution)/shard_map/pallas_call | solution.py:316
  (11 shorter events, 0.1 us)
Async XLA Ops:
  0.0 11.6 %collective-permute-start = (bf16[256,512]{1,0:T(8,128)(2,1)}, bf16[256,512]{1,0:T(8,128)(2,1)S(1)}, u32[]{:S(2)}, u32[]{:S(2)}) collective-permute-start(bf16[256,512]{1,0:T(8,128)(2,1)} %refs_7_.1), channel_id=1, source_target_pairs={{0,8},{8,16},{16,24},{24,28},{28,20},{20,12},{12,4},{4,0},{1,9},{9... | collective-permute-start | bytes 786440 | tf_op jit(solution)/shard_map/ppermute | solution.py:241
  3.0 8.6 %collective-permute-start.1 = (bf16[256,512]{1,0:T(8,128)(2,1)}, bf16[256,512]{1,0:T(8,128)(2,1)S(1)}, u32[]{:S(2)}, u32[]{:S(2)}) collective-permute-start(bf16[256,512]{1,0:T(8,128)(2,1)} %refs_7_.1), channel_id=1, source_target_pairs={{8,0},{16,8},{24,16},{28,24},{20,28},{12,20},{4,12},{0,4},{9,1},{1... | collective-permute-start | bytes 786440 | tf_op jit(solution)/shard_map/ppermute | solution.py:241
  3.0 8.6 %collective-permute-start.3 = (bf16[256,512]{1,0:T(8,128)(2,1)}, bf16[256,512]{1,0:T(8,128)(2,1)S(1)}, u32[]{:S(2)}, u32[]{:S(2)}) collective-permute-start(bf16[256,512]{1,0:T(8,128)(2,1)} %refs_7_.1), channel_id=1, source_target_pairs={{0,2},{1,3},{2,0},{3,1},{4,6},{5,7},{6,4},{7,5},{8,10},{9,11},{10,... | collective-permute-start | bytes 786440 | tf_op jit(solution)/shard_map/ppermute | solution.py:201
  5.0 1.0 %copy-start = (bf16[256,512]{1,0:T(8,128)(2,1)S(1)}, bf16[256,512]{1,0:T(8,128)(2,1)}, u32[]{:S(2)}) copy-start(bf16[256,512]{1,0:T(8,128)(2,1)} %refs_7_.1) | copy-start | bytes 786436
  6.0 0.7 %copy-start.2 = (s32[1,2]{1,0:T(1,128)S(1)}, s32[1,2]{1,0:T(1,128)}, u32[]{:S(2)}) copy-start(s32[1,2]{1,0:T(1,128)} %pattern_hbm.1) | copy-start | bytes 28
  6.6 0.7 %copy-start.3 = (s32[1,2]{1,0:T(1,128)S(1)}, s32[1,2]{1,0:T(1,128)}, u32[]{:S(2)}) copy-start(s32[1,2]{1,0:T(1,128)} %keep_hbm.1) | copy-start | bytes 28
  7.9 3.7 %collective-permute-start.2 = (f32[1,640]{1,0:T(1,128)S(1)}, f32[1,640]{1,0:T(1,128)S(1)}, u32[]{:S(2)}, u32[]{:S(2)}) collective-permute-start(f32[1,640]{1,0:T(1,128)S(1)} %shard_map.37), channel_id=1, source_target_pairs={{0,8},{4,12},{8,0},{12,4},{16,24},{20,28},{24,16},{28,20},{1,9},{5... | collective-permute-start | bytes 7688 | tf_op jit(solution)/shard_map/ppermute | solution.py:201
  11.6 8.2 %collective-permute-start.4 = (bf16[256,512]{1,0:T(8,128)(2,1)S(1)}, bf16[256,512]{1,0:T(8,128)(2,1)S(1)}, u32[]{:S(2)}, u32[]{:S(2)}) collective-permute-start(bf16[256,512]{1,0:T(8,128)(2,1)S(1)} %collective-permute-done.refs_6_), channel_id=1, source_target_pairs={{0,8},{8,16},{16,24},{24,28},{28,20},{20,12},{12,4},{4,0},{1,9},{9... | collective-permute-start | bytes 786440 | tf_op jit(solution)/shard_map/ppermute | solution.py:241
  13.3 6.6 %collective-permute-start.5 = (bf16[256,512]{1,0:T(8,128)(2,1)S(1)}, bf16[256,512]{1,0:T(8,128)(2,1)S(1)}, u32[]{:S(2)}, u32[]{:S(2)}) collective-permute-start(bf16[256,512]{1,0:T(8,128)(2,1)S(1)} %collective-permute-done.1.refs_1_), channel_id=1, source_target_pairs={{8,0},{16,8},{24,16},{28,24},{20,28},{12,20},{4,12},{0,4},{9,1},{1... | collective-permute-start | bytes 786440 | tf_op jit(solution)/shard_map/ppermute | solution.py:241
  13.7 4.5 %collective-permute-start.6 = (f32[1,640]{1,0:T(1,128)S(1)}, f32[1,640]{1,0:T(1,128)S(1)}, u32[]{:S(2)}, u32[]{:S(2)}) collective-permute-start(f32[1,640]{1,0:T(1,128)S(1)} %add.29), channel_id=1, source_target_pairs={{0,4},{4,0},{8,12},{12,8},{16,20},{20,16},{24,28},{28,24},{1,5},{5... | collective-permute-start | bytes 7688 | tf_op jit(solution)/shard_map/ppermute | solution.py:201
  15.2 4.5 %collective-permute-start.7 = (f32[1,640]{1,0:T(1,128)S(1)}, f32[1,640]{1,0:T(1,128)S(1)}, u32[]{:S(2)}, u32[]{:S(2)}) collective-permute-start(f32[1,640]{1,0:T(1,128)S(1)} %add.29), channel_id=1, source_target_pairs={{0,6},{1,7},{2,4},{3,5},{4,2},{5,3},{6,0},{7,1},{8,14},{9,15},{10,... | collective-permute-start | bytes 7688 | tf_op jit(solution)/shard_map/ppermute | solution.py:234
  16.2 3.6 %collective-permute-start.8 = (f32[1,640]{1,0:T(1,128)S(1)}, f32[1,640]{1,0:T(1,128)S(1)}, u32[]{:S(2)}, u32[]{:S(2)}) collective-permute-start(f32[1,640]{1,0:T(1,128)S(1)} %add.29), channel_id=1, source_target_pairs={{0,2},{1,3},{2,0},{3,1},{4,6},{5,7},{6,4},{7,5},{8,10},{9,11},{10,... | collective-permute-start | bytes 7688 | tf_op jit(solution)/shard_map/ppermute | solution.py:201
  19.8 3.2 %copy-start.1 = (bf16[256,512]{1,0:T(8,128)(2,1)S(1)}, bf16[256,512]{1,0:T(8,128)(2,1)}, u32[]{:S(2)}) copy-start(bf16[256,512]{1,0:T(8,128)(2,1)} %refs_7_.1) | copy-start | bytes 786436
  19.9 7.7 %collective-permute-start.10 = (bf16[256,512]{1,0:T(8,128)(2,1)S(1)}, bf16[256,512]{1,0:T(8,128)(2,1)S(1)}, u32[]{:S(2)}, u32[]{:S(2)}) collective-permute-start(bf16[256,512]{1,0:T(8,128)(2,1)S(1)} %collective-permute-done.5.refs_2_), channel_id=1, source_target_pairs={{8,0},{16,8},{24,16},{28,24},{20,28},{12,20},{4,12},{0,4},{9,1},{1... | collective-permute-start | bytes 786440 | tf_op jit(solution)/shard_map/ppermute | solution.py:241
  21.4 6.8 %collective-permute-start.9 = (bf16[256,512]{1,0:T(8,128)(2,1)S(1)}, bf16[256,512]{1,0:T(8,128)(2,1)S(1)}, u32[]{:S(2)}, u32[]{:S(2)}) collective-permute-start(bf16[256,512]{1,0:T(8,128)(2,1)S(1)} %collective-permute-done.4.refs_5_), channel_id=1, source_target_pairs={{0,8},{8,16},{16,24},{24,28},{28,20},{20,12},{12,4},{4,0},{1,9},{9... | collective-permute-start | bytes 786440 | tf_op jit(solution)/shard_map/ppermute | solution.py:241
  21.9 6.4 %collective-permute-start.15 = (bf16[256,512]{1,0:T(8,128)(2,1)S(1)}, bf16[256,512]{1,0:T(8,128)(2,1)S(1)}, u32[]{:S(2)}, u32[]{:S(2)}) collective-permute-start(bf16[256,512]{1,0:T(8,128)(2,1)S(1)} %broadcast_select_fusion.refs_11_), channel_id=1, source_target_pairs={{0,2},{1,3},{2,0},{3,1},{4,6},{5,7},{6,4},{7,5},{8,10},{9,11},{10,... | collective-permute-start | bytes 786440 | tf_op jit(solution)/shard_map/ppermute | solution.py:201
  23.0 5.7 %collective-permute-start.12 = (bf16[256,512]{1,0:T(8,128)(2,1)S(1)}, bf16[256,512]{1,0:T(8,128)(2,1)S(1)}, u32[]{:S(2)}, u32[]{:S(2)}) collective-permute-start(bf16[256,512]{1,0:T(8,128)(2,1)S(1)} %copy-done.1), channel_id=1, source_target_pairs={{0,1},{1,0},{2,3},{3,2},{4,5},{5,4},{6,7},{7,6},{8,9},{9,8},{10,11... | collective-permute-start | bytes 786440 | tf_op jit(solution)/shard_map/ppermute | solution.py:201
  23.0 4.5 %collective-permute-start.11 = (f32[2,640]{1,0:T(2,128)S(1)}, f32[2,640]{1,0:T(2,128)S(1)}, u32[]{:S(2)}, u32[]{:S(2)}) collective-permute-start(f32[2,640]{1,0:T(2,128)S(1)} %pad_maximum_fusion), channel_id=1, source_target_pairs={{0,16},{4,20},{8,24},{12,28},{16,0},{20,4},{24,8},{28,12},{1,17},{... | collective-permute-start | bytes 15368 | tf_op jit(solution)/shard_map/ppermute | solution.py:201
  27.5 4.9 %collective-permute-start.13 = (bf16[256,512]{1,0:T(8,128)(2,1)S(1)}, bf16[256,512]{1,0:T(8,128)(2,1)S(1)}, u32[]{:S(2)}, u32[]{:S(2)}) collective-permute-start(bf16[256,512]{1,0:T(8,128)(2,1)S(1)} %collective-permute-done.3.refs_9_), channel_id=1, source_target_pairs={{0,1},{1,0},{2,3},{3,2},{4,5},{5,4},{6,7},{7,6},{8,9},{9,8},{10,11... | collective-permute-start | bytes 786440 | tf_op jit(solution)/shard_map/ppermute | solution.py:201
  27.6 4.9 %collective-permute-start.14 = (bf16[256,512]{1,0:T(8,128)(2,1)S(1)}, bf16[256,512]{1,0:T(8,128)(2,1)S(1)}, u32[]{:S(2)}, u32[]{:S(2)}) collective-permute-start(bf16[256,512]{1,0:T(8,128)(2,1)S(1)} %broadcast_select_fusion.refs_11_), channel_id=1, source_target_pairs={{0,1},{1,0},{2,3},{3,2},{4,5},{5,4},{6,7},{7,6},{8,9},{9,8},{10,11... | collective-permute-start | bytes 786440 | tf_op jit(solution)/shard_map/ppermute | solution.py:201
  28.1 2.2 %collective-permute-start.17 = (f32[2,640]{1,0:T(2,128)S(1)}, f32[2,640]{1,0:T(2,128)S(1)}, u32[]{:S(2)}, u32[]{:S(2)}) collective-permute-start(f32[2,640]{1,0:T(2,128)S(1)} %add.32), channel_id=1, source_target_pairs={{0,1},{1,0},{2,3},{3,2},{4,5},{5,4},{6,7},{7,6},{8,9},{9,8},{10,11... | collective-permute-start | bytes 15368 | tf_op jit(solution)/shard_map/ppermute | solution.py:201
  28.4 4.1 %collective-permute-start.16 = (bf16[256,512]{1,0:T(8,128)(2,1)S(1)}, bf16[256,512]{1,0:T(8,128)(2,1)S(1)}, u32[]{:S(2)}, u32[]{:S(2)}) collective-permute-start(bf16[256,512]{1,0:T(8,128)(2,1)S(1)} %collective-permute-done.15.refs_13_), channel_id=1, source_target_pairs={{0,1},{1,0},{2,3},{3,2},{4,5},{5,4},{6,7},{7,6},{8,9},{9,8},{10,11... | collective-permute-start | bytes 786440 | tf_op jit(solution)/shard_map/ppermute | solution.py:201
  28.7 6.7 %collective-permute-start.18 = (bf16[128,512]{1,0:T(8,128)(2,1)S(1)}, bf16[128,512]{1,0:T(8,128)(2,1)S(1)}, u32[]{:S(2)}, u32[]{:S(2)}) collective-permute-start(bf16[128,512]{1,0:T(8,128)(2,1)S(1)} %slice.23), channel_id=1, source_target_pairs={{0,8},{8,16},{16,24},{24,28},{28,20},{20,12},{12,4},{4,0},{1,9},{9... | collective-permute-start | bytes 393224 | tf_op jit(solution)/shard_map/ppermute | solution.py:259
  30.3 5.4 %collective-permute-start.19 = (bf16[128,512]{1,0:T(8,128)(2,1)S(1)}, bf16[128,512]{1,0:T(8,128)(2,1)S(1)}, u32[]{:S(2)}, u32[]{:S(2)}) collective-permute-start(bf16[128,512]{1,0:T(8,128)(2,1)S(1)} %slice.24), channel_id=1, source_target_pairs={{8,0},{16,8},{24,16},{28,24},{20,28},{12,20},{4,12},{0,4},{9,1},{1... | collective-permute-start | bytes 393224 | tf_op jit(solution)/shard_map/ppermute | solution.py:260
  36.3 4.9 %collective-permute-start.20 = (f32[1,512]{1,0:T(1,128)S(1)}, f32[1,512]{1,0:T(1,128)S(1)}, u32[]{:S(2)}, u32[]{:S(2)}) collective-permute-start(f32[1,512]{1,0:T(1,128)S(1)} %get-tuple-element.32), channel_id=1, source_target_pairs={{0,12},{4,8},{8,4},{12,0},{16,28},{20,24},{24,20},{28,16},{1,13},{... | collective-permute-start | bytes 6152 | tf_op jit(solution)/shard_map/ppermute | solution.py:201
  39.6 3.6 %collective-permute-start.21 = (f32[1,512]{1,0:T(1,128)S(1)}, f32[1,512]{1,0:T(1,128)S(1)}, u32[]{:S(2)}, u32[]{:S(2)}) collective-permute-start(f32[1,512]{1,0:T(1,128)S(1)} %get-tuple-element.32), channel_id=1, source_target_pairs={{0,4},{4,0},{8,12},{12,8},{16,20},{20,16},{24,28},{28,24},{1,5},{5... | collective-permute-start | bytes 6152 | tf_op jit(solution)/shard_map/ppermute | solution.py:201
  39.6 3.6 %collective-permute-start.22 = (f32[1,512]{1,0:T(1,128)S(1)}, f32[1,512]{1,0:T(1,128)S(1)}, u32[]{:S(2)}, u32[]{:S(2)}) collective-permute-start(f32[1,512]{1,0:T(1,128)S(1)} %get-tuple-element.32), channel_id=1, source_target_pairs={{0,8},{4,12},{8,0},{12,4},{16,24},{20,28},{24,16},{28,20},{1,9},{5... | collective-permute-start | bytes 6152 | tf_op jit(solution)/shard_map/ppermute | solution.py:201
